TPU v7x, 128 devices: a whole 4x4x4 slice. The times are simulated.
128 devices in a mesh: ctx: 32 (over y, x, core), head: 4 (over z).
Axes of the slice: x: 4, y: 4, z: 4, core: 2. Of those that a mesh axis runs over, the one named last changes fastest.
Arguments:
- query_rows: bfloat16 [16384, 2048], P(('ctx', 'head')), may hold values from -6 to 6
- key_rows: bfloat16 [16384, 2048], P(('ctx', 'head')), may hold values from -6 to 6
- value_rows: bfloat16 [16384, 4096], P(('ctx', 'head')), may hold values from -6 to 6
- log_decay: bfloat16 [16384, 32], P(('ctx', 'head')), may hold values from -0.75 to 0, as said below
- beta_logit: bfloat16 [16384, 32], P(('ctx', 'head')), may hold values from -8 to 2
- out_grad: bfloat16 [16384, 4096], P(('ctx', 'head')), may hold values from -48 to 48
Outputs:
- query_grad: bfloat16 [16384, 2048], P(('ctx', 'head'))
- key_grad: bfloat16 [16384, 2048], P(('ctx', 'head'))
- value_grad: bfloat16 [16384, 4096], P(('ctx', 'head'))
- decay_grad: bfloat16 [16384, 32], P(('ctx', 'head'))
- beta_grad: bfloat16 [16384, 32], P(('ctx', 'head'))
Inputs may be any that keep to these rules, and one draw needn't show every extreme that they name: `log_decay`: log decays are negative.
All inputs are finite; a program needn't handle non-finite values.
Results may differ from a plain program's by a relative error of at most 0.017.
Values may be sent and summed in bfloat16 or wider, within the bound.
No kernel may reach another device: no remote copies, remote signals or barrier semaphores. Data moves between devices by JAX's collectives and lax.ppermute only.
A program may use at most 256 MiB of HBM per device.

v0:
```python
import jax
import jax.numpy as jnp
from jax import lax
from jax.sharding import PartitionSpec as P

DK = 128
DV = 128
BLOCK = 64


highest = lax.Precision.HIGHEST


def shifted(shard, axis, by):
    count = lax.axis_size(axis)
    pairs = [(i, i + by) for i in range(count) if 0 <= i + by < count]
    return lax.ppermute(shard, axis, pairs)


def unit_rows(values):
    return values * lax.rsqrt(jnp.sum(values * values, axis=-1, keepdims=True) + 1e-06)


def layer_terms(query_rows, key_rows, value_rows, log_decay, beta_logit):
    tokens_here = log_decay.shape[0]
    head_count = log_decay.shape[1]
    key_heads = query_rows.shape[1] // DK
    group_ratio = head_count // key_heads
    blocks = tokens_here // BLOCK
    query_unit = unit_rows(query_rows.reshape(tokens_here, key_heads, DK)) * DK ** (-0.5)
    key_unit = unit_rows(key_rows.reshape(tokens_here, key_heads, DK))
    query_unit = jnp.repeat(
        query_unit.reshape(blocks, BLOCK, key_heads, DK).transpose(2, 0, 1, 3), group_ratio, axis=0
    )
    key_unit = jnp.repeat(
        key_unit.reshape(blocks, BLOCK, key_heads, DK).transpose(2, 0, 1, 3), group_ratio, axis=0
    )
    value_heads = value_rows.reshape(blocks, BLOCK, head_count, DV).transpose(2, 0, 1, 3)
    decay_heads = log_decay.reshape(blocks, BLOCK, head_count).transpose(2, 0, 1)
    strength = jax.nn.sigmoid(beta_logit.reshape(blocks, BLOCK, head_count).transpose(2, 0, 1))
    log_growth = jnp.cumsum(decay_heads, axis=-1)
    row_index = lax.broadcasted_iota(jnp.int32, (BLOCK, BLOCK), 0)
    col_index = lax.broadcasted_iota(jnp.int32, (BLOCK, BLOCK), 1)
    causal = row_index >= col_index
    before = row_index > col_index
    spread = log_growth[..., :, None] - log_growth[..., None, :]
    decay_mat = jnp.where(causal, jnp.exp(jnp.where(causal, spread, 0.0)), 0.0)
    key_key = jnp.einsum("hncd,hnjd->hncj", key_unit, key_unit, precision=highest)
    query_key = jnp.einsum("hncd,hnjd->hncj", query_unit, key_unit, precision=highest)
    eye_block = (row_index == col_index).astype(jnp.float32)
    system = jnp.where(before, strength[..., :, None] * decay_mat * key_key, 0.0) + eye_block
    value_part = jax.scipy.linalg.solve_triangular(
        system, strength[..., None] * value_heads, lower=True, unit_diagonal=True
    )
    growth = jnp.exp(log_growth)
    key_part = jax.scipy.linalg.solve_triangular(
        system, (strength * growth)[..., None] * key_unit, lower=True, unit_diagonal=True
    )
    to_end = jnp.exp(log_growth[..., -1:] - log_growth)
    key_end = to_end[..., None] * key_unit
    eye_key = jnp.eye(DK, dtype=jnp.float32)
    block_map = growth[..., -1, None, None] * eye_key - jnp.einsum(
        "hnck,hncl->hnkl", key_part, key_end, precision=highest
    )
    block_add = jnp.einsum("hncv,hnck->hnvk", value_part, key_end, precision=highest)

    def advance(running, block_pair):
        running_map, running_add = running
        step_map, step_add = block_pair
        next_map = jnp.einsum("hkl,hlm->hkm", running_map, step_map, precision=highest)
        next_add = jnp.einsum("hvl,hlm->hvm", running_add, step_map, precision=highest) + step_add
        return ((next_map, next_add), (running_map, running_add))

    start = (
        jnp.broadcast_to(eye_key, (head_count, DK, DK)),
        jnp.zeros((head_count, DV, DK), jnp.float32),
    )
    (total_map, total_add), (prior_map, prior_add) = lax.scan(
        advance, start, (jnp.moveaxis(block_map, 1, 0), jnp.moveaxis(block_add, 1, 0))
    )
    prior_map = jnp.moveaxis(prior_map, 0, 1)
    prior_add = jnp.moveaxis(prior_add, 0, 1)
    return (
        query_unit,
        growth,
        decay_mat * query_key,
        value_part,
        key_part,
        prior_map,
        prior_add,
        total_map,
        total_add,
    )


def emit(state, span_free_terms):
    (
        query_unit,
        growth,
        weights,
        value_part,
        key_part,
        prior_map,
        prior_add,
        total_map,
        total_add,
    ) = span_free_terms
    starts = jnp.einsum("hvk,hnkl->hnvl", state, prior_map, precision=highest) + prior_add
    fresh = value_part - jnp.einsum("hnck,hnvk->hncv", key_part, starts, precision=highest)
    result = growth[..., None] * jnp.einsum(
        "hnck,hnvk->hncv", query_unit, starts, precision=highest
    )
    result = result + jnp.einsum("hncj,hnjv->hncv", weights, fresh, precision=highest)
    head_count, blocks, length, columns = result.shape
    result = result.transpose(1, 2, 0, 3).reshape(blocks * length, head_count * columns)
    final = jnp.einsum("hvk,hkl->hvl", state, total_map, precision=highest) + total_add
    return (result, final)


def full_pass(state, query_rows, key_rows, value_rows, log_decay, beta_logit):
    return emit(state, layer_terms(query_rows, key_rows, value_rows, log_decay, beta_logit))


def on_device(query_rows, key_rows, value_rows, log_decay, beta_logit, out_grad):
    query_in, key_in, value_in, decay_in, beta_in, cot_in = (
        lax.all_to_all(query_rows, "head", split_axis=1, concat_axis=0, tiled=True),
        lax.all_to_all(key_rows, "head", split_axis=1, concat_axis=0, tiled=True),
        lax.all_to_all(value_rows, "head", split_axis=1, concat_axis=0, tiled=True),
        lax.all_to_all(log_decay, "head", split_axis=1, concat_axis=0, tiled=True),
        lax.all_to_all(beta_logit, "head", split_axis=1, concat_axis=0, tiled=True),
        lax.all_to_all(out_grad, "head", split_axis=1, concat_axis=0, tiled=True),
    )
    local_inputs = (
        query_in.astype(jnp.float32),
        key_in.astype(jnp.float32),
        value_in.astype(jnp.float32),
        decay_in.astype(jnp.float32),
        beta_in.astype(jnp.float32),
    )
    cotangent = cot_in.astype(jnp.float32)
    segment_terms = layer_terms(*local_inputs)
    total_map = segment_terms[7]
    total_add = segment_terms[8]
    zero_state = jnp.zeros_like(total_add)

    def outputs_only(probe):
        return emit(probe, segment_terms)[0]

    local_grad = jax.vjp(outputs_only, zero_state)[1](cotangent)[0]
    back_map = jnp.swapaxes(total_map, 1, 2)

    def relay(iteration, carried):
        forward_state, behind = carried
        forward_state = shifted(
            (
                jnp.einsum("hvk,hkl->hvl", forward_state, total_map, precision=highest) + total_add
            ).astype(jnp.bfloat16),
            "ctx",
            1,
        ).astype(jnp.float32)
        behind = shifted(
            jnp.einsum("hvk,hkl->hvl", behind, back_map, precision=highest) + local_grad, "ctx", -1
        )
        return (forward_state, behind)

    state_in, state_grad = lax.fori_loop(
        0, lax.axis_size("ctx") - 1, relay, (zero_state, zero_state)
    )
    _, pullback = jax.vjp(full_pass, state_in, *local_inputs)
    gradients = pullback((cotangent, state_grad))
    query_grad = gradients[1].astype(jnp.bfloat16)
    key_grad = gradients[2].astype(jnp.bfloat16)
    value_grad = gradients[3].astype(jnp.bfloat16)
    decay_grad = gradients[4].astype(jnp.bfloat16)
    beta_grad = gradients[5].astype(jnp.bfloat16)
    return (
        lax.all_to_all(query_grad, "head", split_axis=0, concat_axis=1, tiled=True),
        lax.all_to_all(key_grad, "head", split_axis=0, concat_axis=1, tiled=True),
        lax.all_to_all(value_grad, "head", split_axis=0, concat_axis=1, tiled=True),
        lax.all_to_all(decay_grad, "head", split_axis=0, concat_axis=1, tiled=True),
        lax.all_to_all(beta_grad, "head", split_axis=0, concat_axis=1, tiled=True),
    )


def solution(mesh):
    return jax.shard_map(
        on_device,
        mesh=mesh,
        in_specs=(
            P(("ctx", "head"), None),
            P(("ctx", "head"), None),
            P(("ctx", "head"), None),
            P(("ctx", "head"), None),
            P(("ctx", "head"), None),
            P(("ctx", "head"), None),
        ),
        out_specs=(
            P(("ctx", "head"), None),
            P(("ctx", "head"), None),
            P(("ctx", "head"), None),
            P(("ctx", "head"), None),
            P(("ctx", "head"), None),
        ),
        check_vma=False,
    )
```

profile of v0, /device:TPU:24, one launch (start us, length us, event | category | flops | bytes accessed | tf_op | source)
XLA Modules:
  0.0 1469.7 jit_solution(11158650165822748649)
XLA Ops:
  0.7 5.5 all-to-all-start
  20.7 4.8 all-to-all-start.5
  27.6 6.0 all-to-all-done.5
  61.0 316.0 %custom-call.13 = f32[8,8,1,64,64]{3,4,2,1,0:T(8,128)} custom-call(f32[8,8,1,64,64]{4,3,2,1,0:T(8,128)} %add_bitcast_fusion), custom_call_target="InvertDiagBlocksLowerTriangular" | custom-call | tf_op jit(solution)/shard_map/jvp(jit(_solve_triangular))/vmap(vmap())/triangular_solve/custom-call.1 | solution.py:56
  384.6 9.3 bitcast_subtract_fusion
  393.8 5.4 copy.409
  416.6 5.0 all-to-all-start.1
  430.4 8.3 convolution_bitcast_fusion.6
  438.7 5.4 copy.410
  446.7 50.6 %while.67 = (s32[]{:T(128)}, f32[8,128,128]{1,2,0:T(8,128)S(1)}, f32[8,128,128]{1,2,0:T(8,128)}, f32[8,8,128,128]{2,3,1,0:T(8,128)}, f32[8,8,128,128]{2,3,1,0:T(...) while((s32[]{:T(128)}, f32[8,128,128]{1,2,0:T(8,128)S(1)}, ...), condition=%wide.region_5.7_spmd.clone, body=%wide.region_4.6_spmd.clone.sunk | while | flops 402915328 | bytes 6817887 | solution.py:78
  501.6 6.8 fusion.98
  508.5 9.2 fusion.62
  520.7 8.4 fusion.117
  530.0 533.4 %while.68 = (s32[]{:T(128)}, f32[8,128,128]{2,1,0:T(8,128)S(1)}, f32[8,128,128]{2,1,0:T(8,128)}, f32[8,128,128]{2,1,0:T(8,128)}, f32[8,128,128]{2,1,0:T(8,128)},...) while((s32[]{:T(128)}, f32[8,128,128]{2,1,0:T(8,128)S(1)}, ...), condition=%wide.region_8.10_spmd.clone, body=%wide.region_7.9_spmd.clone.sunk | while | flops 403308544 | bytes 7864503 | solution.py:166
  539.5 7.6 collective-permute-done
  556.7 7.6 collective-permute-done
  573.9 7.6 collective-permute-done
  591.1 7.6 collective-permute-done
  608.4 7.6 collective-permute-done
  625.6 7.6 collective-permute-done
  642.8 7.6 collective-permute-done
  660.0 7.6 collective-permute-done
  677.2 7.6 collective-permute-done
  694.4 7.6 collective-permute-done
  711.6 7.6 collective-permute-done
  728.8 7.6 collective-permute-done
  746.0 7.6 collective-permute-done
  763.2 7.6 collective-permute-done
  780.4 7.6 collective-permute-done
  797.6 7.6 collective-permute-done
  814.8 7.6 collective-permute-done
  832.0 7.6 collective-permute-done
  849.2 7.6 collective-permute-done
  866.5 7.6 collective-permute-done
  883.7 7.6 collective-permute-done
  900.9 7.6 collective-permute-done
  918.1 7.6 collective-permute-done
  935.3 7.6 collective-permute-done
  952.5 7.6 collective-permute-done
  969.7 7.6 collective-permute-done
  986.9 7.6 collective-permute-done
  1004.1 7.6 collective-permute-done
  1021.3 7.6 collective-permute-done
  1038.5 7.6 collective-permute-done
  1055.7 7.6 collective-permute-done
  1063.4 10.0 fusion.65
  1083.4 52.3 %while.66 = (s32[]{:T(128)}, f32[8,128,128]{1,2,0:T(8,128)S(1)}, f32[8,128,128]{1,2,0:T(8,128)}, f32[8,8,128,128]{2,3,1,0:T(8,128)}, f32[8,8,128,128]{2,3,1,0:T(...) while((s32[]{:T(128)}, f32[8,128,128]{1,2,0:T(8,128)S(1)}, ...), condition=%wide.region_3.5_spmd.clone, body=%wide.region_2.4_spmd.clone.sunk | while | flops 403046400 | bytes 7866472 | solution.py:78
  1135.7 7.4 bitcast_add_fusion
  1148.2 132.2 %while.65 = (s32[]{:T(128)}, f32[8,128,128]{1,2,0:T(8,128)}, f32[8,128,128]{1,2,0:T(8,128)}, f32[8,8,128,128]{3,2,1,0:T(8,128)}, f32[8,8,128,128]{2,3,1,0:T(8,12...) while((s32[]{:T(128)}, f32[8,128,128]{1,2,0:T(8,128)}, ...), condition=%wide.region_12.14_spmd, body=%wide.region_11.13_spmd.sunk | while | flops 805699584 | bytes 15206573 | solution.py:78
  1280.4 10.4 fusion.54
  1290.9 6.2 fusion.109
  1297.1 8.3 fusion.56
  1305.4 8.2 fusion.100
  1333.3 4.8 fusion.68
  1340.0 6.0 fusion.112
  1353.5 5.7 multiply_reduce_fusion.2
  1359.2 6.4 multiply_reduce_fusion
  1366.4 4.8 all-to-all-start.10
  1375.6 6.5 fusion.115
  1382.1 5.3 bitcast_reduce_fusion
  1396.5 10.3 bitcast_reduce_fusion.1
  1414.0 5.0 all-to-all-start.9
  1445.8 6.1 all-to-all-done.6
  1458.5 7.8 all-to-all-done.8
  (637 shorter events, 720.4 us)
Async XLA Ops:
  0.7 10.8 all-to-all-start
  20.7 12.8 all-to-all-start.5
  33.6 11.5 all-to-all-start.3
  45.1 371.6 %all-to-all-start.4 = ((bf16[128,4,1024]{2,0,1:T(8,128)(2,1)}), bf16[128,4,1024]{2,0,1:T(8,128)(2,1)}, u32[]{:S(2)}, u32[]{:S(2)}) async-start(bf16[128,4,1024]{2,0,1:T(8,128)(2,1)} %bitcast.322), calls=%async_computation.4 | async-start | bytes 2097152 | tf_op jit(solution)/shard_map/all_to_all | solution.py:128
  416.6 80.6 %all-to-all-start.1 = ((bf16[128,4,1024]{2,0,1:T(8,128)(2,1)}), bf16[128,4,1024]{2,0,1:T(8,128)(2,1)}, u32[]{:S(2)}, u32[]{:S(2)}) async-start(bf16[128,4,1024]{2,0,1:T(8,128)(2,1)} %bitcast.408), calls=%async_computation.1 | async-start | bytes 2097152 | tf_op jit(solution)/shard_map/all_to_all | solution.py:131
  532.6 14.5 collective-permute-start.1
  537.1 10.0 collective-permute-start
  549.8 14.5 collective-permute-start.1
  554.3 10.0 collective-permute-start
  567.0 14.5 collective-permute-start.1
  571.5 10.0 collective-permute-start
  584.3 14.5 collective-permute-start.1
  588.7 10.0 collective-permute-start
  601.5 14.5 collective-permute-start.1
  605.9 10.0 collective-permute-start
  618.7 14.5 collective-permute-start.1
  623.2 10.0 collective-permute-start
  635.9 14.5 collective-permute-start.1
  640.4 10.0 collective-permute-start
  653.1 14.5 collective-permute-start.1
  657.6 10.0 collective-permute-start
  670.3 14.5 collective-permute-start.1
  674.8 10.0 collective-permute-start
  687.5 14.5 collective-permute-start.1
  692.0 10.0 collective-permute-start
  704.7 14.5 collective-permute-start.1
  709.2 10.0 collective-permute-start
  721.9 14.5 collective-permute-start.1
  726.4 10.0 collective-permute-start
  739.1 14.5 collective-permute-start.1
  743.6 10.0 collective-permute-start
  756.3 14.5 collective-permute-start.1
  760.8 10.0 collective-permute-start
  773.5 14.5 collective-permute-start.1
  778.0 10.0 collective-permute-start
  790.7 14.5 collective-permute-start.1
  795.2 10.0 collective-permute-start
  807.9 14.5 collective-permute-start.1
  812.4 10.0 collective-permute-start
  825.2 14.5 collective-permute-start.1
  829.6 10.0 collective-permute-start
  842.4 14.5 collective-permute-start.1
  846.8 10.0 collective-permute-start
  859.6 14.5 collective-permute-start.1
  864.1 10.0 collective-permute-start
  876.8 14.5 collective-permute-start.1
  881.3 10.0 collective-permute-start
  894.0 14.5 collective-permute-start.1
  898.5 10.0 collective-permute-start
  911.2 14.5 collective-permute-start.1
  928.4 14.5 collective-permute-start.1
  945.6 14.5 collective-permute-start.1
  962.8 14.5 collective-permute-start.1
  967.3 10.0 collective-permute-start
  980.0 14.5 collective-permute-start.1
  997.2 14.5 collective-permute-start.1
  1014.4 14.5 collective-permute-start.1
  1031.6 14.5 collective-permute-start.1
  1048.8 14.5 collective-permute-start.1
  1366.4 47.6 %all-to-all-start.10 = ((bf16[4,128,8]{1,2,0:T(8,128)(2,1)}), bf16[4,128,8]{1,2,0:T(8,128)(2,1)S(1)}, u32[]{:S(2)}, u32[]{:S(2)}) async-start(bf16[4,128,8]{1,2,0:T(8,128)(2,1)} %copy.468), calls=%async_computation.10 | async-start | bytes 16384 | tf_op jit(solution)/shard_map/all_to_all | solution.py:181
  1414.0 10.3 all-to-all-start.9
  1424.3 14.8 %all-to-all-start.7 = ((bf16[4,128,512]{1,2,0:T(8,128)(2,1)}), bf16[4,128,512]{1,2,0:T(8,128)(2,1)}, u32[]{:S(2)}, u32[]{:S(2)}) async-start(bf16[4,128,512]{1,2,0:T(8,128)(2,1)} %fusion.124), calls=%async_computation.7 | async-start | bytes 1048576 | tf_op jit(solution)/shard_map/all_to_all | solution.py:178
  1439.1 12.8 all-to-all-start.6
  1451.9 14.4 all-to-all-start.8
  (92 other events, 1150.5 us)
where the time goes:
time: 1480 us; the launch traced here: 1470 us
  matrix products  502 us (34%)
  other arithmetic  356 us (24%)
  waiting for transfers between devices  266 us (18%)
  starting transfers between devices  182 us (12%)
  local copies, waits for them, and re-layouts  159 us (11%)
    another operation x4, other arithmetic, layer_terms(): jax.scipy.linalg.solve_triangular(system, (strength * growth)[..., None]...  319 us
    ppermute x62, waiting for transfers between devices, shifted(): return lax.ppermute(shard, axis, pairs)  236 us
    ppermute x62, starting transfers between devices, shifted(): return lax.ppermute(shard, axis, pairs)  133 us
    dot_general x31, matrix products, relay(): jnp.einsum('hvk,hkl->hvl', behind, back_map, precision=highest) + local_grad  82.3 us
    dot_general x32, matrix products, advance(): jnp.einsum('hvl,hlm->hvm', running_add, step_map, precision=highest)  81.4 us
    dot_general x31, matrix products, relay(): jnp.einsum('hvk,hkl->hvl', forward_state, total_map, precision=highest)  79.6 us
    dot_general x32, matrix products, advance(): jnp.einsum('hkl,hlm->hkm', running_map, step_map, precision=highest)  72.8 us
    unnamed x163, local copies, waits for them, and re-layouts  36.6 us
  transfers between devices with their start and end apart: 73, of which 37 were waited for; matrix products, arithmetic and copies ran while one was open for 40% of the time, Pallas kernels for 0%

commit v1 on v0

v1 whole, which is shorter than its diff:
```python
import functools

import jax
import jax.numpy as jnp
from jax import lax
from jax.experimental import pallas as pl
from jax.experimental.pallas import tpu as pltpu
from jax.sharding import PartitionSpec as P

DK = 128
DV = 128
CHUNK = 128
EPS = 1e-06
QUERY_SCALE = DK ** (-0.5)

f32 = jnp.float32
bf16 = jnp.bfloat16

NN = (((1,), (0,)), ((), ()))
NT = (((1,), (1,)), ((), ()))
TN = (((0,), (0,)), ((), ()))


def dot(a, b, dims=NN):
    return lax.dot_general(a, b, dims, preferred_element_type=f32)


def low(x):
    return x.astype(bf16)


def split(x):
    high = x.astype(bf16)
    return high, (x - high.astype(f32)).astype(bf16)


def twice(a, axis):
    return jnp.concatenate([a, a], axis=axis)


def wide(x, axis):
    return jnp.concatenate(split(x), axis=axis)


def dot3(a, b, dims=NN):
    (ca,), (cb,) = dims[0]
    ah, al = split(a)
    bh, bl = split(b)
    return dot(
        jnp.concatenate([ah, al, ah], axis=ca), jnp.concatenate([bh, bh, bl], axis=cb), dims
    )


def grids(shape=(CHUNK, CHUNK)):
    return lax.broadcasted_iota(jnp.int32, shape, 0), lax.broadcasted_iota(jnp.int32, shape, 1)


def chunk_terms(pair, q, k, small):
    row, col = grids()
    causal = row >= col
    before = row > col
    eye = row == col
    key_key = dot(k, k, NT)
    query_key = dot(q, k, NT)
    qf = q.astype(f32)
    kf = k.astype(f32)
    rk_col = lax.rsqrt(jnp.sum(kf * kf, axis=1, keepdims=True) + EPS)
    rk_row = lax.rsqrt(jnp.sum(jnp.where(eye, key_key, 0.0), axis=0, keepdims=True) + EPS)
    rq_col = lax.rsqrt(jnp.sum(qf * qf, axis=1, keepdims=True) + EPS) * QUERY_SCALE
    key_key = key_key * (rk_col * rk_row)
    query_key = query_key * (rq_col * rk_row)
    lower = jnp.where(causal, 1.0, 0.0).astype(bf16)
    upper = jnp.where(row <= col, 1.0, 0.0).astype(bf16)
    ident = jnp.where(eye, 1.0, 0.0).astype(bf16)
    growth_cols = dot(lower, small)
    growth_rows = dot(small, upper, TN)
    small_rows = dot(small, ident, TN)
    small_cols = small.astype(f32)
    heads = []
    for i in range(2):
        at = 2 * pair + i
        g_col = jnp.sum(jnp.where(col == at, growth_cols, 0.0), axis=1, keepdims=True)
        g_row = jnp.sum(jnp.where(row == at, growth_rows, 0.0), axis=0, keepdims=True)
        b_col = jnp.sum(jnp.where(col == at + 8, small_cols, 0.0), axis=1, keepdims=True)
        b_row = jnp.sum(jnp.where(row == at + 8, small_rows, 0.0), axis=0, keepdims=True)
        g_end = g_col[CHUNK - 1 : CHUNK, :]
        decay = jnp.where(causal, jnp.exp(jnp.minimum(g_col - g_row, 0.0)), 0.0)
        heads.append(
            dict(
                decay=decay,
                beta_col=1.0 / (1.0 + jnp.exp(-b_col)),
                beta_row=1.0 / (1.0 + jnp.exp(-b_row)),
                growth_col=jnp.exp(g_col),
                growth_row=jnp.exp(g_row),
                to_end=jnp.exp(g_end - g_col),
                keep=jnp.exp(g_end),
            )
        )
    return dict(
        key_key=key_key,
        query_key=query_key,
        rk_col=rk_col,
        rk_row=rk_row,
        rq_col=rq_col,
        qf=qf,
        kf=kf,
        heads=heads,
    )


def inverses(systems):
    row, col = grids()
    ident = jnp.where(row == col, 1.0, 0.0)
    first = (row // 2 == col // 2) & (row > col)
    found = [ident - jnp.where(first, a, 0.0) for a in systems]
    size = 2
    while size < CHUNK:
        merge = (row // (2 * size) == col // (2 * size)) & (row // size > col // size)
        parts = [low(jnp.where(merge, a, 0.0)) for a in systems]
        lows = [low(t) for t in found]
        inner = [dot(part, t) for part, t in zip(parts, lows)]
        found = [t - dot(tl, low(x)) for t, tl, x in zip(found, lows, inner)]
        size *= 2
    rests = [ident - t - dot3(a, t) for a, t in zip(systems, found)]
    return [t + dot(low(t), low(x)) for t, x in zip(found, rests)]


def local_kernel(q_ref, k_ref, v_ref, o_ref, s_ref, send_ref, w_ref, f_ref, t_ref, u_ref, d_ref, a_ref, l_ref):
    pair = pl.program_id(0)
    row, col = grids()
    before = row > col
    chunks = q_ref.shape[0]
    terms = [chunk_terms(pair, q_ref[c], k_ref[c], s_ref[c]) for c in range(chunks)]
    systems = []
    for c in range(chunks):
        for h in terms[c]["heads"]:
            systems.append(
                jnp.where(before, h["beta_col"] * h["decay"] * terms[c]["key_key"], 0.0)
            )
    solved = inverses(systems)
    devs = [[None] * chunks, [None] * chunks]
    adds = [[None] * chunks, [None] * chunks]
    backs = [[None] * chunks, [None] * chunks]
    for c in range(chunks):
        q, k = q_ref[c], k_ref[c]
        term = terms[c]
        for i in range(2):
            h = term["heads"][i]
            t = solved[2 * c + i]
            v = v_ref[c, :, i * DV : (i + 1) * DV]
            o = o_ref[c, :, i * DV : (i + 1) * DV]
            key_part = dot(
                wide(t * (h["beta_row"] * h["growth_row"] * term["rk_row"]), 1), twice(k, 0)
            )
            value_part = dot(wide(t * h["beta_row"], 1), twice(v, 0))
            to_end = term["rk_col"] * h["to_end"]
            both = jnp.concatenate([-(to_end * key_part), to_end * value_part], axis=1)
            stepped = dot(wide(both, 0), twice(k, 0), TN)
            dev, add = stepped[:DK], stepped[DK:]
            weights = h["decay"] * term["query_key"]
            fresh = dot(wide(weights, 0), twice(o, 0), TN)
            fh, fl = split(fresh)
            wh, wl = split(key_part)
            oh, ol = split(o.astype(f32) * (h["growth_col"] * term["rq_col"]))
            back = dot(
                jnp.concatenate([oh, ol, -fh, -fl, -fh], axis=0),
                jnp.concatenate([q, q, wh, wh, wl], axis=0),
                TN,
            )
            w_ref[i, c] = key_part
            f_ref[i, c] = value_part
            t_ref[i, c] = low(t)
            u_ref[i, c] = fresh
            d_ref[i, c] = dev
            a_ref[i, c] = add
            l_ref[i, c] = back
            devs[i][c], adds[i][c], backs[i][c] = dev, add, back
    for i in range(2):
        keeps = [terms[c]["heads"][i]["keep"] for c in range(chunks)]
        stack = jnp.concatenate([devs[i][0], adds[i][0]], axis=0)
        keep = keeps[0]
        for c in range(1, chunks):
            stack = (
                keeps[c] * stack
                + dot3(stack, devs[i][c])
                + jnp.concatenate([keep * devs[i][c], adds[i][c]], axis=0)
            )
            keep = keep * keeps[c]
        grad = backs[i][chunks - 1]
        for c in reversed(range(chunks - 1)):
            grad = keeps[c] * grad + dot3(grad, devs[i][c], NT) + backs[i][c]
        dev, add = stack[:DK], stack[DK:]
        high, rest = split(keep)
        middle, last = split(keep - high.astype(f32))
        line = lax.broadcasted_iota(jnp.int32, (16, DK), 0)
        scale = low(
            jnp.where(
                line == 0,
                high.astype(f32),
                jnp.where(line == 1, middle.astype(f32), jnp.where(line == 2, last.astype(f32), 0.0)),
            )
        )
        forward, backward = low(dev), low(dev.T)
        for part in range(4):
            half = slice((part % 2) * (DV // 2), (part % 2 + 1) * (DV // 2))
            send_ref[i, part, :DK] = forward if part < 2 else backward
            send_ref[i, part, DK : DK + DV // 2] = low((add if part < 2 else grad)[half])
            send_ref[i, part, DK + DV // 2 :] = scale


def chain_kernel(order_ref, x_ref, out_ref):
    count = x_ref.shape[0]
    state = jnp.zeros((DV // 2, DK), f32)
    flip = order_ref[0]
    for step in range(count):
        at = jnp.where(flip == 1, count - 1 - step, step)
        out_ref[at] = low(state)
        if step < count - 1:
            block = x_ref[at]
            scale = jnp.sum(block[DK + DV // 2 :].astype(f32), axis=0, keepdims=True)
            state = (
                state * scale
                + dot(wide(state, 1), twice(block[:DK], 0))
                + block[DK : DK + DV // 2].astype(f32)
            )


def final_kernel(q_ref, k_ref, v_ref, o_ref, s_ref, w_ref, f_ref, t_ref, u_ref, d_ref, a_ref, l_ref, h_ref, out_ref):
    pair = pl.program_id(0)
    row, col = grids()
    before = row > col
    causal = row >= col
    suffix = jnp.where(row <= col, 1.0, 0.0).astype(bf16)
    chunks = q_ref.shape[0]
    terms = [chunk_terms(pair, q_ref[c], k_ref[c], s_ref[c]) for c in range(chunks)]
    states, grads = [], []
    for i in range(2):
        state = [h_ref[i, 0].astype(f32)]
        for c in range(chunks):
            now = state[c]
            state.append(
                terms[c]["heads"][i]["keep"] * now + dot3(now, d_ref[i, c]) + a_ref[i, c]
            )
        grad = [None] * chunks
        grad[chunks - 1] = h_ref[i, 1].astype(f32)
        for c in reversed(range(1, chunks)):
            now = grad[c]
            grad[c - 1] = (
                terms[c]["heads"][i]["keep"] * now + dot3(now, d_ref[i, c], NT) + l_ref[i, c]
            )
        states.append(state)
        grads.append(grad)

    key_heads = 4
    wide_q = key_heads * DK
    for c in range(chunks):
        q, k = q_ref[c], k_ref[c]
        term = terms[c]
        rk_col, rk_row, rq_col = term["rk_col"], term["rk_row"], term["rq_col"]
        query_unit = term["qf"] * rq_col
        key_unit = term["kf"] * rk_col
        read_sum = 0.0
        erase_sum = 0.0
        query_unit_grad = 0.0
        key_unit_grad = 0.0
        small_out = 0.0
        for i in range(2):
            h = term["heads"][i]
            o = o_ref[c, :, i * DV : (i + 1) * DV]
            state, after, grad = states[i][c], states[i][c + 1], grads[i][c]
            fresh = f_ref[i, c] - dot3(w_ref[i, c], state, NT)
            fresh_grad = u_ref[i, c] + (rk_col * h["to_end"]) * dot(
                twice(k, 1), wide(grad, 1), NT
            )
            solved = dot(twice(t_ref[i, c], 0), wide(fresh_grad, 0), TN)
            value_grad = h["beta_col"] * solved
            base = 2 * wide_q + pair * (2 * DV) + i * DV
            out_ref[c, :, pl.ds(pl.multiple_of(base, DV), DV)] = low(value_grad)
            sides = jnp.concatenate([low(value_grad), o], axis=0)
            fresh_low = low(fresh)
            inner = dot(sides, fresh_low, NT)
            outer = dot(sides, low(state))
            ended = h["to_end"] * dot(fresh_low, low(grad))
            erase = jnp.where(before, h["decay"] * inner[:CHUNK], 0.0)
            read = h["decay"] * inner[CHUNK:]
            key_read = -h["growth_col"] * outer[:CHUNK]
            query_read = h["growth_col"] * outer[CHUNK:]
            spread = read * term["query_key"] - erase * term["key_key"]
            lone = jnp.sum(
                query_unit * query_read + key_unit * (key_read - ended), axis=1, keepdims=True
            )
            lone = jnp.broadcast_to(lone, (CHUNK, CHUNK))
            sums = dot(twice(suffix, 1), wide(jnp.concatenate([spread, lone], axis=1), 0))
            decay_grad = (
                jnp.sum(jnp.where(before, sums[:, :CHUNK], 0.0), axis=1, keepdims=True)
                + sums[:, CHUNK : CHUNK + 1]
                + jnp.sum(jnp.sum(grad * after, axis=1, keepdims=True), axis=0, keepdims=True)
            )
            beta_grad = (1.0 - h["beta_col"]) * jnp.sum(solved * fresh, axis=1, keepdims=True)
            at = 2 * pair + i
            small_out = small_out + jnp.where(col == at, decay_grad, 0.0)
            small_out = small_out + jnp.where(col == at + 8, beta_grad, 0.0)
            read_sum = read_sum + read
            erase_sum = erase_sum + erase
            query_unit_grad = query_unit_grad + query_read
            key_unit_grad = key_unit_grad + key_read + ended
        query_unit_grad = query_unit_grad + dot(wide(read_sum * rk_row, 1), twice(k, 0))
        both = (erase_sum + erase_sum.T) * rk_row
        rh, rl = split((read_sum * rq_col).T)
        bh, bl = split(-both)
        key_unit_grad = key_unit_grad + dot(
            jnp.concatenate([rh, rl, bh, bl], axis=1), jnp.concatenate([q, q, k, k], axis=0)
        )
        query_back = rq_col * (
            query_unit_grad
            - query_unit
            * (DK * jnp.sum(query_unit * query_unit_grad, axis=1, keepdims=True))
        )
        key_back = rk_col * (
            key_unit_grad
            - key_unit * jnp.sum(key_unit * key_unit_grad, axis=1, keepdims=True)
        )
        out_ref[c, :, pl.ds(pl.multiple_of(pair * DK, DK), DK)] = low(query_back)
        out_ref[c, :, pl.ds(pl.multiple_of(wide_q + pair * DK, DK), DK)] = low(key_back)
        place = slice(2 * wide_q + 8 * DV, 2 * wide_q + 8 * DV + 128)
        small_out = low(small_out)
        mine = (col // 2 == pair) | (col // 2 == pair + 4)
        held = out_ref[c, :, place]
        out_ref[c, :, place] = jnp.where(mine, small_out, jnp.where(pair == 0, jnp.zeros_like(held), held))


KEY_HEADS = 4
HEADS = 8
CHUNKS = 4
SMALL_AT = 2 * KEY_HEADS * DK + 2 * HEADS * DV
IN_WIDTH = SMALL_AT + 128
OUT_WIDTH = 2 * KEY_HEADS * DK + HEADS * DV + 128
PAYLOAD = DK + DV // 2 + 16
VMEM = 56 << 20


def packed_specs():
    return [
        pl.BlockSpec((CHUNKS, CHUNK, DK), lambda p: (0, 0, p)),
        pl.BlockSpec((CHUNKS, CHUNK, DK), lambda p: (0, 0, KEY_HEADS + p)),
        pl.BlockSpec((CHUNKS, CHUNK, 2 * DV), lambda p: (0, 0, KEY_HEADS + p)),
        pl.BlockSpec((CHUNKS, CHUNK, 2 * DV), lambda p: (0, 0, 2 * KEY_HEADS + p)),
        pl.BlockSpec((CHUNKS, CHUNK, 128), lambda p: (0, 0, SMALL_AT // 128)),
    ]


SAVED = (f32, f32, bf16, f32, f32, f32, f32)


def saved_specs():
    return [pl.BlockSpec((2, CHUNKS, CHUNK, CHUNK), lambda p: (p, 0, 0, 0)) for _ in SAVED]


def local_pass(packed):
    return pl.pallas_call(
        local_kernel,
        grid=(KEY_HEADS,),
        in_specs=packed_specs(),
        out_specs=[pl.BlockSpec((2, 4, PAYLOAD, DK), lambda p: (p, 0, 0, 0))] + saved_specs(),
        out_shape=[jax.ShapeDtypeStruct((HEADS, 4, PAYLOAD, DK), bf16)]
        + [jax.ShapeDtypeStruct((HEADS, CHUNKS, CHUNK, CHUNK), kind) for kind in SAVED],
        compiler_params=pltpu.CompilerParams(vmem_limit_bytes=VMEM),
        name="local_pass",
    )(*([packed] * 5))


def chain_pass(flip, received):
    count = received.shape[0]
    return pl.pallas_call(
        chain_kernel,
        in_specs=[
            pl.BlockSpec(memory_space=pltpu.SMEM),
            pl.BlockSpec(memory_space=pltpu.VMEM),
        ],
        out_specs=pl.BlockSpec(memory_space=pltpu.VMEM),
        out_shape=jax.ShapeDtypeStruct((count, DV // 2, DK), bf16),
        compiler_params=pltpu.CompilerParams(vmem_limit_bytes=VMEM),
        name="chain_pass",
    )(flip, received)


def final_pass(packed, saved, states):
    return pl.pallas_call(
        final_kernel,
        grid=(KEY_HEADS,),
        in_specs=packed_specs()
        + saved_specs()
        + [pl.BlockSpec((2, 2, DV, DK), lambda p: (p, 0, 0, 0))],
        out_specs=pl.BlockSpec((CHUNKS, CHUNK, OUT_WIDTH), lambda p: (0, 0, 0)),
        out_shape=jax.ShapeDtypeStruct((CHUNKS, CHUNK, OUT_WIDTH), bf16),
        compiler_params=pltpu.CompilerParams(vmem_limit_bytes=VMEM),
        name="final_pass",
    )(*([packed] * 5), *saved, states)


def pack(arrays):
    split_up = [a.reshape(a.shape[0], CHUNKS, -1) for a in arrays]
    filled = sum(a.shape[2] for a in split_up)
    split_up.append(jnp.zeros((CHUNK, CHUNKS, IN_WIDTH - filled), bf16))
    return jnp.concatenate(split_up, axis=2).transpose(1, 0, 2)


def unpack(packed):
    tokens_first = packed.transpose(1, 0, 2)
    outs = []
    at = 0
    for width in (KEY_HEADS * DK, KEY_HEADS * DK, HEADS * DV, HEADS, HEADS):
        outs.append(tokens_first[:, :, at : at + width].reshape(CHUNK, -1))
        at += width
    return tuple(outs)


def on_device(query_rows, key_rows, value_rows, log_decay, beta_logit, out_grad):
    packed = lax.all_to_all(
        pack([query_rows, key_rows, value_rows, out_grad, log_decay, beta_logit]),
        "head",
        split_axis=0,
        concat_axis=0,
        tiled=True,
    )
    sends, *saved = local_pass(packed)
    segments = lax.axis_size("ctx")
    received = lax.all_to_all(
        sends.reshape(segments, PAYLOAD, DK), "ctx", split_axis=0, concat_axis=0, tiled=True
    )
    flip = (lax.axis_index("ctx") % 4 >= 2).astype(jnp.int32).reshape(1)
    chained = chain_pass(flip, received)
    states = lax.all_to_all(chained, "ctx", split_axis=0, concat_axis=0, tiled=True)
    grads = final_pass(packed, saved, states.reshape(HEADS, 2, DV, DK))
    return unpack(lax.all_to_all(grads, "head", split_axis=0, concat_axis=0, tiled=True))


def solution(mesh):
    spec = P(("ctx", "head"), None)
    return jax.shard_map(
        on_device, mesh=mesh, in_specs=(spec,) * 6, out_specs=(spec,) * 5, check_vma=False
    )
```

time: 1480 us -> 215 us (0.15)
  matrix products: 502 us -> 0 us
  other arithmetic: 356 us -> 0 us
  waiting for transfers between devices: 266 us -> 23.1 us
  starting transfers between devices: 182 us -> 7.38 us
  local copies, waits for them, and re-layouts: 159 us -> 22.4 us
  blocking collectives: 0 us -> 92.6 us
  Pallas kernels: 0 us -> 65.9 us
    dot_general x152 -> x0, matrix products: 478 us -> none  [the longest x31 82.3 us: relay(): jnp.einsum('hvk,hkl->hvl', behind, back_map, precision=highest) + local_grad]
    another operation x6 -> x0, other arithmetic: 324 us -> none  [the longest x4 319 us: layer_terms(): jax.scipy.linalg.solve_triangular(system, (strength * growth)[..., None]...]
    ppermute x62 -> x0, waiting for transfers between devices: 236 us -> none  [shifted(): return lax.ppermute(shard, axis, pairs)]
    ppermute x62 -> x0, starting transfers between devices: 133 us -> none  [shifted(): return lax.ppermute(shard, axis, pairs)]
    all_to_all x0 -> x3, blocking collectives: none -> 92.6 us  [the longest x1 44.2 us: on_device(): lax.all_to_all(pack([query_rows, key_rows, value_rows, out_grad, log_deca...]
    pallas_call x0 -> x3, Pallas kernels: none -> 65.9 us  [the longest x1 31 us: final_pass(): pl.pallas_call(final_kernel, grid=(KEY_HEADS,), in_specs=packed_specs() +...]
    all_to_all x11 -> x1, starting transfers between devices: 48.6 us -> 7.38 us  [on_device(): lax.all_to_all(sends.reshape(segments, PAYLOAD, DK), 'ctx', split_axis=0,...]
    dynamic_slice x16 -> x0, local copies, waits for them, and re-layouts: 31.3 us -> none  [layer_terms(): lax.scan(advance, start, (jnp.moveaxis(block_map, 1, 0), jnp.moveaxis(blo...]
  transfers between devices with their start and end apart: 73 -> 1, of which waited for: 37 -> 1; matrix products, arithmetic and copies ran while one was open for 40% -> 0% of each run, Pallas kernels for 0% -> 0%
where the time goes in v1:
time: 215 us; the launch traced here: 212 us
  blocking collectives  92.6 us (43%)
  Pallas kernels  65.9 us (31%)
  waiting for transfers between devices  23.1 us (11%)
  local copies, waits for them, and re-layouts  22.4 us (10%)
  starting transfers between devices  7.38 us (3%)
    all_to_all x1, blocking collectives, on_device(): lax.all_to_all(pack([query_rows, key_rows, value_rows, out_grad, log_deca...  44.2 us
    all_to_all x1, blocking collectives, on_device(): lax.all_to_all(grads, 'head', split_axis=0, concat_axis=0, tiled=True)  32 us
    pallas_call x1, Pallas kernels, final_pass(): pl.pallas_call(final_kernel, grid=(KEY_HEADS,), in_specs=packed_specs() +...  31 us
    pallas_call x1, Pallas kernels, local_pass(): pl.pallas_call(local_kernel, grid=(KEY_HEADS,), in_specs=packed_specs(),...  28.8 us
    all_to_all x1, waiting for transfers between devices, on_device(): lax.all_to_all(sends.reshape(segments, PAYLOAD, DK), 'ctx', split_axis=0,...  23.1 us
    all_to_all x1, blocking collectives, on_device(): lax.all_to_all(chained, 'ctx', split_axis=0, concat_axis=0, tiled=True)  16.3 us
    unnamed x15, local copies, waits for them, and re-layouts  7.54 us
    all_to_all x1, starting transfers between devices, on_device(): lax.all_to_all(sends.reshape(segments, PAYLOAD, DK), 'ctx', split_axis=0,...  7.38 us
  transfers between devices with their start and end apart: 1, of which 1 were waited for; matrix products, arithmetic and copies ran while one was open for 0% of the time, Pallas kernels for 0%

profile of v1, /device:TPU:24, one launch (start us, length us, event | category | flops | bytes accessed | tf_op | source)
XLA Modules:
  0.0 212.0 jit_solution(8819789670361516956)
XLA Ops:
  0.6 0.0 copy-start.3
  0.6 0.9 copy.19
  1.6 0.9 copy.20
  2.4 0.0 copy-start.1
  2.4 1.4 copy.11
  3.8 1.0 copy.15
  4.9 0.0 copy-done.3
  4.9 0.3 copy.12
  5.1 1.0 copy.16
  6.1 0.0 copy-done.1
  6.1 0.0 copy-start.2
  6.2 0.7 copy.13
  6.8 1.3 copy.17
  8.1 0.0 copy-done.2
  8.1 0.7 copy.14
  8.8 1.3 copy.18
  10.1 0.7 broadcast_in_dim.3
  10.8 4.8 %concatenate.3 = bf16[128,4,3200]{2,0,1:T(8,128)(2,1)S(1)} concatenate(bf16[128,4,512]{2,0,1:T(8,128)(2,1)} %copy.15, bf16[128,4,512]{2,0,1:T(8,128)(2,1)} %copy.16, bf16[128,4,1024]{2,0,1:T(8,128)(2,1)} %copy.17, bf16[128,4,1024]{2,0,1:T(8,128)(2,1)} %copy.18, bf16[128,4,8]{2,0,1:T(8,128)(2,1)S(1)} %copy.19, bf16[128,4,8]{2,0,1:T(8,128)(2,1)S(1)} %copy.20, ...), dimensions={2} | concatenate | bytes 6553600 | tf_op jit(solution)/shard_map/concatenate | solution.py:405
  15.6 44.2 %all_to_all.20.q_ref.k_ref.v_ref.o_ref.s_ref = bf16[4,128,3200]{2,1,0:T(8,128)(2,1)} all-to-all(bf16[4,128,3200]{2,1,0:T(8,128)(2,1)S(1)} %bitcast.16), channel_id=1, replica_groups=mesh['ctx'=32,'head'=4] {'head'}, dimensions={0} | all-to-all | bytes 6553600 | tf_op jit(solution)/shard_map/all_to_all | solution.py:419
  59.8 28.8 %local_pass.1 = (bf16[8,4,208,128]{3,2,1,0:T(8,128)(2,1)}, f32[8,4,128,128]{3,2,1,0:T(8,128)}, f32[8,4,128,128]{3,2,1,0:T(8,128)}, bf16[8,4,128,128]{3,2,1,0:T(8...) custom-call(bf16[4,128,3200]{2,1,0:T(8,128)(2,1)} %all_to_all.20.q_r, ...), custom_call_target="tpu_custom_call" | custom-call | tf_op jit(solution)/shard_map/local_pass/pallas_call | solution.py:360
  88.6 7.4 %all-to-all-start.1 = ((bf16[32,208,128]{2,1,0:T(8,128)(2,1)}), bf16[32,208,128]{2,1,0:T(8,128)(2,1)S(1)}, u32[]{:S(2)}, u32[]{:S(2)}) async-start(bf16[32,208,128]{2,1,0:T(8,128)(2,1)} %bitcast.28), calls=%async_computation.1 | async-start | bytes 3407872 | tf_op jit(solution)/shard_map/all_to_all | solution.py:428
  96.0 23.1 %all-to-all-done.1.x_ref = bf16[32,208,128]{2,1,0:T(8,128)(2,1)S(1)} async-done(((bf16[32,208,128]{2,1,0:T(8,128)(2,1)}), bf16[32,208,128]{2,1,0:T(8,128)(2,1)S(1)}, u32[]{:S(2)}, u32[]{:S(2)}) %all-to-all-start.1) | async-done | bytes 1703968 | tf_op jit(solution)/shard_map/all_to_all | solution.py:428
  119.1 0.0 copy-start
  119.1 1.2 copy-done
  120.3 6.1 %chain_pass.1 = bf16[32,64,128]{2,1,0:T(8,128)(2,1)} custom-call(s32[1]{0:T(128)} %bitcast.7.order_ref, bf16[32,208,128]{2,1,0:T(8,128)(2,1)} %copy-done), custom_call_target="tpu_custom_call" | custom-call | tf_op jit(solution)/shard_map/chain_pass/pallas_call | solution.py:374
  126.4 16.3 %all_to_all.21 = bf16[32,64,128]{2,1,0:T(8,128)(2,1)} all-to-all(bf16[32,64,128]{2,1,0:T(8,128)(2,1)} %chain_pass.1), channel_id=1, replica_groups=mesh['ctx'=32,'head'=4] {'ctx'}, dimensions={0} | all-to-all | bytes 1048576 | tf_op jit(solution)/shard_map/all_to_all | solution.py:433
  142.7 31.0 %final_pass.1 = bf16[4,128,2176]{2,1,0:T(8,128)(2,1)} custom-call(bf16[4,128,3200]{2,1,0:T(8,128)(2,1)} %all_to_all.20.q_ref.k_ref.v_ref.o_ref.s_ref, bf16[4,128,3200]{2,1,0:T(8,128)(2,1)} %all_to_all.20.q_ref.k_ref.v_ref.o_ref.s_ref, bf16[4,128,3200]{2,1,0:T(8,128)(2,1)} %all_to_all.20.q_ref.k_ref.v_ref.o_ref.s_ref, ...), custom_call_target="tpu_custom_call" | custom-call | tf_op jit(solution)/shard_map/final_pass/pallas_call | solution.py:388
  173.7 32.0 %all_to_all.22 = bf16[4,128,2176]{2,1,0:T(8,128)(2,1)S(1)} all-to-all(bf16[4,128,2176]{2,1,0:T(8,128)(2,1)} %final_pass.1), channel_id=1, replica_groups=mesh['ctx'=32,'head'=4] {'head'}, dimensions={0} | all-to-all | bytes 4456448 | tf_op jit(solution)/shard_map/all_to_all | solution.py:435
  205.8 0.1 fusion
  205.9 0.1 slice.22
  206.0 0.1 fusion.1
  206.1 0.7 copy.25
  206.8 0.7 copy.24
  207.5 0.3 copy.22
  207.8 1.0 copy.27
  208.8 0.7 copy.23
  209.4 1.3 copy.28
  210.8 0.3 copy.21
  211.0 1.0 copy.26
Async XLA Ops:
  0.6 4.2 %copy-start.3 = (bf16[128,2048]{1,0:T(8,128)(2,1)S(1)}, bf16[128,2048]{1,0:T(8,128)(2,1)}, u32[]{:S(2)}) copy-start(bf16[128,2048]{1,0:T(8,128)(2,1)} %param.7) | copy-start | bytes 1572868
  2.4 3.7 %copy-start.1 = (bf16[128,4096]{1,0:T(8,128)(2,1)S(1)}, bf16[128,4096]{1,0:T(8,128)(2,1)}, u32[]{:S(2)}) copy-start(bf16[128,4096]{1,0:T(8,128)(2,1)} %param.8) | copy-start | bytes 3145732
  6.1 2.0 copy-start.2
  88.6 30.5 %all-to-all-start.1 = ((bf16[32,208,128]{2,1,0:T(8,128)(2,1)}), bf16[32,208,128]{2,1,0:T(8,128)(2,1)S(1)}, u32[]{:S(2)}, u32[]{:S(2)}) async-start(bf16[32,208,128]{2,1,0:T(8,128)(2,1)} %bitcast.28), calls=%async_computation.1 | async-start | bytes 3407872 | tf_op jit(solution)/shard_map/all_to_all | solution.py:428
  119.1 1.2 copy-start

commit v2 on v1

v2 whole, which is shorter than its diff:
```python
import functools

import jax
import jax.numpy as jnp
from jax import lax
from jax.experimental import pallas as pl
from jax.experimental.pallas import tpu as pltpu
from jax.sharding import PartitionSpec as P

DK = 128
DV = 128
CHUNK = 128
EPS = 1e-06
QUERY_SCALE = DK ** (-0.5)

f32 = jnp.float32
bf16 = jnp.bfloat16

NN = (((1,), (0,)), ((), ()))
NT = (((1,), (1,)), ((), ()))
TN = (((0,), (0,)), ((), ()))


def dot(a, b, dims=NN):
    return lax.dot_general(a, b, dims, preferred_element_type=f32)


def low(x):
    return x.astype(bf16)


def split(x):
    high = x.astype(bf16)
    return high, (x - high.astype(f32)).astype(bf16)


def twice(a, axis):
    return jnp.concatenate([a, a], axis=axis)


def wide(x, axis):
    return jnp.concatenate(split(x), axis=axis)


def dot3(a, b, dims=NN):
    (ca,), (cb,) = dims[0]
    ah, al = split(a)
    bh, bl = split(b)
    return dot(
        jnp.concatenate([ah, al, ah], axis=ca), jnp.concatenate([bh, bh, bl], axis=cb), dims
    )


def grids(shape=(CHUNK, CHUNK)):
    return lax.broadcasted_iota(jnp.int32, shape, 0), lax.broadcasted_iota(jnp.int32, shape, 1)


def pickers(pair):
    row, col = grids((128, 4 * 128))
    spread = jnp.where(row == 2 * pair + (col // 128) % 2 + 8 * (col // 256), 1.0, 0.0)
    row, col = grids((32, 128))
    lines = jnp.where(col == 2 * pair + (row // 8) % 2 + 8 * (row // 16), 1.0, 0.0)
    return low(spread), low(lines)


def sigmoid(x):
    return 1.0 / (1.0 + jnp.exp(-x))


def unit_scale(x):
    return lax.rsqrt(jnp.sum(x * x, axis=1, keepdims=True) + EPS)


def chunk_terms(picks, qs, ks, smalls):
    row, col = grids()
    causal = row >= col
    eye = row == col
    spread, lines = picks
    lower = low(jnp.where(causal, 1.0, 0.0))
    upper = low(jnp.where(row <= col, 1.0, 0.0))
    key_keys = [dot(k, k, NT) for k in ks]
    query_keys = [dot(q, k, NT) for q, k in zip(qs, ks)]
    picked = [dot(small, spread) for small in smalls]
    picked_rows = [dot(lines, small, NT) for small in smalls]
    growth_cols = [dot(lower, low(x[:, :256])) for x in picked]
    growth_rows = [dot(low(x[:16]), upper) for x in picked_rows]
    terms = []
    for c in range(len(qs)):
        qf = qs[c].astype(f32)
        kf = ks[c].astype(f32)
        rk_col = unit_scale(kf)
        rk_row = lax.rsqrt(jnp.sum(jnp.where(eye, key_keys[c], 0.0), axis=0, keepdims=True) + EPS)
        rq_col = unit_scale(qf) * QUERY_SCALE
        heads = []
        for i in range(2):
            g_col = growth_cols[c][:, i * 128 : (i + 1) * 128]
            g_row = growth_rows[c][8 * i : 8 * i + 1]
            g_end = g_col[CHUNK - 1 : CHUNK, :]
            heads.append(
                dict(
                    decay=jnp.where(causal, jnp.exp(jnp.minimum(g_col - g_row, 0.0)), 0.0),
                    beta_col=sigmoid(picked[c][:, 256 + i * 128 : 384 + i * 128]),
                    beta_row=sigmoid(picked_rows[c][16 + 8 * i : 17 + 8 * i]),
                    growth_col=jnp.exp(g_col),
                    growth_row=jnp.exp(g_row),
                    to_end=jnp.exp(g_end - g_col),
                    keep=jnp.exp(g_end),
                )
            )
        terms.append(
            dict(
                key_key=key_keys[c] * (rk_col * rk_row),
                query_key=query_keys[c] * (rq_col * rk_row),
                rk_col=rk_col,
                rk_row=rk_row,
                rq_col=rq_col,
                qf=qf,
                kf=kf,
                heads=heads,
            )
        )
    return terms


def inverses(systems):
    row, col = grids()
    ident = jnp.where(row == col, 1.0, 0.0)
    first = (row // 2 == col // 2) & (row > col)
    found = [ident - jnp.where(first, a, 0.0) for a in systems]
    size = 2
    while size < CHUNK:
        merge = (row // (2 * size) == col // (2 * size)) & (row // size > col // size)
        parts = [low(jnp.where(merge, a, 0.0)) for a in systems]
        lows = [low(t) for t in found]
        inner = [dot(part, t) for part, t in zip(parts, lows)]
        found = [t - dot(tl, low(x)) for t, tl, x in zip(found, lows, inner)]
        size *= 2
    rests = [ident - t - dot3(a, t) for a, t in zip(systems, found)]
    return [t + dot(low(t), low(x)) for t, x in zip(found, rests)]


def local_kernel(base, q_ref, k_ref, v_ref, o_ref, s_ref, send_ref, w_ref, f_ref, t_ref, u_ref, d_ref, a_ref, l_ref):
    pair = base + pl.program_id(0)
    row, col = grids()
    before = row > col
    chunks = q_ref.shape[0]
    qs, ks, smalls = ([ref[c] for c in range(chunks)] for ref in (q_ref, k_ref, s_ref))
    terms = chunk_terms(pickers(pair), qs, ks, smalls)
    cases = [(c, i) for c in range(chunks) for i in range(2)]
    gates = [terms[c]["heads"][i] for c, i in cases]
    o_in = [o_ref[c, :, i * DV : (i + 1) * DV] for c, i in cases]
    v_in = [v_ref[c, :, i * DV : (i + 1) * DV] for c, i in cases]
    systems = [
        jnp.where(before, h["beta_col"] * h["decay"] * terms[c]["key_key"], 0.0)
        for (c, i), h in zip(cases, gates)
    ]
    solved = inverses(systems)
    fresh = [
        dot(wide(h["decay"] * terms[c]["query_key"], 0), twice(o, 0), TN)
        for (c, i), h, o in zip(cases, gates, o_in)
    ]
    key_part = [
        dot(wide(t * (h["beta_row"] * h["growth_row"] * terms[c]["rk_row"]), 1), twice(ks[c], 0))
        for (c, i), h, t in zip(cases, gates, solved)
    ]
    value_part = [
        dot(wide(t * h["beta_row"], 1), twice(v, 0)) for h, t, v in zip(gates, solved, v_in)
    ]
    stepped = []
    for (c, i), h, x, y in zip(cases, gates, key_part, value_part):
        to_end = terms[c]["rk_col"] * h["to_end"]
        both = jnp.concatenate([-(to_end * x), to_end * y], axis=1)
        stepped.append(dot(wide(both, 0), twice(ks[c], 0), TN))
    devs = [x[:DK] for x in stepped]
    adds = [x[DK:] for x in stepped]
    backs = []
    for (c, i), h, u, w, o in zip(cases, gates, fresh, key_part, o_in):
        fh, fl = split(u)
        wh, wl = split(w)
        oh, ol = split(o.astype(f32) * (h["growth_col"] * terms[c]["rq_col"]))
        backs.append(
            dot(
                jnp.concatenate([oh, ol, -fh, -fl, -fh], axis=0),
                jnp.concatenate([qs[c], qs[c], wh, wh, wl], axis=0),
                TN,
            )
        )
    for n, (c, i) in enumerate(cases):
        w_ref[i, c] = key_part[n]
        f_ref[i, c] = value_part[n]
        t_ref[i, c] = low(solved[n])
        u_ref[i, c] = fresh[n]
        d_ref[i, c] = devs[n]
        a_ref[i, c] = adds[n]
        l_ref[i, c] = backs[n]
    at = lambda c, i: 2 * c + i
    stacks = [jnp.concatenate([devs[i], adds[i]], axis=0) for i in range(2)]
    keeps = [gates[i]["keep"] for i in range(2)]
    grads = [backs[at(chunks - 1, i)] for i in range(2)]
    for step in range(1, chunks):
        back = chunks - 1 - step
        ahead = [dot3(stacks[i], devs[at(step, i)]) for i in range(2)]
        behind = [dot3(grads[i], devs[at(back, i)], NT) for i in range(2)]
        for i in range(2):
            n, m = at(step, i), at(back, i)
            keep = gates[n]["keep"]
            stacks[i] = (
                keep * stacks[i]
                + ahead[i]
                + jnp.concatenate([keeps[i] * devs[n], adds[n]], axis=0)
            )
            keeps[i] = keeps[i] * keep
            grads[i] = gates[m]["keep"] * grads[i] + behind[i] + backs[m]
    for i in range(2):
        dev, add = stacks[i][:DK], stacks[i][DK:]
        high, rest = split(keeps[i])
        middle, last = split(keeps[i] - high.astype(f32))
        line = lax.broadcasted_iota(jnp.int32, (16, DK), 0)
        scale = jnp.where(line == 2, last.astype(f32), 0.0)
        scale = jnp.where(line == 1, middle.astype(f32), scale)
        scale = low(jnp.where(line == 0, high.astype(f32), scale))
        forward, backward = low(dev), low(dev.T)
        for part in range(4):
            half = slice((part % 2) * (DV // 2), (part % 2 + 1) * (DV // 2))
            send_ref[i, part, :DK] = forward if part < 2 else backward
            send_ref[i, part, DK : DK + DV // 2] = low((add if part < 2 else grads[i])[half])
            send_ref[i, part, DK + DV // 2 :] = scale


def chain_kernel(flip_ref, x_ref, out_ref, state_ref):
    count = x_ref.shape[0]

    @pl.when(pl.program_id(0) == 0)
    def _():
        state_ref[...] = jnp.zeros_like(state_ref)

    state = state_ref[...]
    flip = flip_ref[0]
    for step in range(count):
        at = jnp.where(flip == 1, count - 1 - step, step)
        out_ref[at] = low(state)
        block = x_ref[at]
        scale = jnp.sum(block[DK + DV // 2 :].astype(f32), axis=0, keepdims=True)
        state = (
            state * scale
            + dot(wide(state, 1), twice(block[:DK], 0))
            + block[DK : DK + DV // 2].astype(f32)
        )
    state_ref[...] = state


def final_kernel(base, q_ref, k_ref, v_ref, o_ref, s_ref, w_ref, f_ref, t_ref, u_ref, d_ref, a_ref, l_ref, h_ref, out_ref):
    here = pl.program_id(0)
    pair = base + here
    row, col = grids()
    before = row > col
    suffix = low(jnp.where(row <= col, 1.0, 0.0))
    chunks = q_ref.shape[0]
    qs, ks, smalls = ([ref[c] for c in range(chunks)] for ref in (q_ref, k_ref, s_ref))
    terms = chunk_terms(pickers(pair), qs, ks, smalls)
    cases = [(c, i) for c in range(chunks) for i in range(2)]
    gates = [terms[c]["heads"][i] for c, i in cases]
    o_in = [o_ref[c, :, i * DV : (i + 1) * DV] for c, i in cases]

    states = [[h_ref[i, 0].astype(f32)] for i in range(2)]
    grads = [[h_ref[i, 1].astype(f32)] for i in range(2)]
    for c in range(chunks):
        back = chunks - 1 - c
        ahead = [dot3(states[i][c], d_ref[i, c]) for i in range(2)]
        if back > 0:
            behind = [dot3(grads[i][c], d_ref[i, back], NT) for i in range(2)]
        for i in range(2):
            keep = terms[c]["heads"][i]["keep"]
            states[i].append(keep * states[i][c] + ahead[i] + a_ref[i, c])
            if back > 0:
                keep = terms[back]["heads"][i]["keep"]
                grads[i].append(keep * grads[i][c] + behind[i] + l_ref[i, back])
    state_of = [states[i][c] for c, i in cases]
    after_of = [states[i][c + 1] for c, i in cases]
    grad_of = [grads[i][chunks - 1 - c] for c, i in cases]

    fresh = [
        f_ref[i, c] - dot3(w_ref[i, c], state, NT) for (c, i), state in zip(cases, state_of)
    ]
    fresh_grad = [
        u_ref[i, c]
        + (terms[c]["rk_col"] * h["to_end"]) * dot(twice(ks[c], 1), wide(grad, 1), NT)
        for (c, i), h, grad in zip(cases, gates, grad_of)
    ]
    solved = [
        dot(twice(t_ref[i, c], 0), wide(x, 0), TN) for (c, i), x in zip(cases, fresh_grad)
    ]
    value_grad = [h["beta_col"] * x for h, x in zip(gates, solved)]
    quarter = (out_ref.shape[2] - 128) // 4
    for (c, i), x in zip(cases, value_grad):
        start = 2 * quarter + here * (2 * DV) + i * DV
        out_ref[c, :, pl.ds(pl.multiple_of(start, DV), DV)] = low(x)
    sides = [jnp.concatenate([low(x), o], axis=0) for x, o in zip(value_grad, o_in)]
    fresh_low = [low(x) for x in fresh]
    outer = [dot(x, low(state)) for x, state in zip(sides, state_of)]
    ended = [
        h["to_end"] * dot(x, low(grad)) for h, x, grad in zip(gates, fresh_low, grad_of)
    ]
    inner = [dot(x, y, NT) for x, y in zip(sides, fresh_low)]
    key_read = [-h["growth_col"] * x[:CHUNK] for h, x in zip(gates, outer)]
    query_read = [h["growth_col"] * x[CHUNK:] for h, x in zip(gates, outer)]
    erase = [jnp.where(before, h["decay"] * x[:CHUNK], 0.0) for h, x in zip(gates, inner)]
    read = [h["decay"] * x[CHUNK:] for h, x in zip(gates, inner)]
    units = [(t["qf"] * t["rq_col"], t["kf"] * t["rk_col"]) for t in terms]
    sums = []
    for n, (c, i) in enumerate(cases):
        query_unit, key_unit = units[c]
        spread = read[n] * terms[c]["query_key"] - erase[n] * terms[c]["key_key"]
        lone = query_unit * query_read[n] + key_unit * (key_read[n] - ended[n])
        sums.append(dot(twice(suffix, 1), wide(jnp.concatenate([spread, lone], axis=1), 0)))
    query_inner, key_inner = [], []
    for c in range(chunks):
        term = terms[c]
        read_sum = read[2 * c] + read[2 * c + 1]
        erase_sum = erase[2 * c] + erase[2 * c + 1]
        query_inner.append(dot(wide(read_sum * term["rk_row"], 1), twice(ks[c], 0)))
        key_inner.append(
            dot(wide(erase_sum * -term["rk_row"], 1), twice(ks[c], 0))
            + dot(
                jnp.concatenate(
                    split(read_sum * term["rq_col"]) + split(erase_sum * -term["rk_col"]), axis=0
                ),
                jnp.concatenate([qs[c], qs[c], ks[c], ks[c]], axis=0),
                TN,
            )
        )
    small_out = []
    for c in range(chunks):
        parts, places = [], []
        wholes = 0.0
        for i in range(2):
            n = 2 * c + i
            at = 2 * pair + i
            for place, part in (
                (at, jnp.where(before, sums[n][:, :CHUNK], 0.0) + sums[n][:, CHUNK:]),
                (at + 8, (1.0 - gates[n]["beta_col"]) * solved[n] * fresh[n]),
            ):
                parts += split(part)
                places += [low(jnp.where(col == place, 1.0, 0.0))] * 2
            product = jnp.sum(grad_of[n] * after_of[n], axis=0, keepdims=True)
            whole = jnp.sum(product, axis=1, keepdims=True)
            wholes = wholes + jnp.where(col[:1] == at, whole, 0.0)
        small_out.append(
            dot(jnp.concatenate(parts, axis=1), jnp.concatenate(places, axis=0)) + wholes
        )
    for c in range(chunks):
        term = terms[c]
        query_unit, key_unit = units[c]
        query_grad = query_inner[c] + query_read[2 * c] + query_read[2 * c + 1]
        key_grad = (
            key_inner[c]
            + (key_read[2 * c] + ended[2 * c])
            + (key_read[2 * c + 1] + ended[2 * c + 1])
        )
        query_back = term["rq_col"] * (
            query_grad
            - query_unit * (DK * jnp.sum(query_unit * query_grad, axis=1, keepdims=True))
        )
        key_back = term["rk_col"] * (
            key_grad - key_unit * jnp.sum(key_unit * key_grad, axis=1, keepdims=True)
        )
        out_ref[c, :, pl.ds(pl.multiple_of(here * DK, DK), DK)] = low(query_back)
        out_ref[c, :, pl.ds(pl.multiple_of(quarter + here * DK, DK), DK)] = low(key_back)
        place = slice(4 * quarter, 4 * quarter + 128)
        mine = (col // 2 == pair) | (col // 2 == pair + 4)
        held = out_ref[c, :, place]
        kept = jnp.where(here == 0, jnp.zeros_like(held), held)
        out_ref[c, :, place] = jnp.where(mine, low(small_out[c]), kept)


KEY_HEADS = 4
HEADS = 8
CHUNKS = 4
GROUPS = ((0, 2), (2, 4))
PAYLOAD = DK + DV // 2 + 16
VMEM = 58 << 20


def pack_kernel(*refs):
    out_ref = refs[-1]
    at = 0
    for ref in refs[:4]:
        width = ref.shape[1]
        out_ref[0, :, at : at + width] = ref[...]
        at += width
    if len(refs) > 5:
        d_ref, b_ref = refs[4:6]
        dest = pl.program_id(0)
        row, col = grids((d_ref.shape[0], 128))
        decays = (col < HEADS) & (row == HEADS * dest + col)
        betas = (col >= HEADS) & (col < 2 * HEADS) & (row == HEADS * dest + col - HEADS)
        picks = [low(jnp.where(here, 1.0, 0.0)) for here in (decays, betas)]
        out_ref[0, :, at : at + 128] = low(
            dot(d_ref[...], picks[0], TN) + dot(b_ref[...], picks[1], TN)
        )


def pack(arrays, gates, begin, end):
    count = end - begin
    per = KEY_HEADS // count
    first = begin // count
    widths = [count * size for size in (DK, DK, 2 * DV, 2 * DV)]
    total = sum(widths) + (128 if gates else 0)
    return pl.pallas_call(
        pack_kernel,
        grid=(CHUNKS,),
        in_specs=[pl.BlockSpec((CHUNK, width), lambda j: (0, per * j + first)) for width in widths]
        + [pl.BlockSpec(gate.shape, lambda j: (0, 0)) for gate in gates],
        out_specs=pl.BlockSpec((1, CHUNK, total), lambda j: (j, 0, 0)),
        out_shape=jax.ShapeDtypeStruct((CHUNKS, CHUNK, total), bf16),
        compiler_params=pltpu.CompilerParams(vmem_limit_bytes=VMEM),
        name="pack",
    )(*arrays, *gates)


def unpack_kernel(*refs):
    groups = refs[: len(GROUPS)]
    q_ref, k_ref, v_ref, d_ref, b_ref, d_sum, b_sum = refs[len(GROUPS) :]
    source = pl.program_id(0)

    @pl.when(source == 0)
    def _():
        d_sum[...] = jnp.zeros_like(d_sum)
        b_sum[...] = jnp.zeros_like(b_sum)

    row, col = grids((d_sum.shape[0], 128))
    decays = low(jnp.where((col < HEADS) & (row == HEADS * source + col), 1.0, 0.0))
    betas = (col >= HEADS) & (col < 2 * HEADS) & (row == HEADS * source + col - HEADS)
    betas = low(jnp.where(betas, 1.0, 0.0))
    for (begin, end), ref in zip(GROUPS, groups):
        at = 0
        for out, size in ((q_ref, DK), (k_ref, DK), (v_ref, 2 * DV)):
            width = (end - begin) * size
            out[:, begin * size : end * size] = ref[0, :, at : at + width]
            at += width
        small = ref[0, :, at : at + 128]
        d_sum[...] += dot(decays, small, NT)
        b_sum[...] += dot(betas, small, NT)

    @pl.when(source == pl.num_programs(0) - 1)
    def _():
        d_ref[...] = low(d_sum[...])
        b_ref[...] = low(b_sum[...])


def unpack(groups):
    heads = CHUNKS * HEADS
    sizes = [KEY_HEADS * DK, KEY_HEADS * DK, HEADS * DV]
    q, k, v, d, b = pl.pallas_call(
        unpack_kernel,
        grid=(CHUNKS,),
        in_specs=[pl.BlockSpec((1,) + x.shape[1:], lambda j: (j, 0, 0)) for x in groups],
        out_specs=[pl.BlockSpec((CHUNK, size), lambda j: (0, j)) for size in sizes]
        + [pl.BlockSpec((heads, CHUNK), lambda j: (0, 0))] * 2,
        out_shape=[jax.ShapeDtypeStruct((CHUNK, CHUNKS * size), bf16) for size in sizes]
        + [jax.ShapeDtypeStruct((heads, CHUNK), bf16)] * 2,
        scratch_shapes=[pltpu.VMEM((heads, CHUNK), f32)] * 2,
        compiler_params=pltpu.CompilerParams(vmem_limit_bytes=VMEM),
        name="unpack",
    )(*groups)
    return q, k, v, d.T, b.T


def packed_specs(count, small_at):
    return [
        pl.BlockSpec((CHUNKS, CHUNK, DK), lambda p: (0, 0, p)),
        pl.BlockSpec((CHUNKS, CHUNK, DK), lambda p: (0, 0, count + p)),
        pl.BlockSpec((CHUNKS, CHUNK, 2 * DV), lambda p: (0, 0, count + p)),
        pl.BlockSpec((CHUNKS, CHUNK, 2 * DV), lambda p: (0, 0, 2 * count + p)),
        pl.BlockSpec((CHUNKS, CHUNK, 128), lambda p: (0, 0, small_at)),
    ]


SAVED = (f32, f32, bf16, f32, f32, f32, f32)


def saved_specs():
    return [pl.BlockSpec((2, CHUNKS, CHUNK, CHUNK), lambda p: (p, 0, 0, 0)) for _ in SAVED]


def local_pass(packed, small, small_at, begin, end, sends=None):
    count = end - begin
    kernel = functools.partial(local_kernel, begin)
    aliased = [] if sends is None else [sends]
    if aliased:
        inner = kernel
        kernel = lambda *refs: inner(*refs[:5], *refs[6:])
    return pl.pallas_call(
        kernel,
        grid=(count,),
        in_specs=packed_specs(count, small_at) + [pl.BlockSpec(memory_space=pl.ANY)] * len(aliased),
        out_specs=[pl.BlockSpec((2, 4, PAYLOAD, DK), lambda p: (begin + p, 0, 0, 0))]
        + saved_specs(),
        out_shape=[jax.ShapeDtypeStruct((HEADS, 4, PAYLOAD, DK), bf16)]
        + [jax.ShapeDtypeStruct((2 * count, CHUNKS, CHUNK, CHUNK), kind) for kind in SAVED],
        input_output_aliases={5: 0} if aliased else {},
        compiler_params=pltpu.CompilerParams(vmem_limit_bytes=VMEM),
        cost_estimate=pl.CostEstimate(
            flops=count * 4_000_000_000, bytes_accessed=count * 5_000_000, transcendentals=0
        ),
        name="local_pass",
    )(*([packed] * 4), small, *aliased)


def chain_pass(flip, received):
    count = received.shape[0]
    steps = 4
    size = count // steps
    place = lambda g, flip: (jnp.where(flip[0] == 1, steps - 1 - g, g), 0, 0)
    return pl.pallas_call(
        chain_kernel,
        grid_spec=pltpu.PrefetchScalarGridSpec(
            num_scalar_prefetch=1,
            grid=(steps,),
            in_specs=[pl.BlockSpec((size, PAYLOAD, DK), place)],
            out_specs=pl.BlockSpec((size, DV // 2, DK), place),
            scratch_shapes=[pltpu.VMEM((DV // 2, DK), f32)],
        ),
        out_shape=jax.ShapeDtypeStruct((count, DV // 2, DK), bf16),
        compiler_params=pltpu.CompilerParams(vmem_limit_bytes=VMEM),
        name="chain_pass",
    )(flip, received)


def final_pass(packed, small, small_at, saved, states, begin, end):
    count = end - begin
    width = count * 2 * (DK + DV) + 128
    return pl.pallas_call(
        functools.partial(final_kernel, begin),
        grid=(count,),
        in_specs=packed_specs(count, small_at)
        + saved_specs()
        + [pl.BlockSpec((2, 2, DV, DK), lambda p: (begin + p, 0, 0, 0))],
        out_specs=pl.BlockSpec((CHUNKS, CHUNK, width), lambda p: (0, 0, 0)),
        out_shape=jax.ShapeDtypeStruct((CHUNKS, CHUNK, width), bf16),
        compiler_params=pltpu.CompilerParams(vmem_limit_bytes=VMEM),
        cost_estimate=pl.CostEstimate(
            flops=count * 4_000_000_000, bytes_accessed=count * 5_000_000, transcendentals=0
        ),
        name="final_pass",
    )(*([packed] * 4), small, *saved, states)


def exchange(packed):
    return lax.all_to_all(packed, "head", split_axis=0, concat_axis=0, tiled=True)


def on_device(query_rows, key_rows, value_rows, log_decay, beta_logit, out_grad):
    arrays = [query_rows, key_rows, value_rows, out_grad]
    gates = [log_decay.T, beta_logit.T]
    received = [exchange(pack(arrays, gates if b == 0 else [], b, e)) for b, e in GROUPS]
    small = received[0]
    small_at = small.shape[2] // 128 - 1
    sends, saved = None, []
    for (b, e), packed in zip(GROUPS, received):
        sends, *kept = local_pass(packed, small, small_at, b, e, sends)
        saved.append(kept)
    segments = lax.axis_size("ctx")
    maps = lax.all_to_all(
        sends.reshape(segments, PAYLOAD, DK),
        "ctx",
        split_axis=0,
        concat_axis=0,
        tiled=True,
    )
    flip = (lax.axis_index("ctx") % 4 >= 2).astype(jnp.int32).reshape(1)
    states = lax.all_to_all(
        chain_pass(flip, maps), "ctx", split_axis=0, concat_axis=0, tiled=True
    ).reshape(HEADS, 2, DV, DK)
    outs = []
    for (b, e), packed, kept in zip(GROUPS, received, saved):
        outs.append(exchange(final_pass(packed, small, small_at, kept, states, b, e)))
    return unpack(outs)


def solution(mesh):
    spec = P(("ctx", "head"), None)
    return jax.shard_map(
        on_device, mesh=mesh, in_specs=(spec,) * 6, out_specs=(spec,) * 5, check_vma=False
    )
```

time: 215 us -> 181 us (0.84)
  blocking collectives: 92.6 us -> 37.1 us
  waiting for transfers between devices: 23.1 us -> 55.3 us
  local copies, waits for them, and re-layouts: 22.4 us -> 2.35 us
  starting transfers between devices: 7.38 us -> 19.8 us
  Pallas kernels: 65.9 us -> 63.3 us
    all_to_all x3 -> x2, blocking collectives: 92.6 us -> 37.1 us  [the longest x1 20.7 us: exchange(): lax.all_to_all(packed, 'head', split_axis=0, concat_axis=0, tiled=True)]
    all_to_all x0 -> x3, waiting for transfers between devices: none -> 32.2 us  [exchange(): lax.all_to_all(packed, 'head', split_axis=0, concat_axis=0, tiled=True)]
    all_to_all x0 -> x3, starting transfers between devices: none -> 12.4 us  [exchange(): lax.all_to_all(packed, 'head', split_axis=0, concat_axis=0, tiled=True)]
    reshape x6 -> x0, local copies, waits for them, and re-layouts: 6.43 us -> none  [pack(): split_up = [a.reshape(a.shape[0], CHUNKS, -1) for a in arrays]]
    unnamed x15 -> x8, local copies, waits for them, and re-layouts: 7.54 us -> 2.35 us
    concatenate x1 -> x0, local copies, waits for them, and re-layouts: 4.82 us -> none  [pack(): return jnp.concatenate(split_up, axis=2).transpose(1, 0, 2)]
    slice x8 -> x0, local copies, waits for them, and re-layouts: 2.89 us -> none  [unpack(): outs.append(tokens_first[:, :, at:at + width].reshape(CHUNK, -1))]
    pallas_call x3 -> x8, Pallas kernels: 65.9 us -> 63.3 us  [the longest x2 23.8 us: local_pass(): pl.pallas_call(kernel, grid=(count,), in_specs=packed_specs(count, small_...]
  transfers between devices with their start and end apart: 1 -> 4, of which waited for: 1 -> 4; matrix products, arithmetic and copies ran while one was open for 0% -> 0% of each run, Pallas kernels for 0% -> 15%
where the time goes in v2:
time: 181 us; the launch traced here: 179 us
  Pallas kernels  63.3 us (35%)
  waiting for transfers between devices  55.3 us (31%)
  blocking collectives  37.1 us (20%)
  starting transfers between devices  19.8 us (11%)
  local copies, waits for them, and re-layouts  2.35 us (1%)
    all_to_all x3, waiting for transfers between devices, exchange(): lax.all_to_all(packed, 'head', split_axis=0, concat_axis=0, tiled=True)  32.2 us
    pallas_call x2, Pallas kernels, local_pass(): pl.pallas_call(kernel, grid=(count,), in_specs=packed_specs(count, small_...  23.8 us
    all_to_all x1, waiting for transfers between devices, on_device(): lax.all_to_all(sends.reshape(segments, PAYLOAD, DK), 'ctx', split_axis=0,...  23.1 us
    pallas_call x2, Pallas kernels, final_pass(): pl.pallas_call(functools.partial(final_kernel, begin), grid=(count,), in_...  21.9 us
    all_to_all x1, blocking collectives, exchange(): lax.all_to_all(packed, 'head', split_axis=0, concat_axis=0, tiled=True)  20.7 us
    all_to_all x1, blocking collectives, on_device(): lax.all_to_all(chain_pass(flip, maps), 'ctx', split_axis=0, concat_axis=0...  16.3 us
    all_to_all x3, starting transfers between devices, exchange(): lax.all_to_all(packed, 'head', split_axis=0, concat_axis=0, tiled=True)  12.4 us
    pallas_call x2, Pallas kernels, pack(): pl.pallas_call(pack_kernel, grid=(CHUNKS,), in_specs=[pl.BlockSpec((CHUNK...  7.73 us
  transfers between devices with their start and end apart: 4, of which 4 were waited for; matrix products, arithmetic and copies ran while one was open for 0% of the time, Pallas kernels for 15%

profile of v2, /device:TPU:24, one launch (start us, length us, event | category | flops | bytes accessed | tf_op | source)
XLA Modules:
  0.0 178.6 jit_solution(7158636444007287631)
XLA Ops:
  0.6 4.0 %pack.2 = bf16[4,128,1664]{2,1,0:T(8,128)(2,1)} custom-call(bf16[128,2048]{1,0:T(8,128)(2,1)} %refs_0_.3, bf16[128,2048]{1,0:T(8,128)(2,1)} %refs_1_.3, bf16[128,4096]{1,0:T(8,128)(2,1)} %refs_2_.3, bf16[128,4096]{1,0:T(8,128)(2,1)} %refs_3_.3, bf16[32,128]{1,0:T(8,128)(2,1)} %bitcast.10, bf16[32,128]{1,0:T(8,128)(2,1)} %bitcast.11), custom_call_target="tpu_custom_call" | custom-call | tf_op jit(solution)/shard_map/pack/pallas_call | solution.py:409
  4.7 5.3 %all-to-all-start = ((bf16[4,128,1664]{2,1,0:T(8,128)(2,1)}), bf16[4,128,1664]{2,1,0:T(8,128)(2,1)S(1)}, u32[]{:S(2)}, u32[]{:S(2)}) async-start(bf16[4,128,1664]{2,1,0:T(8,128)(2,1)} %pack.2), calls=%async_computation | async-start | bytes 3407872 | tf_op jit(solution)/shard_map/all_to_all | solution.py:550
  10.0 3.7 %pack.3 = bf16[4,128,1536]{2,1,0:T(8,128)(2,1)} custom-call(bf16[128,2048]{1,0:T(8,128)(2,1)} %refs_0_.3, bf16[128,2048]{1,0:T(8,128)(2,1)} %refs_1_.3, bf16[128,4096]{1,0:T(8,128)(2,1)} %refs_2_.3, bf16[128,4096]{1,0:T(8,128)(2,1)} %refs_3_.3), custom_call_target="tpu_custom_call" | custom-call | tf_op jit(solution)/shard_map/pack/pallas_call | solution.py:409
  13.7 18.4 %all-to-all-done.q_ref.k_ref.v_ref.o_ref.s_ref.refs_4_ = bf16[4,128,1664]{2,1,0:T(8,128)(2,1)S(1)} async-done(((bf16[4,128,1664]{2,1,0:T(8,128)(2,1)}), bf16[4,128,1664]{2,1,0:T(8,128)(2,1)S(1)}, u32[]{:S(2)}, u32[]{:S(2)}) %all-to-all-start) | async-done | bytes 1703968 | tf_op jit(solution)/shard_map/all_to_all | solution.py:550
  32.1 0.0 copy-start.2
  32.1 3.6 %all-to-all-start.1 = ((bf16[4,128,1536]{2,1,0:T(8,128)(2,1)}), bf16[4,128,1536]{2,1,0:T(8,128)(2,1)S(1)}, u32[]{:S(2)}, u32[]{:S(2)}) async-start(bf16[4,128,1536]{2,1,0:T(8,128)(2,1)} %pack.3), calls=%async_computation.1 | async-start | bytes 3145728 | tf_op jit(solution)/shard_map/all_to_all | solution.py:550
  35.7 0.0 copy-done.2
  35.7 11.9 %local_pass.2 = (bf16[8,4,208,128]{3,2,1,0:T(8,128)(2,1)}, f32[4,4,128,128]{3,2,1,0:T(8,128)}, f32[4,4,128,128]{3,2,1,0:T(8,128)}, bf16[4,4,128,128]{3,2,1,0:T(8...) custom-call(bf16[4,128,1664]{2,1,0:T(8,128)(2,1)} %copy-done.2, ...), custom_call_target="tpu_custom_call" | custom-call | flops 8000000000 | bytes 10000000 | tf_op jit(solution)/shard_map/local_pass/pallas_call | solution.py:493
  47.6 7.8 %all-to-all-done.1.refs_0_.refs_1_.refs_2_.refs_3_.q_ref.k_ref.v_ref.o_ref = bf16[4,128,1536]{2,1,0:T(8,128)(2,1)S(1)} async-done(((bf16[4,128,1536]{2,1,0:T(8,128)(2,1)}), bf16[4,128,1536]{2,1,0:T(8,128)(2,1)S(1)}, u32[]{:S(2)}, u32[]{:S(2)}) %all-to-all-start.1) | async-done | bytes 1572896 | tf_op jit(solution)/shard_map/all_to_all | solution.py:550
  55.4 0.0 copy-start.3
  55.4 1.2 copy-done.3
  56.6 11.9 %local_pass.3 = (bf16[8,4,208,128]{3,2,1,0:T(8,128)(2,1)}, f32[4,4,128,128]{3,2,1,0:T(8,128)}, f32[4,4,128,128]{3,2,1,0:T(8,128)}, bf16[4,4,128,128]{3,2,1,0:T(8...) custom-call(bf16[4,128,1536]{2,1,0:T(8,128)(2,1)} %copy-done.3, ...), custom_call_target="tpu_custom_call", output_to_operand_aliasing={{0}: (5, {})} | custom-call | flops 8000000000 | bytes 10000000 | tf_op jit(solution)/shard_map/local_pass/pallas_call | solution.py:493
  68.5 7.4 %all-to-all-start.2 = ((bf16[32,208,128]{2,1,0:T(8,128)(2,1)}), bf16[32,208,128]{2,1,0:T(8,128)(2,1)S(1)}, u32[]{:S(2)}, u32[]{:S(2)}) async-start(bf16[32,208,128]{2,1,0:T(8,128)(2,1)} %bitcast.7), calls=%async_computation.2 | async-start | bytes 3407872 | tf_op jit(solution)/shard_map/all_to_all | solution.py:564
  75.9 23.1 %all-to-all-done.2.x_ref = bf16[32,208,128]{2,1,0:T(8,128)(2,1)S(1)} async-done(((bf16[32,208,128]{2,1,0:T(8,128)(2,1)}), bf16[32,208,128]{2,1,0:T(8,128)(2,1)S(1)}, u32[]{:S(2)}, u32[]{:S(2)}) %all-to-all-start.2) | async-done | bytes 1703968 | tf_op jit(solution)/shard_map/all_to_all | solution.py:564
  99.0 0.0 copy-start
  99.0 1.2 copy-done
  100.2 5.7 %chain_pass.1 = bf16[32,64,128]{2,1,0:T(8,128)(2,1)} custom-call(s32[1]{0:T(128)} %bitcast.2.flip_ref, bf16[32,208,128]{2,1,0:T(8,128)(2,1)} %copy-done), custom_call_target="tpu_custom_call" | custom-call | tf_op jit(solution)/shard_map/chain_pass/pallas_call | solution.py:515
  105.9 16.3 %all_to_all.30 = bf16[32,64,128]{2,1,0:T(8,128)(2,1)} all-to-all(bf16[32,64,128]{2,1,0:T(8,128)(2,1)} %chain_pass.1), channel_id=1, replica_groups=mesh['ctx'=32,'head'=4] {'ctx'}, dimensions={0} | all-to-all | bytes 1048576 | tf_op jit(solution)/shard_map/all_to_all | solution.py:572
  122.2 10.7 %final_pass.2 = bf16[4,128,1152]{2,1,0:T(8,128)(2,1)} custom-call(bf16[4,128,1664]{2,1,0:T(8,128)(2,1)} %copy-done.2, bf16[4,128,1664]{2,1,0:T(8,128)(2,1)} %copy-done.2, bf16[4,128,1664]{2,1,0:T(8,128)(2,1)} %copy-done.2, bf16[4,128,1664]{2,1,0:T(8,128)(2,1)} %copy-done.2, bf16[4,128,1664]{2,1,0:T(8,128)(2,1)} %copy-done.2, ...), custom_call_target="tpu_custom_call" | custom-call | flops 8000000000 | bytes 10000000 | tf_op jit(solution)/shard_map/final_pass/pallas_call | solution.py:533
  132.9 3.5 %all-to-all-start.4 = ((bf16[4,128,1152]{2,1,0:T(8,128)(2,1)}), bf16[4,128,1152]{2,1,0:T(8,128)(2,1)S(1)}, u32[]{:S(2)}, u32[]{:S(2)}) async-start(bf16[4,128,1152]{2,1,0:T(8,128)(2,1)} %final_pass.2), calls=%async_computation.4 | async-start | bytes 2359296 | tf_op jit(solution)/shard_map/all_to_all | solution.py:550
  136.4 11.3 %final_pass.3 = bf16[4,128,1152]{2,1,0:T(8,128)(2,1)} custom-call(bf16[4,128,1536]{2,1,0:T(8,128)(2,1)} %copy-done.3, bf16[4,128,1536]{2,1,0:T(8,128)(2,1)} %copy-done.3, bf16[4,128,1536]{2,1,0:T(8,128)(2,1)} %copy-done.3, bf16[4,128,1536]{2,1,0:T(8,128)(2,1)} %copy-done.3, bf16[4,128,1664]{2,1,0:T(8,128)(2,1)} %copy-done.2, ...), custom_call_target="tpu_custom_call" | custom-call | flops 8000000000 | bytes 10000000 | tf_op jit(solution)/shard_map/final_pass/pallas_call | solution.py:533
  147.7 5.9 %all-to-all-done.4.refs_0_ = bf16[4,128,1152]{2,1,0:T(8,128)(2,1)S(1)} async-done(((bf16[4,128,1152]{2,1,0:T(8,128)(2,1)}), bf16[4,128,1152]{2,1,0:T(8,128)(2,1)S(1)}, u32[]{:S(2)}, u32[]{:S(2)}) %all-to-all-start.4) | async-done | bytes 1179680 | tf_op jit(solution)/shard_map/all_to_all | solution.py:550
  153.6 0.0 copy-start.1
  153.6 20.7 %all_to_all.31.refs_1_ = bf16[4,128,1152]{2,1,0:T(8,128)(2,1)} all-to-all(bf16[4,128,1152]{2,1,0:T(8,128)(2,1)} %final_pass.3), channel_id=1, replica_groups=mesh['ctx'=32,'head'=4] {'head'}, dimensions={0} | all-to-all | bytes 2359296 | tf_op jit(solution)/shard_map/all_to_all | solution.py:550
  174.3 0.0 copy-done.1
  174.3 4.1 %unpack.1 = (bf16[128,2048]{1,0:T(8,128)(2,1)}, bf16[128,2048]{1,0:T(8,128)(2,1)}, bf16[128,4096]{1,0:T(8,128)(2,1)}, bf16[32,128]{1,0:T(8,128)(2,1)}, bf16[32,128]{1,0:T(8,128)(2,1)}) custom-call(bf16[4,128,1152]{2,1,0:T(8,128)(2,1)} %copy-done.1, bf16[4,128,1152]{2,1,0:T(8,128)(2,1)} %all_to_all.31.refs_1_), custom_call_target="tpu_custom_call" | custom-call | tf_op jit(solution)/shard_map/unpack/pallas_call | solution.py:454
Async XLA Ops:
  4.7 27.4 %all-to-all-start = ((bf16[4,128,1664]{2,1,0:T(8,128)(2,1)}), bf16[4,128,1664]{2,1,0:T(8,128)(2,1)S(1)}, u32[]{:S(2)}, u32[]{:S(2)}) async-start(bf16[4,128,1664]{2,1,0:T(8,128)(2,1)} %pack.2), calls=%async_computation | async-start | bytes 3407872 | tf_op jit(solution)/shard_map/all_to_all | solution.py:550
  32.1 3.6 %copy-start.2 = (bf16[4,128,1664]{2,1,0:T(8,128)(2,1)}, bf16[4,128,1664]{2,1,0:T(8,128)(2,1)S(1)}, u32[]{:S(2)}) copy-start(bf16[4,128,1664]{2,1,0:T(8,128)(2,1)S(1)} %all-to-all-done.q_ref.k_ref.v_ref.o_ref.s_ref.refs_4_) | copy-start | bytes 5111812
  32.1 23.3 %all-to-all-start.1 = ((bf16[4,128,1536]{2,1,0:T(8,128)(2,1)}), bf16[4,128,1536]{2,1,0:T(8,128)(2,1)S(1)}, u32[]{:S(2)}, u32[]{:S(2)}) async-start(bf16[4,128,1536]{2,1,0:T(8,128)(2,1)} %pack.3), calls=%async_computation.1 | async-start | bytes 3145728 | tf_op jit(solution)/shard_map/all_to_all | solution.py:550
  55.4 1.2 copy-start.3
  68.5 30.5 %all-to-all-start.2 = ((bf16[32,208,128]{2,1,0:T(8,128)(2,1)}), bf16[32,208,128]{2,1,0:T(8,128)(2,1)S(1)}, u32[]{:S(2)}, u32[]{:S(2)}) async-start(bf16[32,208,128]{2,1,0:T(8,128)(2,1)} %bitcast.7), calls=%async_computation.2 | async-start | bytes 3407872 | tf_op jit(solution)/shard_map/all_to_all | solution.py:564
  99.0 1.2 copy-start
  132.9 20.7 %all-to-all-start.4 = ((bf16[4,128,1152]{2,1,0:T(8,128)(2,1)}), bf16[4,128,1152]{2,1,0:T(8,128)(2,1)S(1)}, u32[]{:S(2)}, u32[]{:S(2)}) async-start(bf16[4,128,1152]{2,1,0:T(8,128)(2,1)} %final_pass.2), calls=%async_computation.4 | async-start | bytes 2359296 | tf_op jit(solution)/shard_map/all_to_all | solution.py:550
  153.6 20.7 %copy-start.1 = (bf16[4,128,1152]{2,1,0:T(8,128)(2,1)}, bf16[4,128,1152]{2,1,0:T(8,128)(2,1)S(1)}, u32[]{:S(2)}) copy-start(bf16[4,128,1152]{2,1,0:T(8,128)(2,1)S(1)} %all-to-all-done.4.refs_0_) | copy-start | bytes 3538948

commit v3 on v2

v3 whole, which is shorter than its diff:
```python
import functools

import jax
import jax.numpy as jnp
from jax import lax
from jax.experimental import pallas as pl
from jax.experimental.pallas import tpu as pltpu
from jax.sharding import PartitionSpec as P

DK = 128
DV = 128
CHUNK = 128
EPS = 1e-06
QUERY_SCALE = DK ** (-0.5)

KEY_HEADS = 4
HEADS = 8
CHUNKS = 4
GROUPS = ((0, 2), (2, 4))
PAYLOAD = DK + DV + 16
VMEM = 58 << 20

f32 = jnp.float32
bf16 = jnp.bfloat16

NN = (((1,), (0,)), ((), ()))
NT = (((1,), (1,)), ((), ()))
TN = (((0,), (0,)), ((), ()))


def dot(a, b, dims=NN):
    return lax.dot_general(a, b, dims, preferred_element_type=f32)


def low(x):
    return x.astype(bf16)


def split(x):
    high = x.astype(bf16)
    return high, (x - high.astype(f32)).astype(bf16)


def twice(a, axis):
    return jnp.concatenate([a, a], axis=axis)


def wide(x, axis):
    return jnp.concatenate(split(x), axis=axis)


def dot3(a, b, dims=NN):
    (ca,), (cb,) = dims[0]
    ah, al = split(a)
    bh, bl = split(b)
    return dot(
        jnp.concatenate([ah, al, ah], axis=ca), jnp.concatenate([bh, bh, bl], axis=cb), dims
    )


def grids(shape=(CHUNK, CHUNK)):
    return lax.broadcasted_iota(jnp.int32, shape, 0), lax.broadcasted_iota(jnp.int32, shape, 1)


def pickers(pair):
    row, col = grids((128, 4 * 128))
    spread = jnp.where(row == 2 * pair + (col // 128) % 2 + 8 * (col // 256), 1.0, 0.0)
    row, col = grids((32, 128))
    lines = jnp.where(col == 2 * pair + (row // 8) % 2 + 8 * (row // 16), 1.0, 0.0)
    return low(spread), low(lines)


def sigmoid(x):
    return 1.0 / (1.0 + jnp.exp(-x))


def unit_scale(x):
    return lax.rsqrt(jnp.sum(x * x, axis=1, keepdims=True) + EPS)


def chunk_terms(picks, qs, ks, smalls):
    row, col = grids()
    causal = row >= col
    eye = row == col
    spread, lines = picks
    lower = low(jnp.where(causal, 1.0, 0.0))
    upper = low(jnp.where(row <= col, 1.0, 0.0))
    key_keys = [dot(k, k, NT) for k in ks]
    query_keys = [dot(q, k, NT) for q, k in zip(qs, ks)]
    picked = [dot(small, spread) for small in smalls]
    picked_rows = [dot(lines, small, NT) for small in smalls]
    growth_cols = [dot(lower, low(x[:, :256])) for x in picked]
    growth_rows = [dot(low(x[:16]), upper) for x in picked_rows]
    terms = []
    for c in range(len(qs)):
        qf = qs[c].astype(f32)
        kf = ks[c].astype(f32)
        rk_col = unit_scale(kf)
        rk_row = lax.rsqrt(jnp.sum(jnp.where(eye, key_keys[c], 0.0), axis=0, keepdims=True) + EPS)
        rq_col = unit_scale(qf) * QUERY_SCALE
        heads = []
        for i in range(2):
            g_col = growth_cols[c][:, i * 128 : (i + 1) * 128]
            g_row = growth_rows[c][8 * i : 8 * i + 1]
            g_end = g_col[CHUNK - 1 : CHUNK, :]
            heads.append(
                dict(
                    decay=jnp.where(causal, jnp.exp(jnp.minimum(g_col - g_row, 0.0)), 0.0),
                    beta_col=sigmoid(picked[c][:, 256 + i * 128 : 384 + i * 128]),
                    beta_row=sigmoid(picked_rows[c][16 + 8 * i : 17 + 8 * i]),
                    growth_col=jnp.exp(g_col),
                    growth_row=jnp.exp(g_row),
                    to_end=jnp.exp(g_end - g_col),
                    keep=jnp.exp(g_end),
                )
            )
        terms.append(
            dict(
                key_key=key_keys[c] * (rk_col * rk_row),
                query_key=query_keys[c] * (rq_col * rk_row),
                rk_col=rk_col,
                rk_row=rk_row,
                rq_col=rq_col,
                qf=qf,
                kf=kf,
                heads=heads,
            )
        )
    return terms


def inverses(systems):
    row, col = grids()
    ident = jnp.where(row == col, 1.0, 0.0)
    first = (row // 2 == col // 2) & (row > col)
    found = [ident - jnp.where(first, a, 0.0) for a in systems]
    size = 2
    while size < CHUNK:
        merge = (row // (2 * size) == col // (2 * size)) & (row // size > col // size)
        parts = [low(jnp.where(merge, a, 0.0)) for a in systems]
        lows = [low(t) for t in found]
        inner = [dot(part, t) for part, t in zip(parts, lows)]
        found = [t - dot(tl, low(x)) for t, tl, x in zip(found, lows, inner)]
        size *= 2
    rests = [ident - t - dot3(a, t) for a, t in zip(systems, found)]
    return [t + dot(low(t), low(x)) for t, x in zip(found, rests)]


def slot_of(me, chunk):
    return lax.rem(me + CHUNKS - chunk, CHUNKS)


def local_kernel(base, me_ref, *refs):
    ins, outs = refs[: 5 * CHUNKS], refs[5 * CHUNKS :]
    send_ref, w_ref, f_ref, t_ref, u_ref, d_ref, a_ref, l_ref, keep_ref = outs
    me = me_ref[0]
    pair = base + pl.program_id(0)
    row, col = grids()
    before = row > col
    chunks = CHUNKS
    qs, ks, vs, os, smalls = ([r[...] for r in ins[n * chunks : (n + 1) * chunks]] for n in range(5))
    terms = chunk_terms(pickers(pair), qs, ks, smalls)
    cases = [(c, i) for c in range(chunks) for i in range(2)]
    gates = [terms[c]["heads"][i] for c, i in cases]
    o_in = [os[c][:, i * DV : (i + 1) * DV] for c, i in cases]
    v_in = [vs[c][:, i * DV : (i + 1) * DV] for c, i in cases]
    systems = [
        jnp.where(before, h["beta_col"] * h["decay"] * terms[c]["key_key"], 0.0)
        for (c, i), h in zip(cases, gates)
    ]
    solved = inverses(systems)
    fresh = [
        dot(wide(h["decay"] * terms[c]["query_key"], 0), twice(o, 0), TN)
        for (c, i), h, o in zip(cases, gates, o_in)
    ]
    key_part = [
        dot(wide(t * (h["beta_row"] * h["growth_row"] * terms[c]["rk_row"]), 1), twice(ks[c], 0))
        for (c, i), h, t in zip(cases, gates, solved)
    ]
    value_part = [
        dot(wide(t * h["beta_row"], 1), twice(v, 0)) for h, t, v in zip(gates, solved, v_in)
    ]
    stepped = []
    for (c, i), h, x, y in zip(cases, gates, key_part, value_part):
        to_end = terms[c]["rk_col"] * h["to_end"]
        both = jnp.concatenate([-(to_end * x), to_end * y], axis=1)
        stepped.append(dot(wide(both, 0), twice(ks[c], 0), TN))
    devs = [x[:DK] for x in stepped]
    adds = [x[DK:] for x in stepped]
    backs = []
    for (c, i), h, u, w, o in zip(cases, gates, fresh, key_part, o_in):
        fh, fl = split(u)
        wh, wl = split(w)
        oh, ol = split(o.astype(f32) * (h["growth_col"] * terms[c]["rq_col"]))
        backs.append(
            dot(
                jnp.concatenate([oh, ol, -fh, -fl, -fh], axis=0),
                jnp.concatenate([qs[c], qs[c], wh, wh, wl], axis=0),
                TN,
            )
        )
    for n, (c, i) in enumerate(cases):
        w_ref[i, c] = key_part[n]
        f_ref[i, c] = value_part[n]
        t_ref[i, c] = low(solved[n])
        u_ref[i, c] = fresh[n]
        d_ref[i, c] = devs[n]
        a_ref[i, c] = adds[n]
        l_ref[i, c] = backs[n]
        keep_ref[i, c] = jnp.broadcast_to(gates[n]["keep"], (8, DK))
    first, last = slot_of(me, 0), slot_of(me, chunks - 1)
    stacks = [jnp.concatenate([d_ref[i, first], a_ref[i, first]], axis=0) for i in range(2)]
    keeps = [keep_ref[i, first][:1] for i in range(2)]
    grads = [l_ref[i, last] for i in range(2)]
    for step in range(1, chunks):
        n, m = slot_of(me, step), slot_of(me, chunks - 1 - step)
        ahead = [dot3(stacks[i], d_ref[i, n]) for i in range(2)]
        behind = [dot3(grads[i], d_ref[i, m], NT) for i in range(2)]
        for i in range(2):
            keep = keep_ref[i, n][:1]
            stacks[i] = (
                keep * stacks[i]
                + ahead[i]
                + jnp.concatenate([keeps[i] * d_ref[i, n], a_ref[i, n]], axis=0)
            )
            keeps[i] = keeps[i] * keep
            grads[i] = keep_ref[i, m][:1] * grads[i] + behind[i] + l_ref[i, m]
    for i in range(2):
        dev, add = stacks[i][:DK], stacks[i][DK:]
        high, rest = split(keeps[i])
        middle, last = split(keeps[i] - high.astype(f32))
        line = lax.broadcasted_iota(jnp.int32, (16, DK), 0)
        scale = jnp.where(line == 2, last.astype(f32), 0.0)
        scale = jnp.where(line == 1, middle.astype(f32), scale)
        scale = low(jnp.where(line == 0, high.astype(f32), scale))
        for way, (step_map, addend) in enumerate(((dev, add), (dev.T, grads[i]))):
            send_ref[i, way, :DK] = low(step_map)
            send_ref[i, way, DK : DK + DV] = low(addend)
            send_ref[i, way, DK + DV :] = scale


def segment_parts(block):
    scale = jnp.sum(block[DK + DV :].astype(f32), axis=0, keepdims=True)
    return block[:DK], block[DK : DK + DV].astype(f32), scale


def combine_kernel(where_ref, x_ref, out_ref):
    count = x_ref.shape[0]
    flip = where_ref[0]
    for step in range(count):
        at = jnp.where(flip == 1, count - 1 - step, step)
        step_map, addend, scale = segment_parts(x_ref[at])
        if step == 0:
            stack = jnp.concatenate([step_map.astype(f32), addend], axis=0)
            keep = scale
        else:
            stack = (
                scale * stack
                + dot(wide(stack, 1), twice(step_map, 0))
                + jnp.concatenate([keep * step_map.astype(f32), addend], axis=0)
            )
            keep = keep * scale
    out_ref[: DK + DV] = stack
    out_ref[DK + DV :] = jnp.broadcast_to(keep, (8, DK))


def chain_kernel(where_ref, x_ref, one_ref, two_ref, three_ref, out_ref):
    count = x_ref.shape[0]
    flip = where_ref[0]
    place = where_ref[1]
    rows = where_ref[2]
    state = jnp.zeros((DV, DK), f32)
    for n, ahead, back in ((3, three_ref, one_ref), (2, two_ref, two_ref), (1, one_ref, three_ref)):
        block = jnp.where(flip == 1, back[...], ahead[...])
        there = jnp.where(flip == 1, place + n < rows, n <= place)
        later = (
            block[DK + DV : DK + DV + 1] * state + dot3(state, block[:DK]) + block[DK : DK + DV]
        )
        state = jnp.where(there, later, state)
    for step in range(count):
        at = jnp.where(flip == 1, count - 1 - step, step)
        out_ref[at] = low(state)
        if step < count - 1:
            step_map, addend, scale = segment_parts(x_ref[at])
            state = state * scale + dot(wide(state, 1), twice(step_map, 0)) + addend


def final_kernel(base, me_ref, *refs):
    ins, refs = refs[: 5 * CHUNKS], refs[5 * CHUNKS :]
    w_ref, f_ref, t_ref, u_ref, d_ref, a_ref, l_ref, h_ref = refs[:8]
    out_refs = refs[8 : 8 + CHUNKS]
    keep_ref, state_ref, after_ref, grad_ref = refs[8 + CHUNKS :]
    me = me_ref[0]
    here = pl.program_id(0)
    pair = base + here
    row, col = grids()
    before = row > col
    suffix = low(jnp.where(row <= col, 1.0, 0.0))
    chunks = CHUNKS
    qs, ks, vs, os, smalls = ([r[...] for r in ins[n * chunks : (n + 1) * chunks]] for n in range(5))
    terms = chunk_terms(pickers(pair), qs, ks, smalls)
    cases = [(c, i) for c in range(chunks) for i in range(2)]
    gates = [terms[c]["heads"][i] for c, i in cases]
    o_in = [os[c][:, i * DV : (i + 1) * DV] for c, i in cases]

    for n, (c, i) in enumerate(cases):
        keep_ref[i, c] = jnp.broadcast_to(gates[n]["keep"], (8, DK))
    states = [h_ref[i, 0].astype(f32) for i in range(2)]
    grads = [h_ref[i, 1].astype(f32) for i in range(2)]
    for step in range(chunks):
        n, m = slot_of(me, step), slot_of(me, chunks - 1 - step)
        for i in range(2):
            state_ref[i, n] = states[i]
            grad_ref[i, m] = grads[i]
        ahead = [dot3(states[i], d_ref[i, n]) for i in range(2)]
        if step < chunks - 1:
            behind = [dot3(grads[i], d_ref[i, m], NT) for i in range(2)]
        for i in range(2):
            states[i] = keep_ref[i, n][:1] * states[i] + ahead[i] + a_ref[i, n]
            after_ref[i, n] = states[i]
            if step < chunks - 1:
                grads[i] = keep_ref[i, m][:1] * grads[i] + behind[i] + l_ref[i, m]
    state_of = [state_ref[i, c] for c, i in cases]
    after_of = [after_ref[i, c] for c, i in cases]
    grad_of = [grad_ref[i, c] for c, i in cases]

    fresh = [
        f_ref[i, c] - dot3(w_ref[i, c], state, NT) for (c, i), state in zip(cases, state_of)
    ]
    fresh_grad = [
        u_ref[i, c]
        + (terms[c]["rk_col"] * h["to_end"]) * dot(twice(ks[c], 1), wide(grad, 1), NT)
        for (c, i), h, grad in zip(cases, gates, grad_of)
    ]
    solved = [
        dot(twice(t_ref[i, c], 0), wide(x, 0), TN) for (c, i), x in zip(cases, fresh_grad)
    ]
    value_grad = [h["beta_col"] * x for h, x in zip(gates, solved)]
    quarter = (out_refs[0].shape[1] - 128) // 4
    for (c, i), x in zip(cases, value_grad):
        start = 2 * quarter + here * (2 * DV) + i * DV
        out_refs[c][:, pl.ds(pl.multiple_of(start, DV), DV)] = low(x)
    sides = [jnp.concatenate([low(x), o], axis=0) for x, o in zip(value_grad, o_in)]
    fresh_low = [low(x) for x in fresh]
    outer = [dot(x, low(state)) for x, state in zip(sides, state_of)]
    ended = [
        h["to_end"] * dot(x, low(grad)) for h, x, grad in zip(gates, fresh_low, grad_of)
    ]
    inner = [dot(x, y, NT) for x, y in zip(sides, fresh_low)]
    key_read = [-h["growth_col"] * x[:CHUNK] for h, x in zip(gates, outer)]
    query_read = [h["growth_col"] * x[CHUNK:] for h, x in zip(gates, outer)]
    erase = [jnp.where(before, h["decay"] * x[:CHUNK], 0.0) for h, x in zip(gates, inner)]
    read = [h["decay"] * x[CHUNK:] for h, x in zip(gates, inner)]
    units = [(t["qf"] * t["rq_col"], t["kf"] * t["rk_col"]) for t in terms]
    sums = []
    for n, (c, i) in enumerate(cases):
        query_unit, key_unit = units[c]
        spread = read[n] * terms[c]["query_key"] - erase[n] * terms[c]["key_key"]
        lone = query_unit * query_read[n] + key_unit * (key_read[n] - ended[n])
        sums.append(dot(twice(suffix, 1), wide(jnp.concatenate([spread, lone], axis=1), 0)))
    query_inner, key_inner = [], []
    for c in range(chunks):
        term = terms[c]
        read_sum = read[2 * c] + read[2 * c + 1]
        erase_sum = erase[2 * c] + erase[2 * c + 1]
        query_inner.append(dot(wide(read_sum * term["rk_row"], 1), twice(ks[c], 0)))
        key_inner.append(
            dot(wide(erase_sum * -term["rk_row"], 1), twice(ks[c], 0))
            + dot(
                jnp.concatenate(
                    split(read_sum * term["rq_col"]) + split(erase_sum * -term["rk_col"]), axis=0
                ),
                jnp.concatenate([qs[c], qs[c], ks[c], ks[c]], axis=0),
                TN,
            )
        )
    small_out = []
    for c in range(chunks):
        parts, places = [], []
        wholes = 0.0
        for i in range(2):
            n = 2 * c + i
            at = 2 * pair + i
            for place, part in (
                (at, jnp.where(before, sums[n][:, :CHUNK], 0.0) + sums[n][:, CHUNK:]),
                (at + 8, (1.0 - gates[n]["beta_col"]) * solved[n] * fresh[n]),
            ):
                parts += split(part)
                places += [low(jnp.where(col == place, 1.0, 0.0))] * 2
            product = jnp.sum(grad_of[n] * after_of[n], axis=0, keepdims=True)
            whole = jnp.sum(product, axis=1, keepdims=True)
            wholes = wholes + jnp.where(col[:1] == at, whole, 0.0)
        small_out.append(
            dot(jnp.concatenate(parts, axis=1), jnp.concatenate(places, axis=0)) + wholes
        )
    for c in range(chunks):
        term = terms[c]
        query_unit, key_unit = units[c]
        query_grad = query_inner[c] + query_read[2 * c] + query_read[2 * c + 1]
        key_grad = (
            key_inner[c]
            + (key_read[2 * c] + ended[2 * c])
            + (key_read[2 * c + 1] + ended[2 * c + 1])
        )
        query_back = term["rq_col"] * (
            query_grad
            - query_unit * (DK * jnp.sum(query_unit * query_grad, axis=1, keepdims=True))
        )
        key_back = term["rk_col"] * (
            key_grad - key_unit * jnp.sum(key_unit * key_grad, axis=1, keepdims=True)
        )
        out_refs[c][:, pl.ds(pl.multiple_of(here * DK, DK), DK)] = low(query_back)
        out_refs[c][:, pl.ds(pl.multiple_of(quarter + here * DK, DK), DK)] = low(key_back)
        place = slice(4 * quarter, 4 * quarter + 128)
        mine = (col // 2 == pair) | (col // 2 == pair + 4)
        held = out_refs[c][:, place]
        kept = jnp.where(here == 0, jnp.zeros_like(held), held)
        out_refs[c][:, place] = jnp.where(mine, low(small_out[c]), kept)


def pack_kernel(me_ref, *refs):
    outs = refs[-CHUNKS:]
    for slot, out_ref in enumerate(outs):
        at = 0
        for ref in refs[4 * slot : 4 * slot + 4]:
            width = ref.shape[1]
            out_ref[:, at : at + width] = ref[...]
            at += width
    if len(refs) > 5 * CHUNKS:
        d_ref, b_ref = refs[4 * CHUNKS : 4 * CHUNKS + 2]
        for slot, out_ref in enumerate(outs):
            dest = lax.rem(me_ref[0] + slot, CHUNKS)
            row, col = grids((d_ref.shape[0], 128))
            decays = (col < HEADS) & (row == HEADS * dest + col)
            betas = (col >= HEADS) & (col < 2 * HEADS) & (row == HEADS * dest + col - HEADS)
            picks = [low(jnp.where(here, 1.0, 0.0)) for here in (decays, betas)]
            out_ref[:, at : at + 128] = low(
                dot(d_ref[...], picks[0], TN) + dot(b_ref[...], picks[1], TN)
            )


def pack(me, arrays, gates, begin, end):
    count = end - begin
    per = KEY_HEADS // count
    first = begin // count
    widths = [count * size for size in (DK, DK, 2 * DV, 2 * DV)]
    total = sum(widths) + (128 if gates else 0)
    specs = []
    for slot in range(CHUNKS):
        for width in widths:
            specs.append(
                pl.BlockSpec(
                    (CHUNK, width),
                    lambda g, me, slot=slot: (0, per * lax.rem(me[0] + slot, CHUNKS) + first),
                )
            )
    return pl.pallas_call(
        pack_kernel,
        grid_spec=pltpu.PrefetchScalarGridSpec(
            num_scalar_prefetch=1,
            grid=(1,),
            in_specs=specs + [pl.BlockSpec(gate.shape, lambda g, me: (0, 0)) for gate in gates],
            out_specs=[pl.BlockSpec((CHUNK, total), lambda g, me: (0, 0))] * CHUNKS,
        ),
        out_shape=[jax.ShapeDtypeStruct((CHUNK, total), bf16)] * CHUNKS,
        compiler_params=pltpu.CompilerParams(vmem_limit_bytes=VMEM),
        name="pack",
    )(me, *(list(arrays) * CHUNKS), *gates)


def unpack_kernel(me_ref, *refs):
    arrived = refs[: len(GROUPS) * CHUNKS]
    q_ref, k_ref, v_ref, d_ref, b_ref = refs[len(GROUPS) * CHUNKS :]
    d_sum, b_sum = 0.0, 0.0
    row, col = grids((d_ref.shape[0], 128))
    for g, (begin, end) in enumerate(GROUPS):
        for slot in range(CHUNKS):
            ref = arrived[g * CHUNKS + slot]
            source = lax.rem(me_ref[0] + slot, CHUNKS)
            at = 0
            for out, size in ((q_ref, DK), (k_ref, DK), (v_ref, 2 * DV)):
                width = (end - begin) * size
                start = pl.multiple_of((source * KEY_HEADS + begin) * size, 128)
                out[:, pl.ds(start, width)] = ref[:, at : at + width]
                at += width
            small = ref[:, at : at + 128]
            decays = (col < HEADS) & (row == HEADS * source + col)
            betas = (col >= HEADS) & (col < 2 * HEADS) & (row == HEADS * source + col - HEADS)
            d_sum = d_sum + dot(low(jnp.where(decays, 1.0, 0.0)), small, NT)
            b_sum = b_sum + dot(low(jnp.where(betas, 1.0, 0.0)), small, NT)
    d_ref[...] = low(d_sum)
    b_ref[...] = low(b_sum)


def whole(shape):
    return pl.BlockSpec(shape, lambda g, me: (0,) * len(shape))


def unpack(me, groups):
    arrived = [x for group in groups for x in group]
    shapes = [(CHUNK, CHUNKS * size) for size in (KEY_HEADS * DK, KEY_HEADS * DK, HEADS * DV)]
    shapes += [(CHUNKS * HEADS, CHUNK)] * 2
    q, k, v, d, b = pl.pallas_call(
        unpack_kernel,
        grid_spec=pltpu.PrefetchScalarGridSpec(
            num_scalar_prefetch=1,
            grid=(1,),
            in_specs=[whole(x.shape) for x in arrived],
            out_specs=[whole(shape) for shape in shapes],
        ),
        out_shape=[jax.ShapeDtypeStruct(shape, bf16) for shape in shapes],
        compiler_params=pltpu.CompilerParams(vmem_limit_bytes=VMEM),
        name="unpack",
    )(me, *arrived)
    return q, k, v, d.T, b.T


def packed_specs(count, small_at):
    return (
        [pl.BlockSpec((CHUNK, DK), lambda p, me: (0, p))] * CHUNKS
        + [pl.BlockSpec((CHUNK, DK), lambda p, me: (0, count + p))] * CHUNKS
        + [pl.BlockSpec((CHUNK, 2 * DV), lambda p, me: (0, count + p))] * CHUNKS
        + [pl.BlockSpec((CHUNK, 2 * DV), lambda p, me: (0, 2 * count + p))] * CHUNKS
        + [pl.BlockSpec((CHUNK, 128), lambda p, me: (0, small_at))] * CHUNKS
    )


SAVED = (f32, f32, bf16, f32, f32, f32, f32)
SAVED_SPECS = [pl.BlockSpec((2, CHUNKS, CHUNK, CHUNK), lambda p, me: (p, 0, 0, 0)) for _ in SAVED]


def cost(count, flops):
    return pl.CostEstimate(flops=count * flops, bytes_accessed=count * 5_000_000, transcendentals=0)


def local_pass(me, packed, small, small_at, begin, end):
    count = end - begin
    return pl.pallas_call(
        functools.partial(local_kernel, begin),
        grid_spec=pltpu.PrefetchScalarGridSpec(
            num_scalar_prefetch=1,
            grid=(count,),
            in_specs=packed_specs(count, small_at),
            out_specs=[pl.BlockSpec((2, 2, PAYLOAD, DK), lambda p, me: (p, 0, 0, 0))] + SAVED_SPECS,
            scratch_shapes=[pltpu.VMEM((2, CHUNKS, 8, DK), f32)],
        ),
        out_shape=[jax.ShapeDtypeStruct((2 * count, 2, PAYLOAD, DK), bf16)]
        + [jax.ShapeDtypeStruct((2 * count, CHUNKS, CHUNK, CHUNK), kind) for kind in SAVED],
        compiler_params=pltpu.CompilerParams(vmem_limit_bytes=VMEM),
        cost_estimate=cost(count, 4_000_000_000),
        name="local_pass",
    )(me, *(list(packed) * 4), *small)


def combine_pass(place, received):
    shape = (DK + DV + 8, DK)
    return pl.pallas_call(
        combine_kernel,
        grid_spec=pltpu.PrefetchScalarGridSpec(
            num_scalar_prefetch=1,
            grid=(1,),
            in_specs=[whole(received.shape)],
            out_specs=whole(shape),
        ),
        out_shape=jax.ShapeDtypeStruct(shape, f32),
        compiler_params=pltpu.CompilerParams(vmem_limit_bytes=VMEM),
        cost_estimate=cost(1, 1_500_000_000),
        name="combine_pass",
    )(place, received)


def chain_pass(place, received, others):
    shape = (received.shape[0], DV, DK)
    return pl.pallas_call(
        chain_kernel,
        grid_spec=pltpu.PrefetchScalarGridSpec(
            num_scalar_prefetch=1,
            grid=(1,),
            in_specs=[whole(received.shape)] + [whole(x.shape) for x in others],
            out_specs=whole(shape),
        ),
        out_shape=jax.ShapeDtypeStruct(shape, bf16),
        compiler_params=pltpu.CompilerParams(vmem_limit_bytes=VMEM),
        cost_estimate=cost(1, 1_500_000_000),
        name="chain_pass",
    )(place, received, *others)


def final_pass(me, packed, small, small_at, saved, states, begin, end):
    count = end - begin
    width = count * 2 * (DK + DV) + 128
    square = (2, CHUNKS, DV, DK)
    return pl.pallas_call(
        functools.partial(final_kernel, begin),
        grid_spec=pltpu.PrefetchScalarGridSpec(
            num_scalar_prefetch=1,
            grid=(count,),
            in_specs=packed_specs(count, small_at)
            + SAVED_SPECS
            + [pl.BlockSpec((2, 2, DV, DK), lambda p, me: (p, 0, 0, 0))],
            out_specs=[pl.BlockSpec((CHUNK, width), lambda p, me: (0, 0))] * CHUNKS,
            scratch_shapes=[pltpu.VMEM((2, CHUNKS, 8, DK), f32)] + [pltpu.VMEM(square, f32)] * 3,
        ),
        out_shape=[jax.ShapeDtypeStruct((CHUNK, width), bf16)] * CHUNKS,
        compiler_params=pltpu.CompilerParams(vmem_limit_bytes=VMEM),
        cost_estimate=cost(count, 4_000_000_000),
        name="final_pass",
    )(me, *(list(packed) * 4), *small, *saved, states)


def turned(slots, way):
    count = lax.axis_size("head")
    return [slots[0]] + [
        lax.ppermute(slots[s], "head", [(i, (i + way * s) % count) for i in range(count)])
        for s in range(1, count)
    ]


def recursion(sends, place):
    segments = lax.axis_size("ctx")
    rows = segments // HEADS
    near = [[y * HEADS + r for r in range(HEADS)] for y in range(rows)]
    received = lax.all_to_all(
        sends, "ctx", split_axis=0, concat_axis=0, axis_index_groups=near, tiled=True
    )
    combined = combine_pass(place, received)
    others = [
        lax.ppermute(
            combined, "ctx", [(i, (i + s * HEADS) % segments) for i in range(segments)]
        )
        for s in range(1, rows)
    ]
    return lax.all_to_all(
        chain_pass(place, received, others),
        "ctx",
        split_axis=0,
        concat_axis=0,
        axis_index_groups=near,
        tiled=True,
    )


def on_device(query_rows, key_rows, value_rows, log_decay, beta_logit, out_grad):
    arrays = [query_rows, key_rows, value_rows, out_grad]
    gates = [log_decay.T, beta_logit.T]
    me = lax.axis_index("head").astype(jnp.int32).reshape(1)
    segment = lax.axis_index("ctx").astype(jnp.int32)
    rows = lax.axis_size("ctx") // HEADS
    place = jnp.stack([segment % 2, segment // HEADS, jnp.int32(rows)])
    received = []
    for b, e in GROUPS:
        slots = pack(me, arrays, gates if b == 0 else [], b, e)
        if received:
            slots, received[-1] = lax.optimization_barrier((slots, received[-1]))
        received.append(turned(slots, 1))
    small = received[0]
    small_at = small[0].shape[1] // 128 - 1
    saved, states, outs = [], [], []
    for (b, e), packed in zip(GROUPS, received):
        sends, *kept = local_pass(me, packed, small, small_at, b, e)
        saved.append(kept)
        found = recursion(sends.reshape(HEADS, PAYLOAD, DK), place)
        states.append(found.reshape(2 * (e - b), 2, DV, DK))
    for (b, e), packed, kept, state in zip(GROUPS, received, saved, states):
        outs.append(turned(final_pass(me, packed, small, small_at, kept, state, b, e), -1))
    return unpack(me, outs)


def solution(mesh):
    spec = P(("ctx", "head"), None)
    return jax.shard_map(
        on_device, mesh=mesh, in_specs=(spec,) * 6, out_specs=(spec,) * 5, check_vma=False
    )
```

time: 181 us -> 159 us (0.88)
  blocking collectives: 37.1 us -> 0 us
  starting transfers between devices: 19.8 us -> 42.8 us
  waiting for transfers between devices: 55.3 us -> 34.9 us
  Pallas kernels: 63.3 us -> 69.5 us
  local copies, waits for them, and re-layouts: 2.35 us -> 8.03 us
    all_to_all x4, waiting for transfers between devices: 55.3 us -> 5.13 us  [the longest x2 2.91 us: recursion(): lax.all_to_all(sends, 'ctx', split_axis=0, concat_axis=0, axis_index_grou...]
    all_to_all x2 -> x0, blocking collectives: 37.1 us -> none  [the longest x1 20.7 us: exchange(): lax.all_to_all(packed, 'head', split_axis=0, concat_axis=0, tiled=True)]
    ppermute x0 -> x18, waiting for transfers between devices: none -> 29.7 us  [the longest x12 29.7 us: turned(): lax.ppermute(slots[s], 'head', [(i, (i + way * s) % count) for i in range...]
    ppermute x0 -> x18, starting transfers between devices: none -> 26.8 us  [the longest x12 19.1 us: turned(): lax.ppermute(slots[s], 'head', [(i, (i + way * s) % count) for i in range...]
    unnamed x8 -> x44, local copies, waits for them, and re-layouts: 2.35 us -> 8.03 us
    pallas_call x7 -> x9, Pallas kernels: 57.7 us -> 61.8 us  [the longest x2 25.2 us: local_pass(): pl.pallas_call(functools.partial(local_kernel, begin), grid_spec=pltpu.Pr...]
    all_to_all x4, starting transfers between devices: 19.8 us -> 15.9 us  [the longest x2 9.11 us: recursion(): lax.all_to_all(sends, 'ctx', split_axis=0, concat_axis=0, axis_index_grou...]
    pallas_call x1 -> x2, Pallas kernels: 5.67 us -> 7.72 us  [chain_pass(): pl.pallas_call(chain_kernel, grid_spec=pltpu.PrefetchScalarGridSpec(num_s...]
  transfers between devices with their start and end apart: 4 -> 22, of which waited for: 4 -> 6; matrix products, arithmetic and copies ran while one was open for 0% -> 0% of each run, Pallas kernels for 15% -> 41%
where the time goes in v3:
time: 159 us; the launch traced here: 157 us
  Pallas kernels  69.5 us (44%)
  starting transfers between devices  42.8 us (27%)
  waiting for transfers between devices  34.9 us (22%)
  local copies, waits for them, and re-layouts  8.03 us (5%)
    ppermute x12, waiting for transfers between devices, turned(): lax.ppermute(slots[s], 'head', [(i, (i + way * s) % count) for i in range...  29.7 us
    pallas_call x2, Pallas kernels, local_pass(): pl.pallas_call(functools.partial(local_kernel, begin), grid_spec=pltpu.Pr...  25.2 us
    pallas_call x2, Pallas kernels, final_pass(): pl.pallas_call(functools.partial(final_kernel, begin), grid_spec=pltpu.Pr...  21.3 us
    ppermute x12, starting transfers between devices, turned(): lax.ppermute(slots[s], 'head', [(i, (i + way * s) % count) for i in range...  19.1 us
    all_to_all x2, starting transfers between devices, recursion(): lax.all_to_all(sends, 'ctx', split_axis=0, concat_axis=0, axis_index_grou...  9.11 us
    unnamed x44, local copies, waits for them, and re-layouts  8.03 us
    ppermute x6, starting transfers between devices, recursion(): lax.ppermute(combined, 'ctx', [(i, (i + s * HEADS) % segments) for i in r...  7.75 us
    pallas_call x2, Pallas kernels, chain_pass(): pl.pallas_call(chain_kernel, grid_spec=pltpu.PrefetchScalarGridSpec(num_s...  7.72 us
  transfers between devices with their start and end apart: 22, of which 6 were waited for; matrix products, arithmetic and copies ran while one was open for 0% of the time, Pallas kernels for 41%

profile of v3, /device:TPU:24, one launch (start us, length us, event | category | flops | bytes accessed | tf_op | source)
XLA Modules:
  0.0 156.6 jit_solution(4870462288571092788)
XLA Ops:
  0.6 2.9 %pack.3 = (bf16[128,1664]{1,0:T(8,128)(2,1)}, bf16[128,1664]{1,0:T(8,128)(2,1)}, bf16[128,1664]{1,0:T(8,128)(2,1)}, bf16[128,1664]{1,0:T(8,128)(2,1)}) custom-call(s32[1]{0:T(128)} %bitcast.me_ref, bf16[128,2048]{1,0:T(8,128)(2,1)} %refs_12_.3, bf16[128,2048]{1,0:T(8,128)(2,1)} %refs_13_.3, bf16[128,4096]{1,0:T(8,128)(2,1)} %refs_14_.3, ...), custom_call_target="tpu_custom_call" | custom-call | tf_op jit(solution)/shard_map/pack/pallas_call | solution.py:457
  3.5 1.9 %collective-permute-start = (bf16[128,1664]{1,0:T(8,128)(2,1)}, bf16[128,1664]{1,0:T(8,128)(2,1)S(1)}, u32[]{:S(2)}, u32[]{:S(2)}) collective-permute-start(bf16[128,1664]{1,0:T(8,128)(2,1)} %get-tuple-element.55), channel_id=1, source_target_pairs={{0,1},{1,2},{2,3},{3,0},{4,5},{5,6},{6,7},{7,4},{8,9},{9,10},{10,1... | collective-permute-start | bytes 1277960 | tf_op jit(solution)/shard_map/ppermute | solution.py:614
  5.5 3.6 %collective-permute-start.1 = (bf16[128,1664]{1,0:T(8,128)(2,1)}, bf16[128,1664]{1,0:T(8,128)(2,1)S(1)}, u32[]{:S(2)}, u32[]{:S(2)}) collective-permute-start(bf16[128,1664]{1,0:T(8,128)(2,1)} %get-tuple-element.56), channel_id=1, source_target_pairs={{0,2},{1,3},{2,0},{3,1},{4,6},{5,7},{6,4},{7,5},{8,10},{9,11},{10,... | collective-permute-start | bytes 1277960 | tf_op jit(solution)/shard_map/ppermute | solution.py:614
  9.0 1.0 collective-permute-start.2
  10.1 2.7 %pack.2 = (bf16[128,1536]{1,0:T(8,128)(2,1)}, bf16[128,1536]{1,0:T(8,128)(2,1)}, bf16[128,1536]{1,0:T(8,128)(2,1)}, bf16[128,1536]{1,0:T(8,128)(2,1)}) custom-call(s32[1]{0:T(128)} %bitcast.me_ref, bf16[128,2048]{1,0:T(8,128)(2,1)} %refs_12_.3, bf16[128,2048]{1,0:T(8,128)(2,1)} %refs_13_.3, bf16[128,4096]{1,0:T(8,128)(2,1)} %refs_14_.3, ...), custom_call_target="tpu_custom_call" | custom-call | tf_op jit(solution)/shard_map/pack/pallas_call | solution.py:457
  12.7 4.9 %collective-permute-done.refs_1_.refs_5_.refs_9_.refs_13_.refs_17_ = bf16[128,1664]{1,0:T(8,128)(2,1)S(1)} collective-permute-done((bf16[128,1664]{1,0:T(8,128)(2,1)}, bf16[128,1664]{1,0:T(8,128)(2,1)S(1)}, u32[]{:S(2)}, u32[]{:S(2)}) %collective-permute-start) | collective-permute-done | bytes 426016 | tf_op jit(solution)/shard_map/ppermute | solution.py:614
  17.6 10.3 %collective-permute-done.1.refs_2_.refs_6_.refs_10_.refs_14_.refs_18_ = bf16[128,1664]{1,0:T(8,128)(2,1)S(1)} collective-permute-done((bf16[128,1664]{1,0:T(8,128)(2,1)}, bf16[128,1664]{1,0:T(8,128)(2,1)S(1)}, u32[]{:S(2)}, u32[]{:S(2)}) %collective-permute-start.1) | collective-permute-done | bytes 426016 | tf_op jit(solution)/shard_map/ppermute | solution.py:614
  27.9 0.0 collective-permute-done.2.refs_3_.refs_7_.refs_11_.refs_15_.refs_19_
  27.9 1.2 collective-permute-start.9
  29.1 2.4 %collective-permute-start.10 = (bf16[128,1536]{1,0:T(8,128)(2,1)}, bf16[128,1536]{1,0:T(8,128)(2,1)S(1)}, u32[]{:S(2)}, u32[]{:S(2)}) collective-permute-start(bf16[128,1536]{1,0:T(8,128)(2,1)} %get-tuple-element.76), channel_id=1, source_target_pairs={{0,2},{1,3},{2,0},{3,1},{4,6},{5,7},{6,4},{7,5},{8,10},{9,11},{10,... | collective-permute-start | bytes 1179656 | tf_op jit(solution)/shard_map/ppermute | solution.py:614
  31.5 1.3 collective-permute-start.11
  32.8 12.7 %local_pass.2 = (bf16[4,2,272,128]{3,2,1,0:T(8,128)(2,1)}, f32[4,4,128,128]{3,2,1,0:T(8,128)}, f32[4,4,128,128]{3,2,1,0:T(8,128)}, bf16[4,4,128,128]{3,2,1,0:T(8...) custom-call(s32[1]{0:T(128)} %bitcast.me_ref, ...), custom_call_target="tpu_custom_call" | custom-call | flops 8000000000 | bytes 10000000 | tf_op jit(solution)/shard_map/local_pass/pallas_call | solution.py:538
  45.5 4.3 %all-to-all-start = ((bf16[8,272,128]{2,1,0:T(8,128)(2,1)}), bf16[8,272,128]{2,1,0:T(8,128)(2,1)S(1)}, u32[]{:S(2)}, u32[]{:S(2)}) async-start(bf16[8,272,128]{2,1,0:T(8,128)(2,1)} %bitcast.12), calls=%async_computation | async-start | bytes 1114112 | tf_op jit(solution)/shard_map/all_to_all | solution.py:623
  49.8 0.0 collective-permute-done.9.refs_1_.refs_5_.refs_9_.refs_13_
  49.8 0.0 collective-permute-done.10.refs_2_.refs_6_.refs_10_.refs_14_
  49.8 0.0 collective-permute-done.11.refs_3_.refs_7_.refs_11_.refs_15_
  49.8 0.7 copy-done.13
  50.5 0.1 copy-done.14
  50.7 0.7 copy-done.15
  51.4 12.5 %local_pass.3 = (bf16[4,2,272,128]{3,2,1,0:T(8,128)(2,1)}, f32[4,4,128,128]{3,2,1,0:T(8,128)}, f32[4,4,128,128]{3,2,1,0:T(8,128)}, bf16[4,4,128,128]{3,2,1,0:T(8...) custom-call(s32[1]{0:T(128)} %bitcast.me_ref, ...), custom_call_target="tpu_custom_call" | custom-call | flops 8000000000 | bytes 10000000 | tf_op jit(solution)/shard_map/local_pass/pallas_call | solution.py:538
  64.0 0.0 all-to-all-done.x_ref
  64.0 0.9 copy-done
  64.9 4.8 %all-to-all-start.2 = ((bf16[8,272,128]{2,1,0:T(8,128)(2,1)}), bf16[8,272,128]{2,1,0:T(8,128)(2,1)S(1)}, u32[]{:S(2)}, u32[]{:S(2)}) async-start(bf16[8,272,128]{2,1,0:T(8,128)(2,1)} %bitcast.11), calls=%async_computation.2 | async-start | bytes 1114112 | tf_op jit(solution)/shard_map/all_to_all | solution.py:623
  69.7 0.6 pad_add_fusion.where_ref
  70.2 3.3 %combine_pass.2 = f32[264,128]{1,0:T(8,128)} custom-call(s32[3]{0:T(128)} %pad_add_fusion.where_ref, bf16[8,272,128]{2,1,0:T(8,128)(2,1)} %copy-done), custom_call_target="tpu_custom_call" | custom-call | flops 1500000000 | bytes 5000000 | tf_op jit(solution)/shard_map/combine_pass/pallas_call | solution.py:557
  73.6 0.7 collective-permute-start.5
  74.3 0.9 collective-permute-start.4
  75.3 2.2 %collective-permute-start.3 = (f32[264,128]{1,0:T(8,128)}, f32[264,128]{1,0:T(8,128)S(1)}, u32[]{:S(2)}, u32[]{:S(2)}) collective-permute-start(f32[264,128]{1,0:T(8,128)} %combine_pass.2), channel_id=1, source_target_pairs={{0,32},{4,36},{8,40},{12,44},{16,48},{20,52},{24,56},{28,60},{32,6... | collective-permute-start | bytes 405512 | tf_op jit(solution)/shard_map/ppermute | solution.py:628
  77.5 2.9 %all-to-all-done.2.x_ref = bf16[8,272,128]{2,1,0:T(8,128)(2,1)S(1)} async-done(((bf16[8,272,128]{2,1,0:T(8,128)(2,1)}), bf16[8,272,128]{2,1,0:T(8,128)(2,1)S(1)}, u32[]{:S(2)}, u32[]{:S(2)}) %all-to-all-start.2) | async-done | bytes 557088 | tf_op jit(solution)/shard_map/all_to_all | solution.py:623
  80.4 0.8 copy-done.1
  81.2 3.3 %combine_pass.3 = f32[264,128]{1,0:T(8,128)} custom-call(s32[3]{0:T(128)} %pad_add_fusion.where_ref, bf16[8,272,128]{2,1,0:T(8,128)(2,1)} %copy-done.1), custom_call_target="tpu_custom_call" | custom-call | flops 1500000000 | bytes 5000000 | tf_op jit(solution)/shard_map/combine_pass/pallas_call | solution.py:557
  84.5 0.7 collective-permute-start.14
  85.2 0.9 collective-permute-start.13
  86.2 0.0 collective-permute-done.5.three_ref
  86.2 2.2 %collective-permute-start.12 = (f32[264,128]{1,0:T(8,128)}, f32[264,128]{1,0:T(8,128)S(1)}, u32[]{:S(2)}, u32[]{:S(2)}) collective-permute-start(f32[264,128]{1,0:T(8,128)} %combine_pass.3), channel_id=1, source_target_pairs={{0,32},{4,36},{8,40},{12,44},{16,48},{20,52},{24,56},{28,60},{32,6... | collective-permute-start | bytes 405512 | tf_op jit(solution)/shard_map/ppermute | solution.py:628
  88.4 0.0 collective-permute-done.4.two_ref
  88.4 0.0 collective-permute-done.3.one_ref
  88.4 0.6 copy-done.19
  89.0 0.7 copy-done.20
  89.7 3.9 %chain_pass.2 = bf16[8,128,128]{2,1,0:T(8,128)(2,1)} custom-call(s32[3]{0:T(128)} %pad_add_fusion.where_ref, bf16[8,272,128]{2,1,0:T(8,128)(2,1)} %copy-done, f32[264,128]{1,0:T(8,128)} %copy-done.20, f32[264,128]{1,0:T(8,128)} %copy-done.19, f32[264,128]{1,0:T(8,128)} %copy-done.17), custom_call_target="tpu_custom_call" | custom-call | flops 1500000000 | bytes 5000000 | tf_op jit(solution)/shard_map/chain_pass/pallas_call | solution.py:574
  93.6 3.4 %all-to-all-start.1 = ((bf16[8,128,128]{2,1,0:T(8,128)(2,1)}), bf16[8,128,128]{2,1,0:T(8,128)(2,1)S(1)}, u32[]{:S(2)}, u32[]{:S(2)}) async-start(bf16[8,128,128]{2,1,0:T(8,128)(2,1)} %chain_pass.2), calls=%async_computation.1 | async-start | bytes 524288 | tf_op jit(solution)/shard_map/all_to_all | solution.py:633
  97.0 0.0 collective-permute-done.14.three_ref
  97.0 0.0 collective-permute-done.13.two_ref
  97.0 0.6 copy-done.16
  97.7 0.1 copy-done.18
  97.7 0.6 copy-done.21
  98.4 3.9 %chain_pass.3 = bf16[8,128,128]{2,1,0:T(8,128)(2,1)} custom-call(s32[3]{0:T(128)} %pad_add_fusion.where_ref, bf16[8,272,128]{2,1,0:T(8,128)(2,1)} %copy-done.1, f32[264,128]{1,0:T(8,128)} %copy-done.21, f32[264,128]{1,0:T(8,128)} %copy-done.18, f32[264,128]{1,0:T(8,128)} %copy-done.16), custom_call_target="tpu_custom_call" | custom-call | flops 1500000000 | bytes 5000000 | tf_op jit(solution)/shard_map/chain_pass/pallas_call | solution.py:574
  102.2 2.2 %all-to-all-done.1 = bf16[8,128,128]{2,1,0:T(8,128)(2,1)S(1)} async-done(((bf16[8,128,128]{2,1,0:T(8,128)(2,1)}), bf16[8,128,128]{2,1,0:T(8,128)(2,1)S(1)}, u32[]{:S(2)}, u32[]{:S(2)}) %all-to-all-start.1) | async-done | bytes 262176 | tf_op jit(solution)/shard_map/all_to_all | solution.py:633
  104.4 0.7 copy-done.9
  105.1 3.4 %all-to-all-start.3 = ((bf16[8,128,128]{2,1,0:T(8,128)(2,1)}), bf16[8,128,128]{2,1,0:T(8,128)(2,1)S(1)}, u32[]{:S(2)}, u32[]{:S(2)}) async-start(bf16[8,128,128]{2,1,0:T(8,128)(2,1)} %chain_pass.3), calls=%async_computation.3 | async-start | bytes 524288 | tf_op jit(solution)/shard_map/all_to_all | solution.py:633
  108.6 10.8 %final_pass.2 = (bf16[128,1152]{1,0:T(8,128)(2,1)}, bf16[128,1152]{1,0:T(8,128)(2,1)}, bf16[128,1152]{1,0:T(8,128)(2,1)}, bf16[128,1152]{1,0:T(8,128)(2,1)}) custom-call(s32[1]{0:T(128)} %bitcast.me_ref, bf16[128,1664]{1,0:T(8,128)(2,1)} %get-tuple-element.58.refs_0_.refs_4_.refs_8_.refs_12_.refs_16_, bf16[128,1664]{1,0:T(8,128)(2,1)} %copy-done.10, ...), custom_call_target="tpu_custom_call" | custom-call | flops 8000000000 | bytes 10000000 | tf_op jit(solution)/shard_map/final_pass/pallas_call | solution.py:593
  119.3 0.5 collective-permute-start.6
  119.8 2.4 %collective-permute-start.7 = (bf16[128,1152]{1,0:T(8,128)(2,1)}, bf16[128,1152]{1,0:T(8,128)(2,1)S(1)}, u32[]{:S(2)}, u32[]{:S(2)}) collective-permute-start(bf16[128,1152]{1,0:T(8,128)(2,1)} %get-tuple-element.72), channel_id=1, source_target_pairs={{0,2},{1,3},{2,0},{3,1},{4,6},{5,7},{6,4},{7,5},{8,10},{9,11},{10,... | collective-permute-start | bytes 884744 | tf_op jit(solution)/shard_map/ppermute | solution.py:614
  122.2 0.0 collective-permute-start.8
  122.2 0.7 copy-done.8
  122.9 10.6 %final_pass.3 = (bf16[128,1152]{1,0:T(8,128)(2,1)}, bf16[128,1152]{1,0:T(8,128)(2,1)}, bf16[128,1152]{1,0:T(8,128)(2,1)}, bf16[128,1152]{1,0:T(8,128)(2,1)}) custom-call(s32[1]{0:T(128)} %bitcast.me_ref, bf16[128,1536]{1,0:T(8,128)(2,1)} %get-tuple-element.74.refs_0_.refs_4_.refs_8_.refs_12_, bf16[128,1536]{1,0:T(8,128)(2,1)} %copy-done.13, ...), custom_call_target="tpu_custom_call" | custom-call | flops 8000000000 | bytes 10000000 | tf_op jit(solution)/shard_map/final_pass/pallas_call | solution.py:593
  133.5 3.3 %collective-permute-start.15 = (bf16[128,1152]{1,0:T(8,128)(2,1)}, bf16[128,1152]{1,0:T(8,128)(2,1)S(1)}, u32[]{:S(2)}, u32[]{:S(2)}) collective-permute-start(bf16[128,1152]{1,0:T(8,128)(2,1)} %get-tuple-element.87), channel_id=1, source_target_pairs={{0,3},{1,0},{2,1},{3,2},{4,7},{5,4},{6,5},{7,6},{8,11},{9,8},{10,9... | collective-permute-start | bytes 884744 | tf_op jit(solution)/shard_map/ppermute | solution.py:614
  136.8 0.2 collective-permute-start.16
  137.0 1.3 collective-permute-start.17
  138.4 11.0 %collective-permute-done.15.refs_5_ = bf16[128,1152]{1,0:T(8,128)(2,1)S(1)} collective-permute-done((bf16[128,1152]{1,0:T(8,128)(2,1)}, bf16[128,1152]{1,0:T(8,128)(2,1)S(1)}, u32[]{:S(2)}, u32[]{:S(2)}) %collective-permute-start.15) | collective-permute-done | bytes 294944 | tf_op jit(solution)/shard_map/ppermute | solution.py:614
  149.4 0.0 collective-permute-done.16.refs_6_
  149.4 3.5 %collective-permute-done.17.refs_7_ = bf16[128,1152]{1,0:T(8,128)(2,1)S(1)} collective-permute-done((bf16[128,1152]{1,0:T(8,128)(2,1)}, bf16[128,1152]{1,0:T(8,128)(2,1)S(1)}, u32[]{:S(2)}, u32[]{:S(2)}) %collective-permute-start.17) | collective-permute-done | bytes 294944 | tf_op jit(solution)/shard_map/ppermute | solution.py:614
  152.9 0.7 copy-done.7
  153.6 3.0 %unpack.1 = (bf16[128,2048]{1,0:T(8,128)(2,1)}, bf16[128,2048]{1,0:T(8,128)(2,1)}, bf16[128,4096]{1,0:T(8,128)(2,1)}, bf16[32,128]{1,0:T(8,128)(2,1)}, bf16[32,128]{1,0:T(8,128)(2,1)}) custom-call(s32[1]{0:T(128)} %bitcast.me_ref, bf16[128,1152]{1,0:T(8,128)(2,1)} %get-tuple-element.70.refs_0_, bf16[128,1152]{1,0:T(8,128)(2,1)} %copy-done.2, ...), custom_call_target="tpu_custom_call" | custom-call | tf_op jit(solution)/shard_map/unpack/pallas_call | solution.py:503
  (36 shorter events, 0.1 us)
Async XLA Ops:
  3.5 14.1 %collective-permute-start = (bf16[128,1664]{1,0:T(8,128)(2,1)}, bf16[128,1664]{1,0:T(8,128)(2,1)S(1)}, u32[]{:S(2)}, u32[]{:S(2)}) collective-permute-start(bf16[128,1664]{1,0:T(8,128)(2,1)} %get-tuple-element.55), channel_id=1, source_target_pairs={{0,1},{1,2},{2,3},{3,0},{4,5},{5,6},{6,7},{7,4},{8,9},{9,10},{10,1... | collective-permute-start | bytes 1277960 | tf_op jit(solution)/shard_map/ppermute | solution.py:614
  5.5 22.5 %collective-permute-start.1 = (bf16[128,1664]{1,0:T(8,128)(2,1)}, bf16[128,1664]{1,0:T(8,128)(2,1)S(1)}, u32[]{:S(2)}, u32[]{:S(2)}) collective-permute-start(bf16[128,1664]{1,0:T(8,128)(2,1)} %get-tuple-element.56), channel_id=1, source_target_pairs={{0,2},{1,3},{2,0},{3,1},{4,6},{5,7},{6,4},{7,5},{8,10},{9,11},{10,... | collective-permute-start | bytes 1277960 | tf_op jit(solution)/shard_map/ppermute | solution.py:614
  9.0 18.9 %collective-permute-start.2 = (bf16[128,1664]{1,0:T(8,128)(2,1)}, bf16[128,1664]{1,0:T(8,128)(2,1)S(1)}, u32[]{:S(2)}, u32[]{:S(2)}) collective-permute-start(bf16[128,1664]{1,0:T(8,128)(2,1)} %get-tuple-element.57), channel_id=1, source_target_pairs={{0,3},{1,0},{2,1},{3,2},{4,7},{5,4},{6,5},{7,6},{8,11},{9,8},{10,9... | collective-permute-start | bytes 1277960 | tf_op jit(solution)/shard_map/ppermute | solution.py:614
  17.6 15.2 %copy-start.10 = (bf16[128,1664]{1,0:T(8,128)(2,1)}, bf16[128,1664]{1,0:T(8,128)(2,1)S(1)}, u32[]{:S(2)}) copy-start(bf16[128,1664]{1,0:T(8,128)(2,1)S(1)} %collective-permute-done.refs_1_.refs_5_.refs_9_.refs_13_.refs_17_) | copy-start | bytes 1277956
  27.9 4.9 %copy-start.11 = (bf16[128,1664]{1,0:T(8,128)(2,1)}, bf16[128,1664]{1,0:T(8,128)(2,1)S(1)}, u32[]{:S(2)}) copy-start(bf16[128,1664]{1,0:T(8,128)(2,1)S(1)} %collective-permute-done.1.refs_2_.refs_6_.refs_10_.refs_14_.refs_18_) | copy-start | bytes 1277956
  27.9 4.9 %copy-start.12 = (bf16[128,1664]{1,0:T(8,128)(2,1)}, bf16[128,1664]{1,0:T(8,128)(2,1)S(1)}, u32[]{:S(2)}) copy-start(bf16[128,1664]{1,0:T(8,128)(2,1)S(1)} %collective-permute-done.2.refs_3_.refs_7_.refs_11_.refs_15_.refs_19_) | copy-start | bytes 1277956
  27.9 21.9 %collective-permute-start.9 = (bf16[128,1536]{1,0:T(8,128)(2,1)}, bf16[128,1536]{1,0:T(8,128)(2,1)S(1)}, u32[]{:S(2)}, u32[]{:S(2)}) collective-permute-start(bf16[128,1536]{1,0:T(8,128)(2,1)} %get-tuple-element.75), channel_id=1, source_target_pairs={{0,1},{1,2},{2,3},{3,0},{4,5},{5,6},{6,7},{7,4},{8,9},{9,10},{10,1... | collective-permute-start | bytes 1179656 | tf_op jit(solution)/shard_map/ppermute | solution.py:614
  29.1 20.7 %collective-permute-start.10 = (bf16[128,1536]{1,0:T(8,128)(2,1)}, bf16[128,1536]{1,0:T(8,128)(2,1)S(1)}, u32[]{:S(2)}, u32[]{:S(2)}) collective-permute-start(bf16[128,1536]{1,0:T(8,128)(2,1)} %get-tuple-element.76), channel_id=1, source_target_pairs={{0,2},{1,3},{2,0},{3,1},{4,6},{5,7},{6,4},{7,5},{8,10},{9,11},{10,... | collective-permute-start | bytes 1179656 | tf_op jit(solution)/shard_map/ppermute | solution.py:614
  31.5 18.3 %collective-permute-start.11 = (bf16[128,1536]{1,0:T(8,128)(2,1)}, bf16[128,1536]{1,0:T(8,128)(2,1)S(1)}, u32[]{:S(2)}, u32[]{:S(2)}) collective-permute-start(bf16[128,1536]{1,0:T(8,128)(2,1)} %get-tuple-element.77), channel_id=1, source_target_pairs={{0,3},{1,0},{2,1},{3,2},{4,7},{5,4},{6,5},{7,6},{8,11},{9,8},{10,9... | collective-permute-start | bytes 1179656 | tf_op jit(solution)/shard_map/ppermute | solution.py:614
  45.5 18.5 %all-to-all-start = ((bf16[8,272,128]{2,1,0:T(8,128)(2,1)}), bf16[8,272,128]{2,1,0:T(8,128)(2,1)S(1)}, u32[]{:S(2)}, u32[]{:S(2)}) async-start(bf16[8,272,128]{2,1,0:T(8,128)(2,1)} %bitcast.12), calls=%async_computation | async-start | bytes 1114112 | tf_op jit(solution)/shard_map/all_to_all | solution.py:623
  49.8 0.8 copy-start.13
  49.8 0.9 copy-start.14
  50.7 0.8 copy-start.15
  64.0 0.9 copy-start
  64.9 15.5 %all-to-all-start.2 = ((bf16[8,272,128]{2,1,0:T(8,128)(2,1)}), bf16[8,272,128]{2,1,0:T(8,128)(2,1)S(1)}, u32[]{:S(2)}, u32[]{:S(2)}) async-start(bf16[8,272,128]{2,1,0:T(8,128)(2,1)} %bitcast.11), calls=%async_computation.2 | async-start | bytes 1114112 | tf_op jit(solution)/shard_map/all_to_all | solution.py:623
  73.6 12.6 %collective-permute-start.5 = (f32[264,128]{1,0:T(8,128)}, f32[264,128]{1,0:T(8,128)S(1)}, u32[]{:S(2)}, u32[]{:S(2)}) collective-permute-start(f32[264,128]{1,0:T(8,128)} %combine_pass.2), channel_id=1, source_target_pairs={{0,96},{4,100},{8,104},{12,108},{16,112},{20,116},{24,120},{28,124... | collective-permute-start | bytes 405512 | tf_op jit(solution)/shard_map/ppermute | solution.py:628
  74.3 14.1 %collective-permute-start.4 = (f32[264,128]{1,0:T(8,128)}, f32[264,128]{1,0:T(8,128)S(1)}, u32[]{:S(2)}, u32[]{:S(2)}) collective-permute-start(f32[264,128]{1,0:T(8,128)} %combine_pass.2), channel_id=1, source_target_pairs={{0,64},{4,68},{8,72},{12,76},{16,80},{20,84},{24,88},{28,92},{32,9... | collective-permute-start | bytes 405512 | tf_op jit(solution)/shard_map/ppermute | solution.py:628
  75.3 13.1 %collective-permute-start.3 = (f32[264,128]{1,0:T(8,128)}, f32[264,128]{1,0:T(8,128)S(1)}, u32[]{:S(2)}, u32[]{:S(2)}) collective-permute-start(f32[264,128]{1,0:T(8,128)} %combine_pass.2), channel_id=1, source_target_pairs={{0,32},{4,36},{8,40},{12,44},{16,48},{20,52},{24,56},{28,60},{32,6... | collective-permute-start | bytes 405512 | tf_op jit(solution)/shard_map/ppermute | solution.py:628
  80.4 0.8 copy-start.1
  84.5 12.5 %collective-permute-start.14 = (f32[264,128]{1,0:T(8,128)}, f32[264,128]{1,0:T(8,128)S(1)}, u32[]{:S(2)}, u32[]{:S(2)}) collective-permute-start(f32[264,128]{1,0:T(8,128)} %combine_pass.3), channel_id=1, source_target_pairs={{0,96},{4,100},{8,104},{12,108},{16,112},{20,116},{24,120},{28,124... | collective-permute-start | bytes 405512 | tf_op jit(solution)/shard_map/ppermute | solution.py:628
  85.2 11.8 %collective-permute-start.13 = (f32[264,128]{1,0:T(8,128)}, f32[264,128]{1,0:T(8,128)S(1)}, u32[]{:S(2)}, u32[]{:S(2)}) collective-permute-start(f32[264,128]{1,0:T(8,128)} %combine_pass.3), channel_id=1, source_target_pairs={{0,64},{4,68},{8,72},{12,76},{16,80},{20,84},{24,88},{28,92},{32,9... | collective-permute-start | bytes 405512 | tf_op jit(solution)/shard_map/ppermute | solution.py:628
  86.2 2.2 %copy-start.17 = (f32[264,128]{1,0:T(8,128)}, f32[264,128]{1,0:T(8,128)S(1)}, u32[]{:S(2)}) copy-start(f32[264,128]{1,0:T(8,128)S(1)} %collective-permute-done.5.three_ref) | copy-start | bytes 405508
  86.2 10.8 %collective-permute-start.12 = (f32[264,128]{1,0:T(8,128)}, f32[264,128]{1,0:T(8,128)S(1)}, u32[]{:S(2)}, u32[]{:S(2)}) collective-permute-start(f32[264,128]{1,0:T(8,128)} %combine_pass.3), channel_id=1, source_target_pairs={{0,32},{4,36},{8,40},{12,44},{16,48},{20,52},{24,56},{28,60},{32,6... | collective-permute-start | bytes 405512 | tf_op jit(solution)/shard_map/ppermute | solution.py:628
  88.4 0.7 copy-start.19
  89.0 0.7 copy-start.20
  93.6 10.9 %all-to-all-start.1 = ((bf16[8,128,128]{2,1,0:T(8,128)(2,1)}), bf16[8,128,128]{2,1,0:T(8,128)(2,1)S(1)}, u32[]{:S(2)}, u32[]{:S(2)}) async-start(bf16[8,128,128]{2,1,0:T(8,128)(2,1)} %chain_pass.2), calls=%async_computation.1 | async-start | bytes 524288 | tf_op jit(solution)/shard_map/all_to_all | solution.py:633
  97.0 0.7 copy-start.16
  97.0 0.7 copy-start.18
  97.7 0.6 copy-start.21
  104.4 0.7 copy-start.9
  105.1 17.1 %all-to-all-start.3 = ((bf16[8,128,128]{2,1,0:T(8,128)(2,1)}), bf16[8,128,128]{2,1,0:T(8,128)(2,1)S(1)}, u32[]{:S(2)}, u32[]{:S(2)}) async-start(bf16[8,128,128]{2,1,0:T(8,128)(2,1)} %chain_pass.3), calls=%async_computation.3 | async-start | bytes 524288 | tf_op jit(solution)/shard_map/all_to_all | solution.py:633
  119.3 17.7 %collective-permute-start.6 = (bf16[128,1152]{1,0:T(8,128)(2,1)}, bf16[128,1152]{1,0:T(8,128)(2,1)S(1)}, u32[]{:S(2)}, u32[]{:S(2)}) collective-permute-start(bf16[128,1152]{1,0:T(8,128)(2,1)} %get-tuple-element.71), channel_id=1, source_target_pairs={{0,3},{1,0},{2,1},{3,2},{4,7},{5,4},{6,5},{7,6},{8,11},{9,8},{10,9... | collective-permute-start | bytes 884744 | tf_op jit(solution)/shard_map/ppermute | solution.py:614
  119.8 18.5 %collective-permute-start.7 = (bf16[128,1152]{1,0:T(8,128)(2,1)}, bf16[128,1152]{1,0:T(8,128)(2,1)S(1)}, u32[]{:S(2)}, u32[]{:S(2)}) collective-permute-start(bf16[128,1152]{1,0:T(8,128)(2,1)} %get-tuple-element.72), channel_id=1, source_target_pairs={{0,2},{1,3},{2,0},{3,1},{4,6},{5,7},{6,4},{7,5},{8,10},{9,11},{10,... | collective-permute-start | bytes 884744 | tf_op jit(solution)/shard_map/ppermute | solution.py:614
  122.2 16.1 %collective-permute-start.8 = (bf16[128,1152]{1,0:T(8,128)(2,1)}, bf16[128,1152]{1,0:T(8,128)(2,1)S(1)}, u32[]{:S(2)}, u32[]{:S(2)}) collective-permute-start(bf16[128,1152]{1,0:T(8,128)(2,1)} %get-tuple-element.73), channel_id=1, source_target_pairs={{0,1},{1,2},{2,3},{3,0},{4,5},{5,6},{6,7},{7,4},{8,9},{9,10},{10,1... | collective-permute-start | bytes 884744 | tf_op jit(solution)/shard_map/ppermute | solution.py:614
  122.2 0.7 copy-start.8
  133.5 15.9 %collective-permute-start.15 = (bf16[128,1152]{1,0:T(8,128)(2,1)}, bf16[128,1152]{1,0:T(8,128)(2,1)S(1)}, u32[]{:S(2)}, u32[]{:S(2)}) collective-permute-start(bf16[128,1152]{1,0:T(8,128)(2,1)} %get-tuple-element.87), channel_id=1, source_target_pairs={{0,3},{1,0},{2,1},{3,2},{4,7},{5,4},{6,5},{7,6},{8,11},{9,8},{10,9... | collective-permute-start | bytes 884744 | tf_op jit(solution)/shard_map/ppermute | solution.py:614
  136.8 12.6 %collective-permute-start.16 = (bf16[128,1152]{1,0:T(8,128)(2,1)}, bf16[128,1152]{1,0:T(8,128)(2,1)S(1)}, u32[]{:S(2)}, u32[]{:S(2)}) collective-permute-start(bf16[128,1152]{1,0:T(8,128)(2,1)} %get-tuple-element.88), channel_id=1, source_target_pairs={{0,2},{1,3},{2,0},{3,1},{4,6},{5,7},{6,4},{7,5},{8,10},{9,11},{10,... | collective-permute-start | bytes 884744 | tf_op jit(solution)/shard_map/ppermute | solution.py:614
  137.0 15.9 %copy-start.2 = (bf16[128,1152]{1,0:T(8,128)(2,1)}, bf16[128,1152]{1,0:T(8,128)(2,1)S(1)}, u32[]{:S(2)}) copy-start(bf16[128,1152]{1,0:T(8,128)(2,1)S(1)} %collective-permute-done.6.refs_1_) | copy-start | bytes 884740
  137.0 15.9 %collective-permute-start.17 = (bf16[128,1152]{1,0:T(8,128)(2,1)}, bf16[128,1152]{1,0:T(8,128)(2,1)S(1)}, u32[]{:S(2)}, u32[]{:S(2)}) collective-permute-start(bf16[128,1152]{1,0:T(8,128)(2,1)} %get-tuple-element.89), channel_id=1, source_target_pairs={{0,1},{1,2},{2,3},{3,0},{4,5},{5,6},{6,7},{7,4},{8,9},{9,10},{10,1... | collective-permute-start | bytes 884744 | tf_op jit(solution)/shard_map/ppermute | solution.py:614
  138.3 14.5 %copy-start.3 = (bf16[128,1152]{1,0:T(8,128)(2,1)}, bf16[128,1152]{1,0:T(8,128)(2,1)S(1)}, u32[]{:S(2)}) copy-start(bf16[128,1152]{1,0:T(8,128)(2,1)S(1)} %collective-permute-done.7.refs_2_) | copy-start | bytes 884740
  138.3 14.5 %copy-start.4 = (bf16[128,1152]{1,0:T(8,128)(2,1)}, bf16[128,1152]{1,0:T(8,128)(2,1)S(1)}, u32[]{:S(2)}) copy-start(bf16[128,1152]{1,0:T(8,128)(2,1)S(1)} %collective-permute-done.8.refs_3_) | copy-start | bytes 884740
  149.4 3.5 %copy-start.5 = (bf16[128,1152]{1,0:T(8,128)(2,1)}, bf16[128,1152]{1,0:T(8,128)(2,1)S(1)}, u32[]{:S(2)}) copy-start(bf16[128,1152]{1,0:T(8,128)(2,1)S(1)} %collective-permute-done.15.refs_5_) | copy-start | bytes 884740
  149.4 3.5 %copy-start.6 = (bf16[128,1152]{1,0:T(8,128)(2,1)}, bf16[128,1152]{1,0:T(8,128)(2,1)S(1)}, u32[]{:S(2)}) copy-start(bf16[128,1152]{1,0:T(8,128)(2,1)S(1)} %collective-permute-done.16.refs_6_) | copy-start | bytes 884740
  152.9 0.7 copy-start.7

commit v4 on v3

--- a/solution.py
+++ b/solution.py
@@ -18,7 +18,7 @@
 CHUNKS = 4
 GROUPS = ((0, 2), (2, 4))
 PAYLOAD = DK + DV + 16
-VMEM = 58 << 20
+VMEM = 64 << 20
 
 f32 = jnp.float32
 bf16 = jnp.bfloat16
@@ -150,15 +150,33 @@
     return lax.rem(me + CHUNKS - chunk, CHUNKS)
 
 
+def in_order(me, slots):
+    ordered = []
+    for chunk in range(CHUNKS):
+        found = slots[0]
+        for slot in range(1, CHUNKS):
+            found = jnp.where(lax.rem(me + CHUNKS - slot, CHUNKS) == chunk, slots[slot], found)
+        ordered.append(found)
+    return ordered
+
+
+def slot_of(me, chunk):
+    return lax.rem(me + CHUNKS - chunk, CHUNKS)
+
+
+def inputs_of(me, refs):
+    return [in_order(me, [r[...] for r in refs[n * CHUNKS : (n + 1) * CHUNKS]]) for n in range(5)]
+
+
 def local_kernel(base, me_ref, *refs):
     ins, outs = refs[: 5 * CHUNKS], refs[5 * CHUNKS :]
-    send_ref, w_ref, f_ref, t_ref, u_ref, d_ref, a_ref, l_ref, keep_ref = outs
+    send_ref, w_ref, f_ref, t_ref, u_ref, d_ref, a_ref, l_ref = outs
     me = me_ref[0]
     pair = base + pl.program_id(0)
     row, col = grids()
     before = row > col
     chunks = CHUNKS
-    qs, ks, vs, os, smalls = ([r[...] for r in ins[n * chunks : (n + 1) * chunks]] for n in range(5))
+    qs, ks, vs, os, smalls = inputs_of(me, ins)
     terms = chunk_terms(pickers(pair), qs, ks, smalls)
     cases = [(c, i) for c in range(chunks) for i in range(2)]
     gates = [terms[c]["heads"][i] for c, i in cases]
@@ -200,39 +218,40 @@
             )
         )
     for n, (c, i) in enumerate(cases):
-        w_ref[i, c] = key_part[n]
-        f_ref[i, c] = value_part[n]
-        t_ref[i, c] = low(solved[n])
-        u_ref[i, c] = fresh[n]
-        d_ref[i, c] = devs[n]
-        a_ref[i, c] = adds[n]
-        l_ref[i, c] = backs[n]
-        keep_ref[i, c] = jnp.broadcast_to(gates[n]["keep"], (8, DK))
-    first, last = slot_of(me, 0), slot_of(me, chunks - 1)
-    stacks = [jnp.concatenate([d_ref[i, first], a_ref[i, first]], axis=0) for i in range(2)]
-    keeps = [keep_ref[i, first][:1] for i in range(2)]
-    grads = [l_ref[i, last] for i in range(2)]
+        slot = slot_of(me, c)
+        w_ref[i, slot] = key_part[n]
+        f_ref[i, slot] = value_part[n]
+        t_ref[i, slot] = low(solved[n])
+        u_ref[i, slot] = fresh[n]
+        d_ref[i, slot] = devs[n]
+        a_ref[i, slot] = adds[n]
+        l_ref[i, slot] = backs[n]
+    at = lambda c, i: 2 * c + i
+    stacks = [jnp.concatenate([devs[i], adds[i]], axis=0) for i in range(2)]
+    keeps = [gates[i]["keep"] for i in range(2)]
+    grads = [backs[at(chunks - 1, i)] for i in range(2)]
     for step in range(1, chunks):
-        n, m = slot_of(me, step), slot_of(me, chunks - 1 - step)
-        ahead = [dot3(stacks[i], d_ref[i, n]) for i in range(2)]
-        behind = [dot3(grads[i], d_ref[i, m], NT) for i in range(2)]
+        back = chunks - 1 - step
+        ahead = [dot3(stacks[i], devs[at(step, i)]) for i in range(2)]
+        behind = [dot3(grads[i], devs[at(back, i)], NT) for i in range(2)]
         for i in range(2):
-            keep = keep_ref[i, n][:1]
+            n, m = at(step, i), at(back, i)
+            keep = gates[n]["keep"]
             stacks[i] = (
                 keep * stacks[i]
                 + ahead[i]
-                + jnp.concatenate([keeps[i] * d_ref[i, n], a_ref[i, n]], axis=0)
+                + jnp.concatenate([keeps[i] * devs[n], adds[n]], axis=0)
             )
             keeps[i] = keeps[i] * keep
-            grads[i] = keep_ref[i, m][:1] * grads[i] + behind[i] + l_ref[i, m]
+            grads[i] = gates[m]["keep"] * grads[i] + behind[i] + backs[m]
     for i in range(2):
-        dev, add = stacks[i][:DK], stacks[i][DK:]
         high, rest = split(keeps[i])
         middle, last = split(keeps[i] - high.astype(f32))
         line = lax.broadcasted_iota(jnp.int32, (16, DK), 0)
         scale = jnp.where(line == 2, last.astype(f32), 0.0)
         scale = jnp.where(line == 1, middle.astype(f32), scale)
         scale = low(jnp.where(line == 0, high.astype(f32), scale))
+        dev, add = stacks[i][:DK], stacks[i][DK:]
         for way, (step_map, addend) in enumerate(((dev, add), (dev.T, grads[i]))):
             send_ref[i, way, :DK] = low(step_map)
             send_ref[i, way, DK : DK + DV] = low(addend)
@@ -244,28 +263,26 @@
     return block[:DK], block[DK : DK + DV].astype(f32), scale
 
 
-def combine_kernel(where_ref, x_ref, out_ref):
+def combine_kernel(where_ref, x_ref, out_ref, before_ref):
     count = x_ref.shape[0]
     flip = where_ref[0]
+    stack = jnp.zeros((DK + DV, DK), f32)
+    keep = jnp.ones((1, DK), f32)
     for step in range(count):
         at = jnp.where(flip == 1, count - 1 - step, step)
+        before_ref[at, : DK + DV] = stack
+        before_ref[at, DK + DV :] = jnp.broadcast_to(keep, (8, DK))
         step_map, addend, scale = segment_parts(x_ref[at])
-        if step == 0:
-            stack = jnp.concatenate([step_map.astype(f32), addend], axis=0)
-            keep = scale
-        else:
-            stack = (
-                scale * stack
-                + dot(wide(stack, 1), twice(step_map, 0))
-                + jnp.concatenate([keep * step_map.astype(f32), addend], axis=0)
-            )
-            keep = keep * scale
+        new = jnp.concatenate([keep * step_map.astype(f32), addend], axis=0)
+        if step > 0:
+            new = new + scale * stack + dot(wide(stack, 1), twice(step_map, 0))
+        stack = new
+        keep = keep * scale
     out_ref[: DK + DV] = stack
     out_ref[DK + DV :] = jnp.broadcast_to(keep, (8, DK))
 
 
-def chain_kernel(where_ref, x_ref, one_ref, two_ref, three_ref, out_ref):
-    count = x_ref.shape[0]
+def chain_kernel(where_ref, before_ref, one_ref, two_ref, three_ref, out_ref):
     flip = where_ref[0]
     place = where_ref[1]
     rows = where_ref[2]
@@ -273,16 +290,14 @@
     for n, ahead, back in ((3, three_ref, one_ref), (2, two_ref, two_ref), (1, one_ref, three_ref)):
         block = jnp.where(flip == 1, back[...], ahead[...])
         there = jnp.where(flip == 1, place + n < rows, n <= place)
-        later = (
-            block[DK + DV : DK + DV + 1] * state + dot3(state, block[:DK]) + block[DK : DK + DV]
-        )
+        later = block[DK + DV : DK + DV + 1] * state + block[DK : DK + DV]
+        if n < 3:
+            later = later + dot3(state, block[:DK])
         state = jnp.where(there, later, state)
-    for step in range(count):
-        at = jnp.where(flip == 1, count - 1 - step, step)
-        out_ref[at] = low(state)
-        if step < count - 1:
-            step_map, addend, scale = segment_parts(x_ref[at])
-            state = state * scale + dot(wide(state, 1), twice(step_map, 0)) + addend
+    for step in range(before_ref.shape[0]):
+        keep = before_ref[step, DK + DV : DK + DV + 1]
+        met = dot3(state, before_ref[step, :DK])
+        out_ref[step] = low(keep * state + met + before_ref[step, DK : DK + DV])
 
 
 def final_kernel(base, me_ref, *refs):
@@ -542,7 +557,6 @@
             grid=(count,),
             in_specs=packed_specs(count, small_at),
             out_specs=[pl.BlockSpec((2, 2, PAYLOAD, DK), lambda p, me: (p, 0, 0, 0))] + SAVED_SPECS,
-            scratch_shapes=[pltpu.VMEM((2, CHUNKS, 8, DK), f32)],
         ),
         out_shape=[jax.ShapeDtypeStruct((2 * count, 2, PAYLOAD, DK), bf16)]
         + [jax.ShapeDtypeStruct((2 * count, CHUNKS, CHUNK, CHUNK), kind) for kind in SAVED],
@@ -554,36 +568,37 @@
 
 def combine_pass(place, received):
     shape = (DK + DV + 8, DK)
+    each = (received.shape[0],) + shape
     return pl.pallas_call(
         combine_kernel,
         grid_spec=pltpu.PrefetchScalarGridSpec(
             num_scalar_prefetch=1,
             grid=(1,),
             in_specs=[whole(received.shape)],
-            out_specs=whole(shape),
+            out_specs=[whole(shape), whole(each)],
         ),
-        out_shape=jax.ShapeDtypeStruct(shape, f32),
+        out_shape=[jax.ShapeDtypeStruct(shape, f32), jax.ShapeDtypeStruct(each, f32)],
         compiler_params=pltpu.CompilerParams(vmem_limit_bytes=VMEM),
         cost_estimate=cost(1, 1_500_000_000),
         name="combine_pass",
     )(place, received)
 
 
-def chain_pass(place, received, others):
-    shape = (received.shape[0], DV, DK)
+def chain_pass(place, before, others):
+    shape = (before.shape[0], DV, DK)
     return pl.pallas_call(
         chain_kernel,
         grid_spec=pltpu.PrefetchScalarGridSpec(
             num_scalar_prefetch=1,
             grid=(1,),
-            in_specs=[whole(received.shape)] + [whole(x.shape) for x in others],
+            in_specs=[whole(before.shape)] + [whole(x.shape) for x in others],
             out_specs=whole(shape),
         ),
         out_shape=jax.ShapeDtypeStruct(shape, bf16),
         compiler_params=pltpu.CompilerParams(vmem_limit_bytes=VMEM),
         cost_estimate=cost(1, 1_500_000_000),
         name="chain_pass",
-    )(place, received, *others)
+    )(place, before, *others)
 
 
 def final_pass(me, packed, small, small_at, saved, states, begin, end):
@@ -623,7 +638,7 @@
     received = lax.all_to_all(
         sends, "ctx", split_axis=0, concat_axis=0, axis_index_groups=near, tiled=True
     )
-    combined = combine_pass(place, received)
+    combined, before = combine_pass(place, received)
     others = [
         lax.ppermute(
             combined, "ctx", [(i, (i + s * HEADS) % segments) for i in range(segments)]
@@ -631,7 +646,7 @@
         for s in range(1, rows)
     ]
     return lax.all_to_all(
-        chain_pass(place, received, others),
+        chain_pass(place, before, others),
         "ctx",
         split_axis=0,
         concat_axis=0,
@@ -651,7 +666,7 @@
     for b, e in GROUPS:
         slots = pack(me, arrays, gates if b == 0 else [], b, e)
         if received:
-            slots, received[-1] = lax.optimization_barrier((slots, received[-1]))
+            slots, received[-1], place = lax.optimization_barrier((slots, received[-1], place))
         received.append(turned(slots, 1))
     small = received[0]
     small_at = small[0].shape[1] // 128 - 1

time: 159 us -> 153 us (0.962)
  local copies, waits for them, and re-layouts: 8.03 us -> 0 us
  waiting for transfers between devices: 34.9 us -> 37 us
    unnamed x44 -> x0, local copies, waits for them, and re-layouts: 8.03 us -> none
    all_to_all x2, waiting for transfers between devices: 2.22 us -> 4.16 us  [recursion(): lax.all_to_all(chain_pass(place, before, others), 'ctx', split_axis=0, co...]
  transfers between devices with their start and end apart: 22 -> 22, of which waited for: 6 -> 7; matrix products, arithmetic and copies ran while one was open for 0% -> 0% of each run, Pallas kernels for 41% -> 41%
where the time goes in v4:
time: 153 us; the launch traced here: 150 us
  Pallas kernels  68.1 us (45%)
  starting transfers between devices  44.1 us (29%)
  waiting for transfers between devices  37 us (24%)
    ppermute x12, waiting for transfers between devices, turned(): lax.ppermute(slots[s], 'head', [(i, (i + way * s) % count) for i in range...  29.4 us
    pallas_call x2, Pallas kernels, local_pass(): pl.pallas_call(functools.partial(local_kernel, begin), grid_spec=pltpu.Pr...  24.3 us
    pallas_call x2, Pallas kernels, final_pass(): pl.pallas_call(functools.partial(final_kernel, begin), grid_spec=pltpu.Pr...  21.3 us
    ppermute x12, starting transfers between devices, turned(): lax.ppermute(slots[s], 'head', [(i, (i + way * s) % count) for i in range...  19.1 us
    all_to_all x2, starting transfers between devices, recursion(): lax.all_to_all(sends, 'ctx', split_axis=0, concat_axis=0, axis_index_grou...  9.12 us
    all_to_all x2, starting transfers between devices, recursion(): lax.all_to_all(chain_pass(place, before, others), 'ctx', split_axis=0, co...  8.09 us
    ppermute x6, starting transfers between devices, recursion(): lax.ppermute(combined, 'ctx', [(i, (i + s * HEADS) % segments) for i in r...  7.73 us
    pallas_call x2, Pallas kernels, combine_pass(): pl.pallas_call(combine_kernel, grid_spec=pltpu.PrefetchScalarGridSpec(num...  7.21 us
  transfers between devices with their start and end apart: 22, of which 7 were waited for; matrix products, arithmetic and copies ran while one was open for 0% of the time, Pallas kernels for 41%

profile of v4, /device:TPU:24, one launch (start us, length us, event | category | flops | bytes accessed | tf_op | source)
XLA Modules:
  0.0 150.4 jit_solution(6768814465642216094)
XLA Ops:
  0.6 2.9 %pack.3 = (bf16[128,1664]{1,0:T(8,128)(2,1)}, bf16[128,1664]{1,0:T(8,128)(2,1)}, bf16[128,1664]{1,0:T(8,128)(2,1)}, bf16[128,1664]{1,0:T(8,128)(2,1)}) custom-call(s32[1]{0:T(128)} %bitcast.me_ref, bf16[128,2048]{1,0:T(8,128)(2,1)} %refs_12_.3, bf16[128,2048]{1,0:T(8,128)(2,1)} %refs_13_.3, bf16[128,4096]{1,0:T(8,128)(2,1)} %refs_14_.3, ...), custom_call_target="tpu_custom_call" | custom-call | tf_op jit(solution)/shard_map/pack/pallas_call | solution.py:472
  3.5 1.9 %collective-permute-start = (bf16[128,1664]{1,0:T(8,128)(2,1)}, bf16[128,1664]{1,0:T(8,128)(2,1)}, u32[]{:S(2)}, u32[]{:S(2)}) collective-permute-start(bf16[128,1664]{1,0:T(8,128)(2,1)} %get-tuple-element.60), channel_id=1, source_target_pairs={{0,1},{1,2},{2,3},{3,0},{4,5},{5,6},{6,7},{7,4},{8,9},{9,10},{10,1... | collective-permute-start | bytes 1277960 | tf_op jit(solution)/shard_map/ppermute | solution.py:629
  5.5 3.6 %collective-permute-start.1 = (bf16[128,1664]{1,0:T(8,128)(2,1)}, bf16[128,1664]{1,0:T(8,128)(2,1)}, u32[]{:S(2)}, u32[]{:S(2)}) collective-permute-start(bf16[128,1664]{1,0:T(8,128)(2,1)} %get-tuple-element.61), channel_id=1, source_target_pairs={{0,2},{1,3},{2,0},{3,1},{4,6},{5,7},{6,4},{7,5},{8,10},{9,11},{10,... | collective-permute-start | bytes 1277960 | tf_op jit(solution)/shard_map/ppermute | solution.py:629
  9.0 1.0 collective-permute-start.2
  10.1 2.7 %pack.2 = (bf16[128,1536]{1,0:T(8,128)(2,1)}, bf16[128,1536]{1,0:T(8,128)(2,1)}, bf16[128,1536]{1,0:T(8,128)(2,1)}, bf16[128,1536]{1,0:T(8,128)(2,1)}) custom-call(s32[1]{0:T(128)} %bitcast.me_ref, bf16[128,2048]{1,0:T(8,128)(2,1)} %refs_12_.3, bf16[128,2048]{1,0:T(8,128)(2,1)} %refs_13_.3, bf16[128,4096]{1,0:T(8,128)(2,1)} %refs_14_.3, ...), custom_call_target="tpu_custom_call" | custom-call | tf_op jit(solution)/shard_map/pack/pallas_call | solution.py:472
  12.7 0.6 pad_add_fusion.where_ref
  13.3 4.4 %collective-permute-done.refs_1_.refs_5_.refs_9_.refs_13_.refs_17_ = bf16[128,1664]{1,0:T(8,128)(2,1)} collective-permute-done((bf16[128,1664]{1,0:T(8,128)(2,1)}, bf16[128,1664]{1,0:T(8,128)(2,1)}, u32[]{:S(2)}, u32[]{:S(2)}) %collective-permute-start) | collective-permute-done | bytes 426016 | tf_op jit(solution)/shard_map/ppermute | solution.py:629
  17.7 10.3 %collective-permute-done.1.refs_2_.refs_6_.refs_10_.refs_14_.refs_18_ = bf16[128,1664]{1,0:T(8,128)(2,1)} collective-permute-done((bf16[128,1664]{1,0:T(8,128)(2,1)}, bf16[128,1664]{1,0:T(8,128)(2,1)}, u32[]{:S(2)}, u32[]{:S(2)}) %collective-permute-start.1) | collective-permute-done | bytes 426016 | tf_op jit(solution)/shard_map/ppermute | solution.py:629
  28.0 0.0 collective-permute-done.2.refs_3_.refs_7_.refs_11_.refs_15_.refs_19_
  28.0 1.2 collective-permute-start.9
  29.2 2.4 %collective-permute-start.10 = (bf16[128,1536]{1,0:T(8,128)(2,1)}, bf16[128,1536]{1,0:T(8,128)(2,1)}, u32[]{:S(2)}, u32[]{:S(2)}) collective-permute-start(bf16[128,1536]{1,0:T(8,128)(2,1)} %get-tuple-element.84), channel_id=1, source_target_pairs={{0,2},{1,3},{2,0},{3,1},{4,6},{5,7},{6,4},{7,5},{8,10},{9,11},{10,... | collective-permute-start | bytes 1179656 | tf_op jit(solution)/shard_map/ppermute | solution.py:629
  31.6 1.2 collective-permute-start.11
  32.9 12.2 %local_pass.2 = (bf16[4,2,272,128]{3,2,1,0:T(8,128)(2,1)}, f32[4,4,128,128]{3,2,1,0:T(8,128)}, f32[4,4,128,128]{3,2,1,0:T(8,128)}, bf16[4,4,128,128]{3,2,1,0:T(8...) custom-call(s32[1]{0:T(128)} %bitcast.me_ref, ...), custom_call_target="tpu_custom_call" | custom-call | flops 8000000000 | bytes 10000000 | tf_op jit(solution)/shard_map/local_pass/pallas_call | solution.py:553
  45.1 4.3 %all-to-all-start = ((bf16[8,272,128]{2,1,0:T(8,128)(2,1)}), bf16[8,272,128]{2,1,0:T(8,128)(2,1)}, u32[]{:S(2)}, u32[]{:S(2)}) async-start(bf16[8,272,128]{2,1,0:T(8,128)(2,1)} %bitcast.11), calls=%async_computation | async-start | bytes 1114112 | tf_op jit(solution)/shard_map/all_to_all | solution.py:638
  49.4 0.0 collective-permute-done.9.refs_1_.refs_5_.refs_9_.refs_13_
  49.4 0.0 collective-permute-done.10.refs_2_.refs_6_.refs_10_.refs_14_
  49.4 0.0 collective-permute-done.11.refs_3_.refs_7_.refs_11_.refs_15_
  49.4 12.2 %local_pass.3 = (bf16[4,2,272,128]{3,2,1,0:T(8,128)(2,1)}, f32[4,4,128,128]{3,2,1,0:T(8,128)}, f32[4,4,128,128]{3,2,1,0:T(8,128)}, bf16[4,4,128,128]{3,2,1,0:T(8...) custom-call(s32[1]{0:T(128)} %bitcast.me_ref, ...), custom_call_target="tpu_custom_call" | custom-call | flops 8000000000 | bytes 10000000 | tf_op jit(solution)/shard_map/local_pass/pallas_call | solution.py:553
  61.6 0.0 all-to-all-done.x_ref
  61.6 4.8 %all-to-all-start.2 = ((bf16[8,272,128]{2,1,0:T(8,128)(2,1)}), bf16[8,272,128]{2,1,0:T(8,128)(2,1)}, u32[]{:S(2)}, u32[]{:S(2)}) async-start(bf16[8,272,128]{2,1,0:T(8,128)(2,1)} %bitcast.12), calls=%async_computation.2 | async-start | bytes 1114112 | tf_op jit(solution)/shard_map/all_to_all | solution.py:638
  66.4 3.6 %combine_pass.2 = (f32[264,128]{1,0:T(8,128)}, f32[8,264,128]{2,1,0:T(8,128)}) custom-call(s32[3]{0:T(128)} %pad_add_fusion.where_ref, bf16[8,272,128]{2,1,0:T(8,128)(2,1)} %all-to-all-done.x_ref), custom_call_target="tpu_custom_call" | custom-call | flops 1500000000 | bytes 5000000 | tf_op jit(solution)/shard_map/combine_pass/pallas_call | solution.py:572
  70.0 0.7 collective-permute-start.5
  70.7 0.9 collective-permute-start.4
  71.7 2.2 %collective-permute-start.3 = (f32[264,128]{1,0:T(8,128)}, f32[264,128]{1,0:T(8,128)}, u32[]{:S(2)}, u32[]{:S(2)}) collective-permute-start(f32[264,128]{1,0:T(8,128)} %get-tuple-element.77), channel_id=1, source_target_pairs={{0,32},{4,36},{8,40},{12,44},{16,48},{20,52},{24,56},{28,60},{32,6... | collective-permute-start | bytes 405512 | tf_op jit(solution)/shard_map/ppermute | solution.py:643
  73.8 3.3 %all-to-all-done.2.x_ref = bf16[8,272,128]{2,1,0:T(8,128)(2,1)} async-done(((bf16[8,272,128]{2,1,0:T(8,128)(2,1)}), bf16[8,272,128]{2,1,0:T(8,128)(2,1)}, u32[]{:S(2)}, u32[]{:S(2)}) %all-to-all-start.2) | async-done | bytes 557088 | tf_op jit(solution)/shard_map/all_to_all | solution.py:638
  77.2 3.6 %combine_pass.3 = (f32[264,128]{1,0:T(8,128)}, f32[8,264,128]{2,1,0:T(8,128)}) custom-call(s32[3]{0:T(128)} %pad_add_fusion.where_ref, bf16[8,272,128]{2,1,0:T(8,128)(2,1)} %all-to-all-done.2.x_ref), custom_call_target="tpu_custom_call" | custom-call | flops 1500000000 | bytes 5000000 | tf_op jit(solution)/shard_map/combine_pass/pallas_call | solution.py:572
  80.8 0.7 collective-permute-start.14
  81.5 0.9 collective-permute-start.13
  82.5 0.0 collective-permute-done.5.three_ref
  82.5 2.2 %collective-permute-start.12 = (f32[264,128]{1,0:T(8,128)}, f32[264,128]{1,0:T(8,128)}, u32[]{:S(2)}, u32[]{:S(2)}) collective-permute-start(f32[264,128]{1,0:T(8,128)} %get-tuple-element.95), channel_id=1, source_target_pairs={{0,32},{4,36},{8,40},{12,44},{16,48},{20,52},{24,56},{28,60},{32,6... | collective-permute-start | bytes 405512 | tf_op jit(solution)/shard_map/ppermute | solution.py:643
  84.7 0.0 collective-permute-done.4.two_ref
  84.7 0.0 collective-permute-done.3.one_ref
  84.7 3.3 %chain_pass.2 = bf16[8,128,128]{2,1,0:T(8,128)(2,1)} custom-call(s32[3]{0:T(128)} %pad_add_fusion.where_ref, f32[8,264,128]{2,1,0:T(8,128)} %get-tuple-element.76.before_ref, f32[264,128]{1,0:T(8,128)} %collective-permute-done.3.one_ref, f32[264,128]{1,0:T(8,128)} %collective-permute-done.4.two_ref, f32[264,128]{1,0:T(8,128)} %collective-permute-done.5.three_ref), custom_call_target="tpu_custom_call" | custom-call | flops 1500000000 | bytes 5000000 | tf_op jit(solution)/shard_map/chain_pass/pallas_call | solution.py:589
  88.0 4.1 %all-to-all-start.1 = ((bf16[8,128,128]{2,1,0:T(8,128)(2,1)}), bf16[8,128,128]{2,1,0:T(8,128)(2,1)}, u32[]{:S(2)}, u32[]{:S(2)}) async-start(bf16[8,128,128]{2,1,0:T(8,128)(2,1)} %chain_pass.2), calls=%async_computation.1 | async-start | bytes 524288 | tf_op jit(solution)/shard_map/all_to_all | solution.py:648
  92.1 0.0 collective-permute-done.14.three_ref
  92.1 0.0 collective-permute-done.13.two_ref
  92.1 0.0 collective-permute-done.12.one_ref
  92.1 3.3 %chain_pass.3 = bf16[8,128,128]{2,1,0:T(8,128)(2,1)} custom-call(s32[3]{0:T(128)} %pad_add_fusion.where_ref, f32[8,264,128]{2,1,0:T(8,128)} %get-tuple-element.94.before_ref, f32[264,128]{1,0:T(8,128)} %collective-permute-done.12.one_ref, f32[264,128]{1,0:T(8,128)} %collective-permute-done.13.two_ref, f32[264,128]{1,0:T(8,128)} %collective-permute-done.14.three_ref), custom_call_target="tpu_custom_call" | custom-call | flops 1500000000 | bytes 5000000 | tf_op jit(solution)/shard_map/chain_pass/pallas_call | solution.py:589
  95.5 4.2 %all-to-all-done.1 = bf16[8,128,128]{2,1,0:T(8,128)(2,1)} async-done(((bf16[8,128,128]{2,1,0:T(8,128)(2,1)}), bf16[8,128,128]{2,1,0:T(8,128)(2,1)}, u32[]{:S(2)}, u32[]{:S(2)}) %all-to-all-start.1) | async-done | bytes 262176 | tf_op jit(solution)/shard_map/all_to_all | solution.py:648
  99.6 4.0 %all-to-all-start.3 = ((bf16[8,128,128]{2,1,0:T(8,128)(2,1)}), bf16[8,128,128]{2,1,0:T(8,128)(2,1)}, u32[]{:S(2)}, u32[]{:S(2)}) async-start(bf16[8,128,128]{2,1,0:T(8,128)(2,1)} %chain_pass.3), calls=%async_computation.3 | async-start | bytes 524288 | tf_op jit(solution)/shard_map/all_to_all | solution.py:648
  103.7 10.7 %final_pass.2 = (bf16[128,1152]{1,0:T(8,128)(2,1)}, bf16[128,1152]{1,0:T(8,128)(2,1)}, bf16[128,1152]{1,0:T(8,128)(2,1)}, bf16[128,1152]{1,0:T(8,128)(2,1)}) custom-call(s32[1]{0:T(128)} %bitcast.me_ref, bf16[128,1664]{1,0:T(8,128)(2,1)} %get-tuple-element.63.refs_0_.refs_4_.refs_8_.refs_12_.refs_16_, ...), custom_call_target="tpu_custom_call" | custom-call | flops 8000000000 | bytes 10000000 | tf_op jit(solution)/shard_map/final_pass/pallas_call | solution.py:608
  114.3 1.6 %collective-permute-start.6 = (bf16[128,1152]{1,0:T(8,128)(2,1)}, bf16[128,1152]{1,0:T(8,128)(2,1)}, u32[]{:S(2)}, u32[]{:S(2)}) collective-permute-start(bf16[128,1152]{1,0:T(8,128)(2,1)} %get-tuple-element.79), channel_id=1, source_target_pairs={{0,3},{1,0},{2,1},{3,2},{4,7},{5,4},{6,5},{7,6},{8,11},{9,8},{10,9... | collective-permute-start | bytes 884744 | tf_op jit(solution)/shard_map/ppermute | solution.py:629
  116.0 1.3 collective-permute-start.7
  117.3 0.0 collective-permute-start.8
  117.3 0.0 all-to-all-done.3
  117.3 10.6 %final_pass.3 = (bf16[128,1152]{1,0:T(8,128)(2,1)}, bf16[128,1152]{1,0:T(8,128)(2,1)}, bf16[128,1152]{1,0:T(8,128)(2,1)}, bf16[128,1152]{1,0:T(8,128)(2,1)}) custom-call(s32[1]{0:T(128)} %bitcast.me_ref, bf16[128,1536]{1,0:T(8,128)(2,1)} %get-tuple-element.82.refs_0_.refs_4_.refs_8_.refs_12_, ...), custom_call_target="tpu_custom_call" | custom-call | flops 8000000000 | bytes 10000000 | tf_op jit(solution)/shard_map/final_pass/pallas_call | solution.py:608
  127.9 3.3 %collective-permute-start.15 = (bf16[128,1152]{1,0:T(8,128)(2,1)}, bf16[128,1152]{1,0:T(8,128)(2,1)}, u32[]{:S(2)}, u32[]{:S(2)}) collective-permute-start(bf16[128,1152]{1,0:T(8,128)(2,1)} %get-tuple-element.97), channel_id=1, source_target_pairs={{0,3},{1,0},{2,1},{3,2},{4,7},{5,4},{6,5},{7,6},{8,11},{9,8},{10,9... | collective-permute-start | bytes 884744 | tf_op jit(solution)/shard_map/ppermute | solution.py:629
  131.2 1.0 collective-permute-start.16
  132.2 0.0 collective-permute-done.6.refs_1_
  132.2 0.5 collective-permute-start.17
  132.7 0.0 collective-permute-done.7.refs_2_
  132.7 0.4 collective-permute-done.8.refs_3_
  133.0 10.7 %collective-permute-done.15.refs_5_ = bf16[128,1152]{1,0:T(8,128)(2,1)} collective-permute-done((bf16[128,1152]{1,0:T(8,128)(2,1)}, bf16[128,1152]{1,0:T(8,128)(2,1)}, u32[]{:S(2)}, u32[]{:S(2)}) %collective-permute-start.15) | collective-permute-done | bytes 294944 | tf_op jit(solution)/shard_map/ppermute | solution.py:629
  143.7 0.0 collective-permute-done.16.refs_6_
  143.7 3.7 %collective-permute-done.17.refs_7_ = bf16[128,1152]{1,0:T(8,128)(2,1)} collective-permute-done((bf16[128,1152]{1,0:T(8,128)(2,1)}, bf16[128,1152]{1,0:T(8,128)(2,1)}, u32[]{:S(2)}, u32[]{:S(2)}) %collective-permute-start.17) | collective-permute-done | bytes 294944 | tf_op jit(solution)/shard_map/ppermute | solution.py:629
  147.4 3.0 %unpack.1 = (bf16[128,2048]{1,0:T(8,128)(2,1)}, bf16[128,2048]{1,0:T(8,128)(2,1)}, bf16[128,4096]{1,0:T(8,128)(2,1)}, bf16[32,128]{1,0:T(8,128)(2,1)}, bf16[32,128]{1,0:T(8,128)(2,1)}) custom-call(s32[1]{0:T(128)} %bitcast.me_ref, bf16[128,1152]{1,0:T(8,128)(2,1)} %get-tuple-element.78.refs_0_, bf16[128,1152]{1,0:T(8,128)(2,1)} %collective-permute-done.6.refs_1_, ...), custom_call_target="tpu_custom_call" | custom-call | tf_op jit(solution)/shard_map/unpack/pallas_call | solution.py:518
Async XLA Ops:
  3.5 14.2 %collective-permute-start = (bf16[128,1664]{1,0:T(8,128)(2,1)}, bf16[128,1664]{1,0:T(8,128)(2,1)}, u32[]{:S(2)}, u32[]{:S(2)}) collective-permute-start(bf16[128,1664]{1,0:T(8,128)(2,1)} %get-tuple-element.60), channel_id=1, source_target_pairs={{0,1},{1,2},{2,3},{3,0},{4,5},{5,6},{6,7},{7,4},{8,9},{9,10},{10,1... | collective-permute-start | bytes 1277960 | tf_op jit(solution)/shard_map/ppermute | solution.py:629
  5.5 22.6 %collective-permute-start.1 = (bf16[128,1664]{1,0:T(8,128)(2,1)}, bf16[128,1664]{1,0:T(8,128)(2,1)}, u32[]{:S(2)}, u32[]{:S(2)}) collective-permute-start(bf16[128,1664]{1,0:T(8,128)(2,1)} %get-tuple-element.61), channel_id=1, source_target_pairs={{0,2},{1,3},{2,0},{3,1},{4,6},{5,7},{6,4},{7,5},{8,10},{9,11},{10,... | collective-permute-start | bytes 1277960 | tf_op jit(solution)/shard_map/ppermute | solution.py:629
  9.0 19.0 %collective-permute-start.2 = (bf16[128,1664]{1,0:T(8,128)(2,1)}, bf16[128,1664]{1,0:T(8,128)(2,1)}, u32[]{:S(2)}, u32[]{:S(2)}) collective-permute-start(bf16[128,1664]{1,0:T(8,128)(2,1)} %get-tuple-element.62), channel_id=1, source_target_pairs={{0,3},{1,0},{2,1},{3,2},{4,7},{5,4},{6,5},{7,6},{8,11},{9,8},{10,9... | collective-permute-start | bytes 1277960 | tf_op jit(solution)/shard_map/ppermute | solution.py:629
  28.0 21.4 %collective-permute-start.9 = (bf16[128,1536]{1,0:T(8,128)(2,1)}, bf16[128,1536]{1,0:T(8,128)(2,1)}, u32[]{:S(2)}, u32[]{:S(2)}) collective-permute-start(bf16[128,1536]{1,0:T(8,128)(2,1)} %get-tuple-element.83), channel_id=1, source_target_pairs={{0,1},{1,2},{2,3},{3,0},{4,5},{5,6},{6,7},{7,4},{8,9},{9,10},{10,1... | collective-permute-start | bytes 1179656 | tf_op jit(solution)/shard_map/ppermute | solution.py:629
  29.2 20.1 %collective-permute-start.10 = (bf16[128,1536]{1,0:T(8,128)(2,1)}, bf16[128,1536]{1,0:T(8,128)(2,1)}, u32[]{:S(2)}, u32[]{:S(2)}) collective-permute-start(bf16[128,1536]{1,0:T(8,128)(2,1)} %get-tuple-element.84), channel_id=1, source_target_pairs={{0,2},{1,3},{2,0},{3,1},{4,6},{5,7},{6,4},{7,5},{8,10},{9,11},{10,... | collective-permute-start | bytes 1179656 | tf_op jit(solution)/shard_map/ppermute | solution.py:629
  31.6 17.8 %collective-permute-start.11 = (bf16[128,1536]{1,0:T(8,128)(2,1)}, bf16[128,1536]{1,0:T(8,128)(2,1)}, u32[]{:S(2)}, u32[]{:S(2)}) collective-permute-start(bf16[128,1536]{1,0:T(8,128)(2,1)} %get-tuple-element.85), channel_id=1, source_target_pairs={{0,3},{1,0},{2,1},{3,2},{4,7},{5,4},{6,5},{7,6},{8,11},{9,8},{10,9... | collective-permute-start | bytes 1179656 | tf_op jit(solution)/shard_map/ppermute | solution.py:629
  45.1 16.5 %all-to-all-start = ((bf16[8,272,128]{2,1,0:T(8,128)(2,1)}), bf16[8,272,128]{2,1,0:T(8,128)(2,1)}, u32[]{:S(2)}, u32[]{:S(2)}) async-start(bf16[8,272,128]{2,1,0:T(8,128)(2,1)} %bitcast.11), calls=%async_computation | async-start | bytes 1114112 | tf_op jit(solution)/shard_map/all_to_all | solution.py:638
  61.6 15.6 %all-to-all-start.2 = ((bf16[8,272,128]{2,1,0:T(8,128)(2,1)}), bf16[8,272,128]{2,1,0:T(8,128)(2,1)}, u32[]{:S(2)}, u32[]{:S(2)}) async-start(bf16[8,272,128]{2,1,0:T(8,128)(2,1)} %bitcast.12), calls=%async_computation.2 | async-start | bytes 1114112 | tf_op jit(solution)/shard_map/all_to_all | solution.py:638
  70.0 12.5 %collective-permute-start.5 = (f32[264,128]{1,0:T(8,128)}, f32[264,128]{1,0:T(8,128)}, u32[]{:S(2)}, u32[]{:S(2)}) collective-permute-start(f32[264,128]{1,0:T(8,128)} %get-tuple-element.77), channel_id=1, source_target_pairs={{0,96},{4,100},{8,104},{12,108},{16,112},{20,116},{24,120},{28,124... | collective-permute-start | bytes 405512 | tf_op jit(solution)/shard_map/ppermute | solution.py:643
  70.7 13.9 %collective-permute-start.4 = (f32[264,128]{1,0:T(8,128)}, f32[264,128]{1,0:T(8,128)}, u32[]{:S(2)}, u32[]{:S(2)}) collective-permute-start(f32[264,128]{1,0:T(8,128)} %get-tuple-element.77), channel_id=1, source_target_pairs={{0,64},{4,68},{8,72},{12,76},{16,80},{20,84},{24,88},{28,92},{32,9... | collective-permute-start | bytes 405512 | tf_op jit(solution)/shard_map/ppermute | solution.py:643
  71.7 13.0 %collective-permute-start.3 = (f32[264,128]{1,0:T(8,128)}, f32[264,128]{1,0:T(8,128)}, u32[]{:S(2)}, u32[]{:S(2)}) collective-permute-start(f32[264,128]{1,0:T(8,128)} %get-tuple-element.77), channel_id=1, source_target_pairs={{0,32},{4,36},{8,40},{12,44},{16,48},{20,52},{24,56},{28,60},{32,6... | collective-permute-start | bytes 405512 | tf_op jit(solution)/shard_map/ppermute | solution.py:643
  80.8 11.3 %collective-permute-start.14 = (f32[264,128]{1,0:T(8,128)}, f32[264,128]{1,0:T(8,128)}, u32[]{:S(2)}, u32[]{:S(2)}) collective-permute-start(f32[264,128]{1,0:T(8,128)} %get-tuple-element.95), channel_id=1, source_target_pairs={{0,96},{4,100},{8,104},{12,108},{16,112},{20,116},{24,120},{28,124... | collective-permute-start | bytes 405512 | tf_op jit(solution)/shard_map/ppermute | solution.py:643
  81.5 10.6 %collective-permute-start.13 = (f32[264,128]{1,0:T(8,128)}, f32[264,128]{1,0:T(8,128)}, u32[]{:S(2)}, u32[]{:S(2)}) collective-permute-start(f32[264,128]{1,0:T(8,128)} %get-tuple-element.95), channel_id=1, source_target_pairs={{0,64},{4,68},{8,72},{12,76},{16,80},{20,84},{24,88},{28,92},{32,9... | collective-permute-start | bytes 405512 | tf_op jit(solution)/shard_map/ppermute | solution.py:643
  82.5 9.6 %collective-permute-start.12 = (f32[264,128]{1,0:T(8,128)}, f32[264,128]{1,0:T(8,128)}, u32[]{:S(2)}, u32[]{:S(2)}) collective-permute-start(f32[264,128]{1,0:T(8,128)} %get-tuple-element.95), channel_id=1, source_target_pairs={{0,32},{4,36},{8,40},{12,44},{16,48},{20,52},{24,56},{28,60},{32,6... | collective-permute-start | bytes 405512 | tf_op jit(solution)/shard_map/ppermute | solution.py:643
  88.0 11.6 %all-to-all-start.1 = ((bf16[8,128,128]{2,1,0:T(8,128)(2,1)}), bf16[8,128,128]{2,1,0:T(8,128)(2,1)}, u32[]{:S(2)}, u32[]{:S(2)}) async-start(bf16[8,128,128]{2,1,0:T(8,128)(2,1)} %chain_pass.2), calls=%async_computation.1 | async-start | bytes 524288 | tf_op jit(solution)/shard_map/all_to_all | solution.py:648
  99.6 17.6 %all-to-all-start.3 = ((bf16[8,128,128]{2,1,0:T(8,128)(2,1)}), bf16[8,128,128]{2,1,0:T(8,128)(2,1)}, u32[]{:S(2)}, u32[]{:S(2)}) async-start(bf16[8,128,128]{2,1,0:T(8,128)(2,1)} %chain_pass.3), calls=%async_computation.3 | async-start | bytes 524288 | tf_op jit(solution)/shard_map/all_to_all | solution.py:648
  114.3 17.9 %collective-permute-start.6 = (bf16[128,1152]{1,0:T(8,128)(2,1)}, bf16[128,1152]{1,0:T(8,128)(2,1)}, u32[]{:S(2)}, u32[]{:S(2)}) collective-permute-start(bf16[128,1152]{1,0:T(8,128)(2,1)} %get-tuple-element.79), channel_id=1, source_target_pairs={{0,3},{1,0},{2,1},{3,2},{4,7},{5,4},{6,5},{7,6},{8,11},{9,8},{10,9... | collective-permute-start | bytes 884744 | tf_op jit(solution)/shard_map/ppermute | solution.py:629
  116.0 16.7 %collective-permute-start.7 = (bf16[128,1152]{1,0:T(8,128)(2,1)}, bf16[128,1152]{1,0:T(8,128)(2,1)}, u32[]{:S(2)}, u32[]{:S(2)}) collective-permute-start(bf16[128,1152]{1,0:T(8,128)(2,1)} %get-tuple-element.80), channel_id=1, source_target_pairs={{0,2},{1,3},{2,0},{3,1},{4,6},{5,7},{6,4},{7,5},{8,10},{9,11},{10,... | collective-permute-start | bytes 884744 | tf_op jit(solution)/shard_map/ppermute | solution.py:629
  117.3 15.8 %collective-permute-start.8 = (bf16[128,1152]{1,0:T(8,128)(2,1)}, bf16[128,1152]{1,0:T(8,128)(2,1)}, u32[]{:S(2)}, u32[]{:S(2)}) collective-permute-start(bf16[128,1152]{1,0:T(8,128)(2,1)} %get-tuple-element.81), channel_id=1, source_target_pairs={{0,1},{1,2},{2,3},{3,0},{4,5},{5,6},{6,7},{7,4},{8,9},{9,10},{10,1... | collective-permute-start | bytes 884744 | tf_op jit(solution)/shard_map/ppermute | solution.py:629
  127.9 15.9 %collective-permute-start.15 = (bf16[128,1152]{1,0:T(8,128)(2,1)}, bf16[128,1152]{1,0:T(8,128)(2,1)}, u32[]{:S(2)}, u32[]{:S(2)}) collective-permute-start(bf16[128,1152]{1,0:T(8,128)(2,1)} %get-tuple-element.97), channel_id=1, source_target_pairs={{0,3},{1,0},{2,1},{3,2},{4,7},{5,4},{6,5},{7,6},{8,11},{9,8},{10,9... | collective-permute-start | bytes 884744 | tf_op jit(solution)/shard_map/ppermute | solution.py:629
  131.2 12.6 %collective-permute-start.16 = (bf16[128,1152]{1,0:T(8,128)(2,1)}, bf16[128,1152]{1,0:T(8,128)(2,1)}, u32[]{:S(2)}, u32[]{:S(2)}) collective-permute-start(bf16[128,1152]{1,0:T(8,128)(2,1)} %get-tuple-element.98), channel_id=1, source_target_pairs={{0,2},{1,3},{2,0},{3,1},{4,6},{5,7},{6,4},{7,5},{8,10},{9,11},{10,... | collective-permute-start | bytes 884744 | tf_op jit(solution)/shard_map/ppermute | solution.py:629
  132.2 15.2 %collective-permute-start.17 = (bf16[128,1152]{1,0:T(8,128)(2,1)}, bf16[128,1152]{1,0:T(8,128)(2,1)}, u32[]{:S(2)}, u32[]{:S(2)}) collective-permute-start(bf16[128,1152]{1,0:T(8,128)(2,1)} %get-tuple-element.99), channel_id=1, source_target_pairs={{0,1},{1,2},{2,3},{3,0},{4,5},{5,6},{6,7},{7,4},{8,9},{9,10},{10,1... | collective-permute-start | bytes 884744 | tf_op jit(solution)/shard_map/ppermute | solution.py:629

commit v5 on v4

--- a/solution.py
+++ b/solution.py
@@ -17,6 +17,7 @@
 HEADS = 8
 CHUNKS = 4
 GROUPS = ((0, 2), (2, 4))
+
 PAYLOAD = DK + DV + 16
 VMEM = 64 << 20
 
@@ -27,27 +28,21 @@
 NT = (((1,), (1,)), ((), ()))
 TN = (((0,), (0,)), ((), ()))
 
-
 def dot(a, b, dims=NN):
     return lax.dot_general(a, b, dims, preferred_element_type=f32)
 
-
 def low(x):
     return x.astype(bf16)
-
 
 def split(x):
     high = x.astype(bf16)
     return high, (x - high.astype(f32)).astype(bf16)
 
-
 def twice(a, axis):
     return jnp.concatenate([a, a], axis=axis)
 
-
 def wide(x, axis):
     return jnp.concatenate(split(x), axis=axis)
-
 
 def dot3(a, b, dims=NN):
     (ca,), (cb,) = dims[0]
@@ -57,10 +52,8 @@
         jnp.concatenate([ah, al, ah], axis=ca), jnp.concatenate([bh, bh, bl], axis=cb), dims
     )
 
-
 def grids(shape=(CHUNK, CHUNK)):
     return lax.broadcasted_iota(jnp.int32, shape, 0), lax.broadcasted_iota(jnp.int32, shape, 1)
-
 
 def pickers(pair):
     row, col = grids((128, 4 * 128))
@@ -69,14 +62,11 @@
     lines = jnp.where(col == 2 * pair + (row // 8) % 2 + 8 * (row // 16), 1.0, 0.0)
     return low(spread), low(lines)
 
-
 def sigmoid(x):
     return 1.0 / (1.0 + jnp.exp(-x))
 
-
 def unit_scale(x):
     return lax.rsqrt(jnp.sum(x * x, axis=1, keepdims=True) + EPS)
-
 
 def chunk_terms(picks, qs, ks, smalls):
     row, col = grids()
@@ -128,13 +118,35 @@
         )
     return terms
 
+def block_inverses(systems):
+    size = 8
+    count = CHUNK // size
+    row, col = grids((size, CHUNK))
+    own = [col // size == r for r in range(count)]
+    packed = []
+    for a in systems:
+        rows = [jnp.where(own[r], a[r * size : (r + 1) * size], 0.0) for r in range(count)]
+        while len(rows) > 1:
+            rows = [x + y for x, y in zip(rows[::2], rows[1::2])]
+        packed.append(rows[0])
+    at, lane = grids((CHUNK, (size - 1) * CHUNK))
+    spread = low(jnp.where(at == (lane % CHUNK) // size * size + lane // CHUNK, 1.0, 0.0))
+    columns = dot(low(jnp.concatenate(packed, axis=0)), spread)
+    found = [jnp.where(row == col % size, 1.0, 0.0) for _ in systems]
+    for m in range(size - 1):
+        found = [
+            x - columns[n * size : (n + 1) * size, m * CHUNK : (m + 1) * CHUNK] * x[m : m + 1]
+            for n, x in enumerate(found)
+        ]
+    return [
+        jnp.concatenate([jnp.where(own[r], x, 0.0) for r in range(count)], axis=0) for x in found
+    ]
 
 def inverses(systems):
     row, col = grids()
     ident = jnp.where(row == col, 1.0, 0.0)
-    first = (row // 2 == col // 2) & (row > col)
-    found = [ident - jnp.where(first, a, 0.0) for a in systems]
-    size = 2
+    found = block_inverses(systems)
+    size = 8
     while size < CHUNK:
         merge = (row // (2 * size) == col // (2 * size)) & (row // size > col // size)
         parts = [low(jnp.where(merge, a, 0.0)) for a in systems]
@@ -145,10 +157,8 @@
     rests = [ident - t - dot3(a, t) for a, t in zip(systems, found)]
     return [t + dot(low(t), low(x)) for t, x in zip(found, rests)]
 
-
 def slot_of(me, chunk):
     return lax.rem(me + CHUNKS - chunk, CHUNKS)
-
 
 def in_order(me, slots):
     ordered = []
@@ -159,14 +169,11 @@
         ordered.append(found)
     return ordered
 
-
 def slot_of(me, chunk):
     return lax.rem(me + CHUNKS - chunk, CHUNKS)
 
-
 def inputs_of(me, refs):
     return [in_order(me, [r[...] for r in refs[n * CHUNKS : (n + 1) * CHUNKS]]) for n in range(5)]
-
 
 def local_kernel(base, me_ref, *refs):
     ins, outs = refs[: 5 * CHUNKS], refs[5 * CHUNKS :]
@@ -219,11 +226,11 @@
         )
     for n, (c, i) in enumerate(cases):
         slot = slot_of(me, c)
-        w_ref[i, slot] = key_part[n]
+        w_ref[i, slot] = low(key_part[n])
         f_ref[i, slot] = value_part[n]
         t_ref[i, slot] = low(solved[n])
         u_ref[i, slot] = fresh[n]
-        d_ref[i, slot] = devs[n]
+        d_ref[i, slot] = low(devs[n])
         a_ref[i, slot] = adds[n]
         l_ref[i, slot] = backs[n]
     at = lambda c, i: 2 * c + i
@@ -257,30 +264,40 @@
             send_ref[i, way, DK : DK + DV] = low(addend)
             send_ref[i, way, DK + DV :] = scale
 
-
 def segment_parts(block):
     scale = jnp.sum(block[DK + DV :].astype(f32), axis=0, keepdims=True)
     return block[:DK], block[DK : DK + DV].astype(f32), scale
 
-
 def combine_kernel(where_ref, x_ref, out_ref, before_ref):
     count = x_ref.shape[0]
     flip = where_ref[0]
-    stack = jnp.zeros((DK + DV, DK), f32)
-    keep = jnp.ones((1, DK), f32)
-    for step in range(count):
-        at = jnp.where(flip == 1, count - 1 - step, step)
-        before_ref[at, : DK + DV] = stack
-        before_ref[at, DK + DV :] = jnp.broadcast_to(keep, (8, DK))
-        step_map, addend, scale = segment_parts(x_ref[at])
-        new = jnp.concatenate([keep * step_map.astype(f32), addend], axis=0)
-        if step > 0:
-            new = new + scale * stack + dot(wide(stack, 1), twice(step_map, 0))
-        stack = new
-        keep = keep * scale
-    out_ref[: DK + DV] = stack
-    out_ref[DK + DV :] = jnp.broadcast_to(keep, (8, DK))
-
+    order = [jnp.where(flip == 1, count - 1 - step, step) for step in range(count)]
+    parts = [segment_parts(x_ref[at]) for at in order]
+    stacks = [jnp.concatenate([m.astype(f32), addend], axis=0) for m, addend, _ in parts]
+    keeps = [scale for _, _, scale in parts]
+    reach = 1
+    while reach < count:
+        joined = range(reach, count)
+        if reach == 1:
+            met = [dot(low(stacks[n - 1]), parts[n][0]) for n in joined]
+        else:
+            met = [dot3(stacks[n - reach], stacks[n][:DK]) for n in joined]
+        met = [
+            keeps[n] * stacks[n - reach]
+            + x
+            + jnp.concatenate([keeps[n - reach] * stacks[n][:DK], stacks[n][DK:]], axis=0)
+            for n, x in zip(joined, met)
+        ]
+        stacks = stacks[:reach] + met
+        keeps = keeps[:reach] + [keeps[n] * keeps[n - reach] for n in joined]
+        reach *= 2
+    stacks = [jnp.zeros_like(stacks[0])] + stacks
+    keeps = [jnp.ones_like(keeps[0])] + keeps
+    for step, at in enumerate(order):
+        before_ref[at, : DK + DV] = stacks[step]
+        before_ref[at, DK + DV :] = jnp.broadcast_to(keeps[step], (8, DK))
+    out_ref[: DK + DV] = stacks[count]
+    out_ref[DK + DV :] = jnp.broadcast_to(keeps[count], (8, DK))
 
 def chain_kernel(where_ref, before_ref, one_ref, two_ref, three_ref, out_ref):
     flip = where_ref[0]
@@ -298,7 +315,6 @@
         keep = before_ref[step, DK + DV : DK + DV + 1]
         met = dot3(state, before_ref[step, :DK])
         out_ref[step] = low(keep * state + met + before_ref[step, DK : DK + DV])
-
 
 def final_kernel(base, me_ref, *refs):
     ins, refs = refs[: 5 * CHUNKS], refs[5 * CHUNKS :]
@@ -327,9 +343,9 @@
         for i in range(2):
             state_ref[i, n] = states[i]
             grad_ref[i, m] = grads[i]
-        ahead = [dot3(states[i], d_ref[i, n]) for i in range(2)]
+        ahead = [dot(wide(states[i], 1), twice(d_ref[i, n], 0)) for i in range(2)]
         if step < chunks - 1:
-            behind = [dot3(grads[i], d_ref[i, m], NT) for i in range(2)]
+            behind = [dot(wide(grads[i], 1), twice(d_ref[i, m], 1), NT) for i in range(2)]
         for i in range(2):
             states[i] = keep_ref[i, n][:1] * states[i] + ahead[i] + a_ref[i, n]
             after_ref[i, n] = states[i]
@@ -340,7 +356,8 @@
     grad_of = [grad_ref[i, c] for c, i in cases]
 
     fresh = [
-        f_ref[i, c] - dot3(w_ref[i, c], state, NT) for (c, i), state in zip(cases, state_of)
+        f_ref[i, c] - dot(twice(w_ref[i, c], 1), wide(state, 1), NT)
+        for (c, i), state in zip(cases, state_of)
     ]
     fresh_grad = [
         u_ref[i, c]
@@ -432,7 +449,6 @@
         kept = jnp.where(here == 0, jnp.zeros_like(held), held)
         out_refs[c][:, place] = jnp.where(mine, low(small_out[c]), kept)
 
-
 def pack_kernel(me_ref, *refs):
     outs = refs[-CHUNKS:]
     for slot, out_ref in enumerate(outs):
@@ -452,7 +468,6 @@
             out_ref[:, at : at + 128] = low(
                 dot(d_ref[...], picks[0], TN) + dot(b_ref[...], picks[1], TN)
             )
-
 
 def pack(me, arrays, gates, begin, end):
     count = end - begin
@@ -482,7 +497,6 @@
         name="pack",
     )(me, *(list(arrays) * CHUNKS), *gates)
 
-
 def unpack_kernel(me_ref, *refs):
     arrived = refs[: len(GROUPS) * CHUNKS]
     q_ref, k_ref, v_ref, d_ref, b_ref = refs[len(GROUPS) * CHUNKS :]
@@ -506,10 +520,8 @@
     d_ref[...] = low(d_sum)
     b_ref[...] = low(b_sum)
 
-
 def whole(shape):
     return pl.BlockSpec(shape, lambda g, me: (0,) * len(shape))
-
 
 def unpack(me, groups):
     arrived = [x for group in groups for x in group]
@@ -529,24 +541,23 @@
     )(me, *arrived)
     return q, k, v, d.T, b.T
 
-
-def packed_specs(count, small_at):
+def packed_specs(count, small_at, off=0):
     return (
-        [pl.BlockSpec((CHUNK, DK), lambda p, me: (0, p))] * CHUNKS
-        + [pl.BlockSpec((CHUNK, DK), lambda p, me: (0, count + p))] * CHUNKS
-        + [pl.BlockSpec((CHUNK, 2 * DV), lambda p, me: (0, count + p))] * CHUNKS
-        + [pl.BlockSpec((CHUNK, 2 * DV), lambda p, me: (0, 2 * count + p))] * CHUNKS
+        [pl.BlockSpec((CHUNK, DK), lambda p, me: (0, off + p))] * CHUNKS
+        + [pl.BlockSpec((CHUNK, DK), lambda p, me: (0, count + off + p))] * CHUNKS
+        + [pl.BlockSpec((CHUNK, 2 * DV), lambda p, me: (0, count + off + p))] * CHUNKS
+        + [pl.BlockSpec((CHUNK, 2 * DV), lambda p, me: (0, 2 * count + off + p))] * CHUNKS
         + [pl.BlockSpec((CHUNK, 128), lambda p, me: (0, small_at))] * CHUNKS
     )
 
-
-SAVED = (f32, f32, bf16, f32, f32, f32, f32)
-SAVED_SPECS = [pl.BlockSpec((2, CHUNKS, CHUNK, CHUNK), lambda p, me: (p, 0, 0, 0)) for _ in SAVED]
-
+SAVED = (bf16, f32, bf16, f32, bf16, f32, f32)
+
+def saved_specs(off=0):
+    square = (2, CHUNKS, CHUNK, CHUNK)
+    return [pl.BlockSpec(square, lambda p, me: (off + p, 0, 0, 0)) for _ in SAVED]
 
 def cost(count, flops):
     return pl.CostEstimate(flops=count * flops, bytes_accessed=count * 5_000_000, transcendentals=0)
-
 
 def local_pass(me, packed, small, small_at, begin, end):
     count = end - begin
@@ -556,7 +567,7 @@
             num_scalar_prefetch=1,
             grid=(count,),
             in_specs=packed_specs(count, small_at),
-            out_specs=[pl.BlockSpec((2, 2, PAYLOAD, DK), lambda p, me: (p, 0, 0, 0))] + SAVED_SPECS,
+            out_specs=[pl.BlockSpec((2, 2, PAYLOAD, DK), lambda p, me: (p, 0, 0, 0))] + saved_specs(),
         ),
         out_shape=[jax.ShapeDtypeStruct((2 * count, 2, PAYLOAD, DK), bf16)]
         + [jax.ShapeDtypeStruct((2 * count, CHUNKS, CHUNK, CHUNK), kind) for kind in SAVED],
@@ -564,7 +575,6 @@
         cost_estimate=cost(count, 4_000_000_000),
         name="local_pass",
     )(me, *(list(packed) * 4), *small)
-
 
 def combine_pass(place, received):
     shape = (DK + DV + 8, DK)
@@ -583,7 +593,6 @@
         name="combine_pass",
     )(place, received)
 
-
 def chain_pass(place, before, others):
     shape = (before.shape[0], DV, DK)
     return pl.pallas_call(
@@ -600,9 +609,9 @@
         name="chain_pass",
     )(place, before, *others)
 
-
-def final_pass(me, packed, small, small_at, saved, states, begin, end):
+def final_pass(me, packed, small, small_at, saved, states, group, begin, end):
     count = end - begin
+    held, off = group[1] - group[0], begin - group[0]
     width = count * 2 * (DK + DV) + 128
     square = (2, CHUNKS, DV, DK)
     return pl.pallas_call(
@@ -610,9 +619,9 @@
         grid_spec=pltpu.PrefetchScalarGridSpec(
             num_scalar_prefetch=1,
             grid=(count,),
-            in_specs=packed_specs(count, small_at)
-            + SAVED_SPECS
-            + [pl.BlockSpec((2, 2, DV, DK), lambda p, me: (p, 0, 0, 0))],
+            in_specs=packed_specs(held, small_at, off)
+            + saved_specs(off)
+            + [pl.BlockSpec((2, 2, DV, DK), lambda p, me: (off + p, 0, 0, 0))],
             out_specs=[pl.BlockSpec((CHUNK, width), lambda p, me: (0, 0))] * CHUNKS,
             scratch_shapes=[pltpu.VMEM((2, CHUNKS, 8, DK), f32)] + [pltpu.VMEM(square, f32)] * 3,
         ),
@@ -622,14 +631,12 @@
         name="final_pass",
     )(me, *(list(packed) * 4), *small, *saved, states)
 
-
 def turned(slots, way):
     count = lax.axis_size("head")
     return [slots[0]] + [
         lax.ppermute(slots[s], "head", [(i, (i + way * s) % count) for i in range(count)])
         for s in range(1, count)
     ]
-
 
 def recursion(sends, place):
     segments = lax.axis_size("ctx")
@@ -653,7 +660,6 @@
         axis_index_groups=near,
         tiled=True,
     )
-
 
 def on_device(query_rows, key_rows, value_rows, log_decay, beta_logit, out_grad):
     arrays = [query_rows, key_rows, value_rows, out_grad]
@@ -676,10 +682,13 @@
         saved.append(kept)
         found = recursion(sends.reshape(HEADS, PAYLOAD, DK), place)
         states.append(found.reshape(2 * (e - b), 2, DV, DK))
-    for (b, e), packed, kept, state in zip(GROUPS, received, saved, states):
-        outs.append(turned(final_pass(me, packed, small, small_at, kept, state, b, e), -1))
+    for b, e in GROUPS:
+        n = [g for g, (first, last) in enumerate(GROUPS) if first <= b < last][0]
+        grads = final_pass(
+            me, received[n], small, small_at, saved[n], states[n], GROUPS[n], b, e
+        )
+        outs.append(turned(grads, -1))
     return unpack(me, outs)
-
 
 def solution(mesh):
     spec = P(("ctx", "head"), None)

time: 153 us -> 151 us (0.987)
  Pallas kernels: 68.1 us -> 65.6 us
    pallas_call x2, Pallas kernels: 24.3 us -> 22.7 us  [local_pass(): pl.pallas_call(functools.partial(local_kernel, begin), grid_spec=pltpu.Pr...]
  transfers between devices with their start and end apart: 22 -> 22, of which waited for: 7 -> 8; matrix products, arithmetic and copies ran while one was open for 0% -> 0% of each run, Pallas kernels for 41% -> 40%
where the time goes in v5:
time: 151 us; the launch traced here: 148 us
  Pallas kernels  65.6 us (43%)
  starting transfers between devices  43.7 us (29%)
  waiting for transfers between devices  37.4 us (25%)
    ppermute x12, waiting for transfers between devices, turned(): lax.ppermute(slots[s], 'head', [(i, (i + way * s) % count) for i in range...  30.2 us
    pallas_call x2, Pallas kernels, local_pass(): pl.pallas_call(functools.partial(local_kernel, begin), grid_spec=pltpu.Pr...  22.7 us
    pallas_call x2, Pallas kernels, final_pass(): pl.pallas_call(functools.partial(final_kernel, begin), grid_spec=pltpu.Pr...  20 us
    ppermute x12, starting transfers between devices, turned(): lax.ppermute(slots[s], 'head', [(i, (i + way * s) % count) for i in range...  19.1 us
    all_to_all x2, starting transfers between devices, recursion(): lax.all_to_all(sends, 'ctx', split_axis=0, concat_axis=0, axis_index_grou...  8.71 us
    all_to_all x2, starting transfers between devices, recursion(): lax.all_to_all(chain_pass(place, before, others), 'ctx', split_axis=0, co...  8.08 us
    ppermute x6, starting transfers between devices, recursion(): lax.ppermute(combined, 'ctx', [(i, (i + s * HEADS) % segments) for i in r...  7.73 us
    pallas_call x2, Pallas kernels, combine_pass(): pl.pallas_call(combine_kernel, grid_spec=pltpu.PrefetchScalarGridSpec(num...  7.53 us
  transfers between devices with their start and end apart: 22, of which 8 were waited for; matrix products, arithmetic and copies ran while one was open for 0% of the time, Pallas kernels for 40%

profile of v5, /device:TPU:24, one launch (start us, length us, event | category | flops | bytes accessed | tf_op | source)
XLA Modules:
  0.0 148.0 jit_solution(6338539932944883886)
XLA Ops:
  0.6 2.9 %pack.3 = (bf16[128,1664]{1,0:T(8,128)(2,1)}, bf16[128,1664]{1,0:T(8,128)(2,1)}, bf16[128,1664]{1,0:T(8,128)(2,1)}, bf16[128,1664]{1,0:T(8,128)(2,1)}) custom-call(s32[1]{0:T(128)} %bitcast.me_ref, bf16[128,2048]{1,0:T(8,128)(2,1)} %refs_12_.3, bf16[128,2048]{1,0:T(8,128)(2,1)} %refs_13_.3, bf16[128,4096]{1,0:T(8,128)(2,1)} %refs_14_.3, ...), custom_call_target="tpu_custom_call" | custom-call | tf_op jit(solution)/shard_map/pack/pallas_call | solution.py:487
  3.5 1.9 %collective-permute-start = (bf16[128,1664]{1,0:T(8,128)(2,1)}, bf16[128,1664]{1,0:T(8,128)(2,1)}, u32[]{:S(2)}, u32[]{:S(2)}) collective-permute-start(bf16[128,1664]{1,0:T(8,128)(2,1)} %get-tuple-element.60), channel_id=1, source_target_pairs={{0,1},{1,2},{2,3},{3,0},{4,5},{5,6},{6,7},{7,4},{8,9},{9,10},{10,1... | collective-permute-start | bytes 1277960 | tf_op jit(solution)/shard_map/ppermute | solution.py:637
  5.5 3.6 %collective-permute-start.1 = (bf16[128,1664]{1,0:T(8,128)(2,1)}, bf16[128,1664]{1,0:T(8,128)(2,1)}, u32[]{:S(2)}, u32[]{:S(2)}) collective-permute-start(bf16[128,1664]{1,0:T(8,128)(2,1)} %get-tuple-element.61), channel_id=1, source_target_pairs={{0,2},{1,3},{2,0},{3,1},{4,6},{5,7},{6,4},{7,5},{8,10},{9,11},{10,... | collective-permute-start | bytes 1277960 | tf_op jit(solution)/shard_map/ppermute | solution.py:637
  9.0 1.0 collective-permute-start.2
  10.1 2.7 %pack.2 = (bf16[128,1536]{1,0:T(8,128)(2,1)}, bf16[128,1536]{1,0:T(8,128)(2,1)}, bf16[128,1536]{1,0:T(8,128)(2,1)}, bf16[128,1536]{1,0:T(8,128)(2,1)}) custom-call(s32[1]{0:T(128)} %bitcast.me_ref, bf16[128,2048]{1,0:T(8,128)(2,1)} %refs_12_.3, bf16[128,2048]{1,0:T(8,128)(2,1)} %refs_13_.3, bf16[128,4096]{1,0:T(8,128)(2,1)} %refs_14_.3, ...), custom_call_target="tpu_custom_call" | custom-call | tf_op jit(solution)/shard_map/pack/pallas_call | solution.py:487
  12.7 0.6 pad_add_fusion.where_ref
  13.3 4.4 %collective-permute-done.refs_1_.refs_5_.refs_9_.refs_13_.refs_17_ = bf16[128,1664]{1,0:T(8,128)(2,1)} collective-permute-done((bf16[128,1664]{1,0:T(8,128)(2,1)}, bf16[128,1664]{1,0:T(8,128)(2,1)}, u32[]{:S(2)}, u32[]{:S(2)}) %collective-permute-start) | collective-permute-done | bytes 426016 | tf_op jit(solution)/shard_map/ppermute | solution.py:637
  17.7 10.3 %collective-permute-done.1.refs_2_.refs_6_.refs_10_.refs_14_.refs_18_ = bf16[128,1664]{1,0:T(8,128)(2,1)} collective-permute-done((bf16[128,1664]{1,0:T(8,128)(2,1)}, bf16[128,1664]{1,0:T(8,128)(2,1)}, u32[]{:S(2)}, u32[]{:S(2)}) %collective-permute-start.1) | collective-permute-done | bytes 426016 | tf_op jit(solution)/shard_map/ppermute | solution.py:637
  28.0 0.0 collective-permute-done.2.refs_3_.refs_7_.refs_11_.refs_15_.refs_19_
  28.0 1.2 collective-permute-start.9
  29.2 2.4 %collective-permute-start.10 = (bf16[128,1536]{1,0:T(8,128)(2,1)}, bf16[128,1536]{1,0:T(8,128)(2,1)}, u32[]{:S(2)}, u32[]{:S(2)}) collective-permute-start(bf16[128,1536]{1,0:T(8,128)(2,1)} %get-tuple-element.84), channel_id=1, source_target_pairs={{0,2},{1,3},{2,0},{3,1},{4,6},{5,7},{6,4},{7,5},{8,10},{9,11},{10,... | collective-permute-start | bytes 1179656 | tf_op jit(solution)/shard_map/ppermute | solution.py:637
  31.6 1.2 collective-permute-start.11
  32.9 11.4 %local_pass.2 = (bf16[4,2,272,128]{3,2,1,0:T(8,128)(2,1)}, bf16[4,4,128,128]{3,2,1,0:T(8,128)(2,1)}, f32[4,4,128,128]{3,2,1,0:T(8,128)}, bf16[4,4,128,128]{3,2,1...) custom-call(s32[1]{0:T(128)} %bitcast.me_ref, ...), custom_call_target="tpu_custom_call" | custom-call | flops 8000000000 | bytes 10000000 | tf_op jit(solution)/shard_map/local_pass/pallas_call | solution.py:564
  44.3 4.3 %all-to-all-start = ((bf16[8,272,128]{2,1,0:T(8,128)(2,1)}), bf16[8,272,128]{2,1,0:T(8,128)(2,1)}, u32[]{:S(2)}, u32[]{:S(2)}) async-start(bf16[8,272,128]{2,1,0:T(8,128)(2,1)} %bitcast.11), calls=%async_computation | async-start | bytes 1114112 | tf_op jit(solution)/shard_map/all_to_all | solution.py:645
  48.6 0.0 collective-permute-done.9.refs_1_.refs_5_.refs_9_.refs_13_
  48.6 0.8 collective-permute-done.10.refs_2_.refs_6_.refs_10_.refs_14_
  49.4 0.0 collective-permute-done.11.refs_3_.refs_7_.refs_11_.refs_15_
  49.4 11.4 %local_pass.3 = (bf16[4,2,272,128]{3,2,1,0:T(8,128)(2,1)}, bf16[4,4,128,128]{3,2,1,0:T(8,128)(2,1)}, f32[4,4,128,128]{3,2,1,0:T(8,128)}, bf16[4,4,128,128]{3,2,1...) custom-call(s32[1]{0:T(128)} %bitcast.me_ref, ...), custom_call_target="tpu_custom_call" | custom-call | flops 8000000000 | bytes 10000000 | tf_op jit(solution)/shard_map/local_pass/pallas_call | solution.py:564
  60.8 0.0 all-to-all-done.x_ref
  60.8 4.4 %all-to-all-start.2 = ((bf16[8,272,128]{2,1,0:T(8,128)(2,1)}), bf16[8,272,128]{2,1,0:T(8,128)(2,1)}, u32[]{:S(2)}, u32[]{:S(2)}) async-start(bf16[8,272,128]{2,1,0:T(8,128)(2,1)} %bitcast.12), calls=%async_computation.2 | async-start | bytes 1114112 | tf_op jit(solution)/shard_map/all_to_all | solution.py:645
  65.2 3.8 %combine_pass.2 = (f32[264,128]{1,0:T(8,128)}, f32[8,264,128]{2,1,0:T(8,128)}) custom-call(s32[3]{0:T(128)} %pad_add_fusion.where_ref, bf16[8,272,128]{2,1,0:T(8,128)(2,1)} %all-to-all-done.x_ref), custom_call_target="tpu_custom_call" | custom-call | flops 1500000000 | bytes 5000000 | tf_op jit(solution)/shard_map/combine_pass/pallas_call | solution.py:582
  69.0 0.7 collective-permute-start.5
  69.7 0.9 collective-permute-start.4
  70.6 2.2 %collective-permute-start.3 = (f32[264,128]{1,0:T(8,128)}, f32[264,128]{1,0:T(8,128)}, u32[]{:S(2)}, u32[]{:S(2)}) collective-permute-start(f32[264,128]{1,0:T(8,128)} %get-tuple-element.77), channel_id=1, source_target_pairs={{0,32},{4,36},{8,40},{12,44},{16,48},{20,52},{24,56},{28,60},{32,6... | collective-permute-start | bytes 405512 | tf_op jit(solution)/shard_map/ppermute | solution.py:650
  72.8 3.1 %all-to-all-done.2.x_ref = bf16[8,272,128]{2,1,0:T(8,128)(2,1)} async-done(((bf16[8,272,128]{2,1,0:T(8,128)(2,1)}), bf16[8,272,128]{2,1,0:T(8,128)(2,1)}, u32[]{:S(2)}, u32[]{:S(2)}) %all-to-all-start.2) | async-done | bytes 557088 | tf_op jit(solution)/shard_map/all_to_all | solution.py:645
  75.9 3.8 %combine_pass.3 = (f32[264,128]{1,0:T(8,128)}, f32[8,264,128]{2,1,0:T(8,128)}) custom-call(s32[3]{0:T(128)} %pad_add_fusion.where_ref, bf16[8,272,128]{2,1,0:T(8,128)(2,1)} %all-to-all-done.2.x_ref), custom_call_target="tpu_custom_call" | custom-call | flops 1500000000 | bytes 5000000 | tf_op jit(solution)/shard_map/combine_pass/pallas_call | solution.py:582
  79.7 0.7 collective-permute-start.14
  80.4 0.9 collective-permute-start.13
  81.4 0.0 collective-permute-done.5.three_ref
  81.4 2.2 %collective-permute-start.12 = (f32[264,128]{1,0:T(8,128)}, f32[264,128]{1,0:T(8,128)}, u32[]{:S(2)}, u32[]{:S(2)}) collective-permute-start(f32[264,128]{1,0:T(8,128)} %get-tuple-element.95), channel_id=1, source_target_pairs={{0,32},{4,36},{8,40},{12,44},{16,48},{20,52},{24,56},{28,60},{32,6... | collective-permute-start | bytes 405512 | tf_op jit(solution)/shard_map/ppermute | solution.py:650
  83.5 0.0 collective-permute-done.4.two_ref
  83.5 0.0 collective-permute-done.3.one_ref
  83.5 3.4 %chain_pass.2 = bf16[8,128,128]{2,1,0:T(8,128)(2,1)} custom-call(s32[3]{0:T(128)} %pad_add_fusion.where_ref, f32[8,264,128]{2,1,0:T(8,128)} %get-tuple-element.76.before_ref, f32[264,128]{1,0:T(8,128)} %collective-permute-done.3.one_ref, f32[264,128]{1,0:T(8,128)} %collective-permute-done.4.two_ref, f32[264,128]{1,0:T(8,128)} %collective-permute-done.5.three_ref), custom_call_target="tpu_custom_call" | custom-call | flops 1500000000 | bytes 5000000 | tf_op jit(solution)/shard_map/chain_pass/pallas_call | solution.py:598
  86.9 4.0 %all-to-all-start.1 = ((bf16[8,128,128]{2,1,0:T(8,128)(2,1)}), bf16[8,128,128]{2,1,0:T(8,128)(2,1)}, u32[]{:S(2)}, u32[]{:S(2)}) async-start(bf16[8,128,128]{2,1,0:T(8,128)(2,1)} %chain_pass.2), calls=%async_computation.1 | async-start | bytes 524288 | tf_op jit(solution)/shard_map/all_to_all | solution.py:655
  91.0 0.0 collective-permute-done.14.three_ref
  91.0 0.0 collective-permute-done.13.two_ref
  91.0 0.0 collective-permute-done.12.one_ref
  91.0 3.4 %chain_pass.3 = bf16[8,128,128]{2,1,0:T(8,128)(2,1)} custom-call(s32[3]{0:T(128)} %pad_add_fusion.where_ref, f32[8,264,128]{2,1,0:T(8,128)} %get-tuple-element.94.before_ref, f32[264,128]{1,0:T(8,128)} %collective-permute-done.12.one_ref, f32[264,128]{1,0:T(8,128)} %collective-permute-done.13.two_ref, f32[264,128]{1,0:T(8,128)} %collective-permute-done.14.three_ref), custom_call_target="tpu_custom_call" | custom-call | flops 1500000000 | bytes 5000000 | tf_op jit(solution)/shard_map/chain_pass/pallas_call | solution.py:598
  94.3 4.2 %all-to-all-done.1 = bf16[8,128,128]{2,1,0:T(8,128)(2,1)} async-done(((bf16[8,128,128]{2,1,0:T(8,128)(2,1)}), bf16[8,128,128]{2,1,0:T(8,128)(2,1)}, u32[]{:S(2)}, u32[]{:S(2)}) %all-to-all-start.1) | async-done | bytes 262176 | tf_op jit(solution)/shard_map/all_to_all | solution.py:655
  98.5 4.0 %all-to-all-start.3 = ((bf16[8,128,128]{2,1,0:T(8,128)(2,1)}), bf16[8,128,128]{2,1,0:T(8,128)(2,1)}, u32[]{:S(2)}, u32[]{:S(2)}) async-start(bf16[8,128,128]{2,1,0:T(8,128)(2,1)} %chain_pass.3), calls=%async_computation.3 | async-start | bytes 524288 | tf_op jit(solution)/shard_map/all_to_all | solution.py:655
  102.5 10.1 %final_pass.2 = (bf16[128,1152]{1,0:T(8,128)(2,1)}, bf16[128,1152]{1,0:T(8,128)(2,1)}, bf16[128,1152]{1,0:T(8,128)(2,1)}, bf16[128,1152]{1,0:T(8,128)(2,1)}) custom-call(s32[1]{0:T(128)} %bitcast.me_ref, bf16[128,1664]{1,0:T(8,128)(2,1)} %get-tuple-element.63.refs_0_.refs_4_.refs_8_.refs_12_.refs_16_, ...), custom_call_target="tpu_custom_call" | custom-call | flops 8000000000 | bytes 10000000 | tf_op jit(solution)/shard_map/final_pass/pallas_call | solution.py:617
  112.6 2.2 %collective-permute-start.6 = (bf16[128,1152]{1,0:T(8,128)(2,1)}, bf16[128,1152]{1,0:T(8,128)(2,1)}, u32[]{:S(2)}, u32[]{:S(2)}) collective-permute-start(bf16[128,1152]{1,0:T(8,128)(2,1)} %get-tuple-element.79), channel_id=1, source_target_pairs={{0,3},{1,0},{2,1},{3,2},{4,7},{5,4},{6,5},{7,6},{8,11},{9,8},{10,9... | collective-permute-start | bytes 884744 | tf_op jit(solution)/shard_map/ppermute | solution.py:637
  114.8 0.7 collective-permute-start.7
  115.5 0.2 collective-permute-start.8
  115.7 0.0 all-to-all-done.3
  115.7 9.9 %final_pass.3 = (bf16[128,1152]{1,0:T(8,128)(2,1)}, bf16[128,1152]{1,0:T(8,128)(2,1)}, bf16[128,1152]{1,0:T(8,128)(2,1)}, bf16[128,1152]{1,0:T(8,128)(2,1)}) custom-call(s32[1]{0:T(128)} %bitcast.me_ref, bf16[128,1536]{1,0:T(8,128)(2,1)} %get-tuple-element.82.refs_0_.refs_4_.refs_8_.refs_12_, ...), custom_call_target="tpu_custom_call" | custom-call | flops 8000000000 | bytes 10000000 | tf_op jit(solution)/shard_map/final_pass/pallas_call | solution.py:617
  125.7 3.1 %collective-permute-start.15 = (bf16[128,1152]{1,0:T(8,128)(2,1)}, bf16[128,1152]{1,0:T(8,128)(2,1)}, u32[]{:S(2)}, u32[]{:S(2)}) collective-permute-start(bf16[128,1152]{1,0:T(8,128)(2,1)} %get-tuple-element.97), channel_id=1, source_target_pairs={{0,3},{1,0},{2,1},{3,2},{4,7},{5,4},{6,5},{7,6},{8,11},{9,8},{10,9... | collective-permute-start | bytes 884744 | tf_op jit(solution)/shard_map/ppermute | solution.py:637
  128.8 1.6 %collective-permute-start.16 = (bf16[128,1152]{1,0:T(8,128)(2,1)}, bf16[128,1152]{1,0:T(8,128)(2,1)}, u32[]{:S(2)}, u32[]{:S(2)}) collective-permute-start(bf16[128,1152]{1,0:T(8,128)(2,1)} %get-tuple-element.98), channel_id=1, source_target_pairs={{0,2},{1,3},{2,0},{3,1},{4,6},{5,7},{6,4},{7,5},{8,10},{9,11},{10,... | collective-permute-start | bytes 884744 | tf_op jit(solution)/shard_map/ppermute | solution.py:637
  130.3 0.0 collective-permute-done.6.refs_1_
  130.3 0.0 collective-permute-start.17
  130.3 0.0 collective-permute-done.7.refs_2_
  130.3 1.5 %collective-permute-done.8.refs_3_ = bf16[128,1152]{1,0:T(8,128)(2,1)} collective-permute-done((bf16[128,1152]{1,0:T(8,128)(2,1)}, bf16[128,1152]{1,0:T(8,128)(2,1)}, u32[]{:S(2)}, u32[]{:S(2)}) %collective-permute-start.8) | collective-permute-done | bytes 294944 | tf_op jit(solution)/shard_map/ppermute | solution.py:637
  131.8 9.5 %collective-permute-done.15.refs_5_ = bf16[128,1152]{1,0:T(8,128)(2,1)} collective-permute-done((bf16[128,1152]{1,0:T(8,128)(2,1)}, bf16[128,1152]{1,0:T(8,128)(2,1)}, u32[]{:S(2)}, u32[]{:S(2)}) %collective-permute-start.15) | collective-permute-done | bytes 294944 | tf_op jit(solution)/shard_map/ppermute | solution.py:637
  141.3 0.0 collective-permute-done.16.refs_6_
  141.3 3.7 %collective-permute-done.17.refs_7_ = bf16[128,1152]{1,0:T(8,128)(2,1)} collective-permute-done((bf16[128,1152]{1,0:T(8,128)(2,1)}, bf16[128,1152]{1,0:T(8,128)(2,1)}, u32[]{:S(2)}, u32[]{:S(2)}) %collective-permute-start.17) | collective-permute-done | bytes 294944 | tf_op jit(solution)/shard_map/ppermute | solution.py:637
  145.0 3.0 %unpack.1 = (bf16[128,2048]{1,0:T(8,128)(2,1)}, bf16[128,2048]{1,0:T(8,128)(2,1)}, bf16[128,4096]{1,0:T(8,128)(2,1)}, bf16[32,128]{1,0:T(8,128)(2,1)}, bf16[32,128]{1,0:T(8,128)(2,1)}) custom-call(s32[1]{0:T(128)} %bitcast.me_ref, bf16[128,1152]{1,0:T(8,128)(2,1)} %get-tuple-element.78.refs_0_, bf16[128,1152]{1,0:T(8,128)(2,1)} %collective-permute-done.6.refs_1_, ...), custom_call_target="tpu_custom_call" | custom-call | tf_op jit(solution)/shard_map/unpack/pallas_call | solution.py:530
Async XLA Ops:
  3.5 14.2 %collective-permute-start = (bf16[128,1664]{1,0:T(8,128)(2,1)}, bf16[128,1664]{1,0:T(8,128)(2,1)}, u32[]{:S(2)}, u32[]{:S(2)}) collective-permute-start(bf16[128,1664]{1,0:T(8,128)(2,1)} %get-tuple-element.60), channel_id=1, source_target_pairs={{0,1},{1,2},{2,3},{3,0},{4,5},{5,6},{6,7},{7,4},{8,9},{9,10},{10,1... | collective-permute-start | bytes 1277960 | tf_op jit(solution)/shard_map/ppermute | solution.py:637
  5.5 22.6 %collective-permute-start.1 = (bf16[128,1664]{1,0:T(8,128)(2,1)}, bf16[128,1664]{1,0:T(8,128)(2,1)}, u32[]{:S(2)}, u32[]{:S(2)}) collective-permute-start(bf16[128,1664]{1,0:T(8,128)(2,1)} %get-tuple-element.61), channel_id=1, source_target_pairs={{0,2},{1,3},{2,0},{3,1},{4,6},{5,7},{6,4},{7,5},{8,10},{9,11},{10,... | collective-permute-start | bytes 1277960 | tf_op jit(solution)/shard_map/ppermute | solution.py:637
  9.0 19.0 %collective-permute-start.2 = (bf16[128,1664]{1,0:T(8,128)(2,1)}, bf16[128,1664]{1,0:T(8,128)(2,1)}, u32[]{:S(2)}, u32[]{:S(2)}) collective-permute-start(bf16[128,1664]{1,0:T(8,128)(2,1)} %get-tuple-element.62), channel_id=1, source_target_pairs={{0,3},{1,0},{2,1},{3,2},{4,7},{5,4},{6,5},{7,6},{8,11},{9,8},{10,9... | collective-permute-start | bytes 1277960 | tf_op jit(solution)/shard_map/ppermute | solution.py:637
  28.0 20.6 %collective-permute-start.9 = (bf16[128,1536]{1,0:T(8,128)(2,1)}, bf16[128,1536]{1,0:T(8,128)(2,1)}, u32[]{:S(2)}, u32[]{:S(2)}) collective-permute-start(bf16[128,1536]{1,0:T(8,128)(2,1)} %get-tuple-element.83), channel_id=1, source_target_pairs={{0,1},{1,2},{2,3},{3,0},{4,5},{5,6},{6,7},{7,4},{8,9},{9,10},{10,1... | collective-permute-start | bytes 1179656 | tf_op jit(solution)/shard_map/ppermute | solution.py:637
  29.2 20.1 %collective-permute-start.10 = (bf16[128,1536]{1,0:T(8,128)(2,1)}, bf16[128,1536]{1,0:T(8,128)(2,1)}, u32[]{:S(2)}, u32[]{:S(2)}) collective-permute-start(bf16[128,1536]{1,0:T(8,128)(2,1)} %get-tuple-element.84), channel_id=1, source_target_pairs={{0,2},{1,3},{2,0},{3,1},{4,6},{5,7},{6,4},{7,5},{8,10},{9,11},{10,... | collective-permute-start | bytes 1179656 | tf_op jit(solution)/shard_map/ppermute | solution.py:637
  31.6 17.8 %collective-permute-start.11 = (bf16[128,1536]{1,0:T(8,128)(2,1)}, bf16[128,1536]{1,0:T(8,128)(2,1)}, u32[]{:S(2)}, u32[]{:S(2)}) collective-permute-start(bf16[128,1536]{1,0:T(8,128)(2,1)} %get-tuple-element.85), channel_id=1, source_target_pairs={{0,3},{1,0},{2,1},{3,2},{4,7},{5,4},{6,5},{7,6},{8,11},{9,8},{10,9... | collective-permute-start | bytes 1179656 | tf_op jit(solution)/shard_map/ppermute | solution.py:637
  44.3 16.5 %all-to-all-start = ((bf16[8,272,128]{2,1,0:T(8,128)(2,1)}), bf16[8,272,128]{2,1,0:T(8,128)(2,1)}, u32[]{:S(2)}, u32[]{:S(2)}) async-start(bf16[8,272,128]{2,1,0:T(8,128)(2,1)} %bitcast.11), calls=%async_computation | async-start | bytes 1114112 | tf_op jit(solution)/shard_map/all_to_all | solution.py:645
  60.8 15.1 %all-to-all-start.2 = ((bf16[8,272,128]{2,1,0:T(8,128)(2,1)}), bf16[8,272,128]{2,1,0:T(8,128)(2,1)}, u32[]{:S(2)}, u32[]{:S(2)}) async-start(bf16[8,272,128]{2,1,0:T(8,128)(2,1)} %bitcast.12), calls=%async_computation.2 | async-start | bytes 1114112 | tf_op jit(solution)/shard_map/all_to_all | solution.py:645
  69.0 12.4 %collective-permute-start.5 = (f32[264,128]{1,0:T(8,128)}, f32[264,128]{1,0:T(8,128)}, u32[]{:S(2)}, u32[]{:S(2)}) collective-permute-start(f32[264,128]{1,0:T(8,128)} %get-tuple-element.77), channel_id=1, source_target_pairs={{0,96},{4,100},{8,104},{12,108},{16,112},{20,116},{24,120},{28,124... | collective-permute-start | bytes 405512 | tf_op jit(solution)/shard_map/ppermute | solution.py:650
  69.7 13.8 %collective-permute-start.4 = (f32[264,128]{1,0:T(8,128)}, f32[264,128]{1,0:T(8,128)}, u32[]{:S(2)}, u32[]{:S(2)}) collective-permute-start(f32[264,128]{1,0:T(8,128)} %get-tuple-element.77), channel_id=1, source_target_pairs={{0,64},{4,68},{8,72},{12,76},{16,80},{20,84},{24,88},{28,92},{32,9... | collective-permute-start | bytes 405512 | tf_op jit(solution)/shard_map/ppermute | solution.py:650
  70.6 12.9 %collective-permute-start.3 = (f32[264,128]{1,0:T(8,128)}, f32[264,128]{1,0:T(8,128)}, u32[]{:S(2)}, u32[]{:S(2)}) collective-permute-start(f32[264,128]{1,0:T(8,128)} %get-tuple-element.77), channel_id=1, source_target_pairs={{0,32},{4,36},{8,40},{12,44},{16,48},{20,52},{24,56},{28,60},{32,6... | collective-permute-start | bytes 405512 | tf_op jit(solution)/shard_map/ppermute | solution.py:650
  79.7 11.3 %collective-permute-start.14 = (f32[264,128]{1,0:T(8,128)}, f32[264,128]{1,0:T(8,128)}, u32[]{:S(2)}, u32[]{:S(2)}) collective-permute-start(f32[264,128]{1,0:T(8,128)} %get-tuple-element.95), channel_id=1, source_target_pairs={{0,96},{4,100},{8,104},{12,108},{16,112},{20,116},{24,120},{28,124... | collective-permute-start | bytes 405512 | tf_op jit(solution)/shard_map/ppermute | solution.py:650
  80.4 10.6 %collective-permute-start.13 = (f32[264,128]{1,0:T(8,128)}, f32[264,128]{1,0:T(8,128)}, u32[]{:S(2)}, u32[]{:S(2)}) collective-permute-start(f32[264,128]{1,0:T(8,128)} %get-tuple-element.95), channel_id=1, source_target_pairs={{0,64},{4,68},{8,72},{12,76},{16,80},{20,84},{24,88},{28,92},{32,9... | collective-permute-start | bytes 405512 | tf_op jit(solution)/shard_map/ppermute | solution.py:650
  81.4 9.6 %collective-permute-start.12 = (f32[264,128]{1,0:T(8,128)}, f32[264,128]{1,0:T(8,128)}, u32[]{:S(2)}, u32[]{:S(2)}) collective-permute-start(f32[264,128]{1,0:T(8,128)} %get-tuple-element.95), channel_id=1, source_target_pairs={{0,32},{4,36},{8,40},{12,44},{16,48},{20,52},{24,56},{28,60},{32,6... | collective-permute-start | bytes 405512 | tf_op jit(solution)/shard_map/ppermute | solution.py:650
  86.9 11.6 %all-to-all-start.1 = ((bf16[8,128,128]{2,1,0:T(8,128)(2,1)}), bf16[8,128,128]{2,1,0:T(8,128)(2,1)}, u32[]{:S(2)}, u32[]{:S(2)}) async-start(bf16[8,128,128]{2,1,0:T(8,128)(2,1)} %chain_pass.2), calls=%async_computation.1 | async-start | bytes 524288 | tf_op jit(solution)/shard_map/all_to_all | solution.py:655
  98.5 17.2 %all-to-all-start.3 = ((bf16[8,128,128]{2,1,0:T(8,128)(2,1)}), bf16[8,128,128]{2,1,0:T(8,128)(2,1)}, u32[]{:S(2)}, u32[]{:S(2)}) async-start(bf16[8,128,128]{2,1,0:T(8,128)(2,1)} %chain_pass.3), calls=%async_computation.3 | async-start | bytes 524288 | tf_op jit(solution)/shard_map/all_to_all | solution.py:655
  112.6 17.7 %collective-permute-start.6 = (bf16[128,1152]{1,0:T(8,128)(2,1)}, bf16[128,1152]{1,0:T(8,128)(2,1)}, u32[]{:S(2)}, u32[]{:S(2)}) collective-permute-start(bf16[128,1152]{1,0:T(8,128)(2,1)} %get-tuple-element.79), channel_id=1, source_target_pairs={{0,3},{1,0},{2,1},{3,2},{4,7},{5,4},{6,5},{7,6},{8,11},{9,8},{10,9... | collective-permute-start | bytes 884744 | tf_op jit(solution)/shard_map/ppermute | solution.py:637
  114.8 15.6 %collective-permute-start.7 = (bf16[128,1152]{1,0:T(8,128)(2,1)}, bf16[128,1152]{1,0:T(8,128)(2,1)}, u32[]{:S(2)}, u32[]{:S(2)}) collective-permute-start(bf16[128,1152]{1,0:T(8,128)(2,1)} %get-tuple-element.80), channel_id=1, source_target_pairs={{0,2},{1,3},{2,0},{3,1},{4,6},{5,7},{6,4},{7,5},{8,10},{9,11},{10,... | collective-permute-start | bytes 884744 | tf_op jit(solution)/shard_map/ppermute | solution.py:637
  115.5 16.4 %collective-permute-start.8 = (bf16[128,1152]{1,0:T(8,128)(2,1)}, bf16[128,1152]{1,0:T(8,128)(2,1)}, u32[]{:S(2)}, u32[]{:S(2)}) collective-permute-start(bf16[128,1152]{1,0:T(8,128)(2,1)} %get-tuple-element.81), channel_id=1, source_target_pairs={{0,1},{1,2},{2,3},{3,0},{4,5},{5,6},{6,7},{7,4},{8,9},{9,10},{10,1... | collective-permute-start | bytes 884744 | tf_op jit(solution)/shard_map/ppermute | solution.py:637
  125.7 15.7 %collective-permute-start.15 = (bf16[128,1152]{1,0:T(8,128)(2,1)}, bf16[128,1152]{1,0:T(8,128)(2,1)}, u32[]{:S(2)}, u32[]{:S(2)}) collective-permute-start(bf16[128,1152]{1,0:T(8,128)(2,1)} %get-tuple-element.97), channel_id=1, source_target_pairs={{0,3},{1,0},{2,1},{3,2},{4,7},{5,4},{6,5},{7,6},{8,11},{9,8},{10,9... | collective-permute-start | bytes 884744 | tf_op jit(solution)/shard_map/ppermute | solution.py:637
  128.8 12.6 %collective-permute-start.16 = (bf16[128,1152]{1,0:T(8,128)(2,1)}, bf16[128,1152]{1,0:T(8,128)(2,1)}, u32[]{:S(2)}, u32[]{:S(2)}) collective-permute-start(bf16[128,1152]{1,0:T(8,128)(2,1)} %get-tuple-element.98), channel_id=1, source_target_pairs={{0,2},{1,3},{2,0},{3,1},{4,6},{5,7},{6,4},{7,5},{8,10},{9,11},{10,... | collective-permute-start | bytes 884744 | tf_op jit(solution)/shard_map/ppermute | solution.py:637
  130.3 14.7 %collective-permute-start.17 = (bf16[128,1152]{1,0:T(8,128)(2,1)}, bf16[128,1152]{1,0:T(8,128)(2,1)}, u32[]{:S(2)}, u32[]{:S(2)}) collective-permute-start(bf16[128,1152]{1,0:T(8,128)(2,1)} %get-tuple-element.99), channel_id=1, source_target_pairs={{0,1},{1,2},{2,3},{3,0},{4,5},{5,6},{6,7},{7,4},{8,9},{9,10},{10,1... | collective-permute-start | bytes 884744 | tf_op jit(solution)/shard_map/ppermute | solution.py:637

commit v6 on v5

--- a/solution.py
+++ b/solution.py
@@ -228,7 +228,7 @@
         slot = slot_of(me, c)
         w_ref[i, slot] = low(key_part[n])
         f_ref[i, slot] = value_part[n]
-        t_ref[i, slot] = low(solved[n])
+        t_ref[i, slot] = solved[n]
         u_ref[i, slot] = fresh[n]
         d_ref[i, slot] = low(devs[n])
         a_ref[i, slot] = adds[n]
@@ -365,7 +365,7 @@
         for (c, i), h, grad in zip(cases, gates, grad_of)
     ]
     solved = [
-        dot(twice(t_ref[i, c], 0), wide(x, 0), TN) for (c, i), x in zip(cases, fresh_grad)
+        dot3(t_ref[i, c], x, TN) for (c, i), x in zip(cases, fresh_grad)
     ]
     value_grad = [h["beta_col"] * x for h, x in zip(gates, solved)]
     quarter = (out_refs[0].shape[1] - 128) // 4
@@ -550,7 +550,7 @@
         + [pl.BlockSpec((CHUNK, 128), lambda p, me: (0, small_at))] * CHUNKS
     )
 
-SAVED = (bf16, f32, bf16, f32, bf16, f32, f32)
+SAVED = (bf16, f32, f32, f32, bf16, f32, f32)
 
 def saved_specs(off=0):
     square = (2, CHUNKS, CHUNK, CHUNK)

time: 151 us -> 151 us (level)
  no operation moved by 1% of the time
where the time goes in v6:
time: 151 us; the launch traced here: 148 us
  Pallas kernels  65.8 us (44%)
  starting transfers between devices  43.7 us (29%)
  waiting for transfers between devices  37.5 us (25%)
    ppermute x12, waiting for transfers between devices, turned(): lax.ppermute(slots[s], 'head', [(i, (i + way * s) % count) for i in range...  30.2 us
    pallas_call x2, Pallas kernels, local_pass(): pl.pallas_call(functools.partial(local_kernel, begin), grid_spec=pltpu.Pr...  22.6 us
    pallas_call x2, Pallas kernels, final_pass(): pl.pallas_call(functools.partial(final_kernel, begin), grid_spec=pltpu.Pr...  20.4 us
    ppermute x12, starting transfers between devices, turned(): lax.ppermute(slots[s], 'head', [(i, (i + way * s) % count) for i in range...  19.2 us
    all_to_all x2, starting transfers between devices, recursion(): lax.all_to_all(sends, 'ctx', split_axis=0, concat_axis=0, axis_index_grou...  8.7 us
    all_to_all x2, starting transfers between devices, recursion(): lax.all_to_all(chain_pass(place, before, others), 'ctx', split_axis=0, co...  8.08 us
    ppermute x6, starting transfers between devices, recursion(): lax.ppermute(combined, 'ctx', [(i, (i + s * HEADS) % segments) for i in r...  7.73 us
    pallas_call x2, Pallas kernels, combine_pass(): pl.pallas_call(combine_kernel, grid_spec=pltpu.PrefetchScalarGridSpec(num...  7.46 us
  transfers between devices with their start and end apart: 22, of which 8 were waited for; matrix products, arithmetic and copies ran while one was open for 0% of the time, Pallas kernels for 40%

profile of v6, /device:TPU:24, one launch (start us, length us, event | category | flops | bytes accessed | tf_op | source)
XLA Modules:
  0.0 148.3 jit_solution(14808451533768175584)
XLA Ops:
  0.6 2.9 %pack.3 = (bf16[128,1664]{1,0:T(8,128)(2,1)}, bf16[128,1664]{1,0:T(8,128)(2,1)}, bf16[128,1664]{1,0:T(8,128)(2,1)}, bf16[128,1664]{1,0:T(8,128)(2,1)}) custom-call(s32[1]{0:T(128)} %bitcast.me_ref, bf16[128,2048]{1,0:T(8,128)(2,1)} %refs_12_.3, bf16[128,2048]{1,0:T(8,128)(2,1)} %refs_13_.3, bf16[128,4096]{1,0:T(8,128)(2,1)} %refs_14_.3, ...), custom_call_target="tpu_custom_call" | custom-call | tf_op jit(solution)/shard_map/pack/pallas_call | solution.py:487
  3.5 1.9 %collective-permute-start = (bf16[128,1664]{1,0:T(8,128)(2,1)}, bf16[128,1664]{1,0:T(8,128)(2,1)}, u32[]{:S(2)}, u32[]{:S(2)}) collective-permute-start(bf16[128,1664]{1,0:T(8,128)(2,1)} %get-tuple-element.60), channel_id=1, source_target_pairs={{0,1},{1,2},{2,3},{3,0},{4,5},{5,6},{6,7},{7,4},{8,9},{9,10},{10,1... | collective-permute-start | bytes 1277960 | tf_op jit(solution)/shard_map/ppermute | solution.py:637
  5.5 3.6 %collective-permute-start.1 = (bf16[128,1664]{1,0:T(8,128)(2,1)}, bf16[128,1664]{1,0:T(8,128)(2,1)}, u32[]{:S(2)}, u32[]{:S(2)}) collective-permute-start(bf16[128,1664]{1,0:T(8,128)(2,1)} %get-tuple-element.61), channel_id=1, source_target_pairs={{0,2},{1,3},{2,0},{3,1},{4,6},{5,7},{6,4},{7,5},{8,10},{9,11},{10,... | collective-permute-start | bytes 1277960 | tf_op jit(solution)/shard_map/ppermute | solution.py:637
  9.0 1.0 collective-permute-start.2
  10.1 2.7 %pack.2 = (bf16[128,1536]{1,0:T(8,128)(2,1)}, bf16[128,1536]{1,0:T(8,128)(2,1)}, bf16[128,1536]{1,0:T(8,128)(2,1)}, bf16[128,1536]{1,0:T(8,128)(2,1)}) custom-call(s32[1]{0:T(128)} %bitcast.me_ref, bf16[128,2048]{1,0:T(8,128)(2,1)} %refs_12_.3, bf16[128,2048]{1,0:T(8,128)(2,1)} %refs_13_.3, bf16[128,4096]{1,0:T(8,128)(2,1)} %refs_14_.3, ...), custom_call_target="tpu_custom_call" | custom-call | tf_op jit(solution)/shard_map/pack/pallas_call | solution.py:487
  12.7 0.6 pad_add_fusion.where_ref
  13.3 4.4 %collective-permute-done.refs_1_.refs_5_.refs_9_.refs_13_.refs_17_ = bf16[128,1664]{1,0:T(8,128)(2,1)} collective-permute-done((bf16[128,1664]{1,0:T(8,128)(2,1)}, bf16[128,1664]{1,0:T(8,128)(2,1)}, u32[]{:S(2)}, u32[]{:S(2)}) %collective-permute-start) | collective-permute-done | bytes 426016 | tf_op jit(solution)/shard_map/ppermute | solution.py:637
  17.7 10.3 %collective-permute-done.1.refs_2_.refs_6_.refs_10_.refs_14_.refs_18_ = bf16[128,1664]{1,0:T(8,128)(2,1)} collective-permute-done((bf16[128,1664]{1,0:T(8,128)(2,1)}, bf16[128,1664]{1,0:T(8,128)(2,1)}, u32[]{:S(2)}, u32[]{:S(2)}) %collective-permute-start.1) | collective-permute-done | bytes 426016 | tf_op jit(solution)/shard_map/ppermute | solution.py:637
  28.0 0.0 collective-permute-done.2.refs_3_.refs_7_.refs_11_.refs_15_.refs_19_
  28.0 1.2 collective-permute-start.9
  29.2 2.4 %collective-permute-start.10 = (bf16[128,1536]{1,0:T(8,128)(2,1)}, bf16[128,1536]{1,0:T(8,128)(2,1)}, u32[]{:S(2)}, u32[]{:S(2)}) collective-permute-start(bf16[128,1536]{1,0:T(8,128)(2,1)} %get-tuple-element.84), channel_id=1, source_target_pairs={{0,2},{1,3},{2,0},{3,1},{4,6},{5,7},{6,4},{7,5},{8,10},{9,11},{10,... | collective-permute-start | bytes 1179656 | tf_op jit(solution)/shard_map/ppermute | solution.py:637
  31.6 1.2 collective-permute-start.11
  32.9 11.3 %local_pass.2 = (bf16[4,2,272,128]{3,2,1,0:T(8,128)(2,1)}, bf16[4,4,128,128]{3,2,1,0:T(8,128)(2,1)}, f32[4,4,128,128]{3,2,1,0:T(8,128)}, f32[4,4,128,128]{3,2,1,...) custom-call(s32[1]{0:T(128)} %bitcast.me_ref, ...), custom_call_target="tpu_custom_call" | custom-call | flops 8000000000 | bytes 10000000 | tf_op jit(solution)/shard_map/local_pass/pallas_call | solution.py:564
  44.2 4.3 %all-to-all-start = ((bf16[8,272,128]{2,1,0:T(8,128)(2,1)}), bf16[8,272,128]{2,1,0:T(8,128)(2,1)}, u32[]{:S(2)}, u32[]{:S(2)}) async-start(bf16[8,272,128]{2,1,0:T(8,128)(2,1)} %bitcast.11), calls=%async_computation | async-start | bytes 1114112 | tf_op jit(solution)/shard_map/all_to_all | solution.py:645
  48.5 0.0 collective-permute-done.9.refs_1_.refs_5_.refs_9_.refs_13_
  48.5 0.9 collective-permute-done.10.refs_2_.refs_6_.refs_10_.refs_14_
  49.4 0.0 collective-permute-done.11.refs_3_.refs_7_.refs_11_.refs_15_
  49.4 11.3 %local_pass.3 = (bf16[4,2,272,128]{3,2,1,0:T(8,128)(2,1)}, bf16[4,4,128,128]{3,2,1,0:T(8,128)(2,1)}, f32[4,4,128,128]{3,2,1,0:T(8,128)}, f32[4,4,128,128]{3,2,1,...) custom-call(s32[1]{0:T(128)} %bitcast.me_ref, ...), custom_call_target="tpu_custom_call" | custom-call | flops 8000000000 | bytes 10000000 | tf_op jit(solution)/shard_map/local_pass/pallas_call | solution.py:564
  60.7 0.0 all-to-all-done.x_ref
  60.7 4.4 %all-to-all-start.2 = ((bf16[8,272,128]{2,1,0:T(8,128)(2,1)}), bf16[8,272,128]{2,1,0:T(8,128)(2,1)}, u32[]{:S(2)}, u32[]{:S(2)}) async-start(bf16[8,272,128]{2,1,0:T(8,128)(2,1)} %bitcast.12), calls=%async_computation.2 | async-start | bytes 1114112 | tf_op jit(solution)/shard_map/all_to_all | solution.py:645
  65.1 3.7 %combine_pass.2 = (f32[264,128]{1,0:T(8,128)}, f32[8,264,128]{2,1,0:T(8,128)}) custom-call(s32[3]{0:T(128)} %pad_add_fusion.where_ref, bf16[8,272,128]{2,1,0:T(8,128)(2,1)} %all-to-all-done.x_ref), custom_call_target="tpu_custom_call" | custom-call | flops 1500000000 | bytes 5000000 | tf_op jit(solution)/shard_map/combine_pass/pallas_call | solution.py:582
  68.8 0.7 collective-permute-start.5
  69.6 0.9 collective-permute-start.4
  70.5 2.2 %collective-permute-start.3 = (f32[264,128]{1,0:T(8,128)}, f32[264,128]{1,0:T(8,128)}, u32[]{:S(2)}, u32[]{:S(2)}) collective-permute-start(f32[264,128]{1,0:T(8,128)} %get-tuple-element.77), channel_id=1, source_target_pairs={{0,32},{4,36},{8,40},{12,44},{16,48},{20,52},{24,56},{28,60},{32,6... | collective-permute-start | bytes 405512 | tf_op jit(solution)/shard_map/ppermute | solution.py:650
  72.7 3.1 %all-to-all-done.2.x_ref = bf16[8,272,128]{2,1,0:T(8,128)(2,1)} async-done(((bf16[8,272,128]{2,1,0:T(8,128)(2,1)}), bf16[8,272,128]{2,1,0:T(8,128)(2,1)}, u32[]{:S(2)}, u32[]{:S(2)}) %all-to-all-start.2) | async-done | bytes 557088 | tf_op jit(solution)/shard_map/all_to_all | solution.py:645
  75.8 3.7 %combine_pass.3 = (f32[264,128]{1,0:T(8,128)}, f32[8,264,128]{2,1,0:T(8,128)}) custom-call(s32[3]{0:T(128)} %pad_add_fusion.where_ref, bf16[8,272,128]{2,1,0:T(8,128)(2,1)} %all-to-all-done.2.x_ref), custom_call_target="tpu_custom_call" | custom-call | flops 1500000000 | bytes 5000000 | tf_op jit(solution)/shard_map/combine_pass/pallas_call | solution.py:582
  79.6 0.7 collective-permute-start.14
  80.3 0.9 collective-permute-start.13
  81.3 0.0 collective-permute-done.5.three_ref
  81.3 2.2 %collective-permute-start.12 = (f32[264,128]{1,0:T(8,128)}, f32[264,128]{1,0:T(8,128)}, u32[]{:S(2)}, u32[]{:S(2)}) collective-permute-start(f32[264,128]{1,0:T(8,128)} %get-tuple-element.95), channel_id=1, source_target_pairs={{0,32},{4,36},{8,40},{12,44},{16,48},{20,52},{24,56},{28,60},{32,6... | collective-permute-start | bytes 405512 | tf_op jit(solution)/shard_map/ppermute | solution.py:650
  83.4 0.0 collective-permute-done.4.two_ref
  83.4 0.0 collective-permute-done.3.one_ref
  83.4 3.3 %chain_pass.2 = bf16[8,128,128]{2,1,0:T(8,128)(2,1)} custom-call(s32[3]{0:T(128)} %pad_add_fusion.where_ref, f32[8,264,128]{2,1,0:T(8,128)} %get-tuple-element.76.before_ref, f32[264,128]{1,0:T(8,128)} %collective-permute-done.3.one_ref, f32[264,128]{1,0:T(8,128)} %collective-permute-done.4.two_ref, f32[264,128]{1,0:T(8,128)} %collective-permute-done.5.three_ref), custom_call_target="tpu_custom_call" | custom-call | flops 1500000000 | bytes 5000000 | tf_op jit(solution)/shard_map/chain_pass/pallas_call | solution.py:598
  86.8 4.0 %all-to-all-start.1 = ((bf16[8,128,128]{2,1,0:T(8,128)(2,1)}), bf16[8,128,128]{2,1,0:T(8,128)(2,1)}, u32[]{:S(2)}, u32[]{:S(2)}) async-start(bf16[8,128,128]{2,1,0:T(8,128)(2,1)} %chain_pass.2), calls=%async_computation.1 | async-start | bytes 524288 | tf_op jit(solution)/shard_map/all_to_all | solution.py:655
  90.8 0.0 collective-permute-done.14.three_ref
  90.8 0.0 collective-permute-done.13.two_ref
  90.9 0.0 collective-permute-done.12.one_ref
  90.9 3.4 %chain_pass.3 = bf16[8,128,128]{2,1,0:T(8,128)(2,1)} custom-call(s32[3]{0:T(128)} %pad_add_fusion.where_ref, f32[8,264,128]{2,1,0:T(8,128)} %get-tuple-element.94.before_ref, f32[264,128]{1,0:T(8,128)} %collective-permute-done.12.one_ref, f32[264,128]{1,0:T(8,128)} %collective-permute-done.13.two_ref, f32[264,128]{1,0:T(8,128)} %collective-permute-done.14.three_ref), custom_call_target="tpu_custom_call" | custom-call | flops 1500000000 | bytes 5000000 | tf_op jit(solution)/shard_map/chain_pass/pallas_call | solution.py:598
  94.2 4.2 %all-to-all-done.1 = bf16[8,128,128]{2,1,0:T(8,128)(2,1)} async-done(((bf16[8,128,128]{2,1,0:T(8,128)(2,1)}), bf16[8,128,128]{2,1,0:T(8,128)(2,1)}, u32[]{:S(2)}, u32[]{:S(2)}) %all-to-all-start.1) | async-done | bytes 262176 | tf_op jit(solution)/shard_map/all_to_all | solution.py:655
  98.4 4.0 %all-to-all-start.3 = ((bf16[8,128,128]{2,1,0:T(8,128)(2,1)}), bf16[8,128,128]{2,1,0:T(8,128)(2,1)}, u32[]{:S(2)}, u32[]{:S(2)}) async-start(bf16[8,128,128]{2,1,0:T(8,128)(2,1)} %chain_pass.3), calls=%async_computation.3 | async-start | bytes 524288 | tf_op jit(solution)/shard_map/all_to_all | solution.py:655
  102.4 10.3 %final_pass.2 = (bf16[128,1152]{1,0:T(8,128)(2,1)}, bf16[128,1152]{1,0:T(8,128)(2,1)}, bf16[128,1152]{1,0:T(8,128)(2,1)}, bf16[128,1152]{1,0:T(8,128)(2,1)}) custom-call(s32[1]{0:T(128)} %bitcast.me_ref, bf16[128,1664]{1,0:T(8,128)(2,1)} %get-tuple-element.63.refs_0_.refs_4_.refs_8_.refs_12_.refs_16_, ...), custom_call_target="tpu_custom_call" | custom-call | flops 8000000000 | bytes 10000000 | tf_op jit(solution)/shard_map/final_pass/pallas_call | solution.py:617
  112.7 2.2 %collective-permute-start.6 = (bf16[128,1152]{1,0:T(8,128)(2,1)}, bf16[128,1152]{1,0:T(8,128)(2,1)}, u32[]{:S(2)}, u32[]{:S(2)}) collective-permute-start(bf16[128,1152]{1,0:T(8,128)(2,1)} %get-tuple-element.79), channel_id=1, source_target_pairs={{0,3},{1,0},{2,1},{3,2},{4,7},{5,4},{6,5},{7,6},{8,11},{9,8},{10,9... | collective-permute-start | bytes 884744 | tf_op jit(solution)/shard_map/ppermute | solution.py:637
  114.9 0.7 collective-permute-start.7
  115.6 0.2 collective-permute-start.8
  115.8 0.0 all-to-all-done.3
  115.8 10.2 %final_pass.3 = (bf16[128,1152]{1,0:T(8,128)(2,1)}, bf16[128,1152]{1,0:T(8,128)(2,1)}, bf16[128,1152]{1,0:T(8,128)(2,1)}, bf16[128,1152]{1,0:T(8,128)(2,1)}) custom-call(s32[1]{0:T(128)} %bitcast.me_ref, bf16[128,1536]{1,0:T(8,128)(2,1)} %get-tuple-element.82.refs_0_.refs_4_.refs_8_.refs_12_, ...), custom_call_target="tpu_custom_call" | custom-call | flops 8000000000 | bytes 10000000 | tf_op jit(solution)/shard_map/final_pass/pallas_call | solution.py:617
  126.0 3.1 %collective-permute-start.15 = (bf16[128,1152]{1,0:T(8,128)(2,1)}, bf16[128,1152]{1,0:T(8,128)(2,1)}, u32[]{:S(2)}, u32[]{:S(2)}) collective-permute-start(bf16[128,1152]{1,0:T(8,128)(2,1)} %get-tuple-element.97), channel_id=1, source_target_pairs={{0,3},{1,0},{2,1},{3,2},{4,7},{5,4},{6,5},{7,6},{8,11},{9,8},{10,9... | collective-permute-start | bytes 884744 | tf_op jit(solution)/shard_map/ppermute | solution.py:637
  129.1 1.6 %collective-permute-start.16 = (bf16[128,1152]{1,0:T(8,128)(2,1)}, bf16[128,1152]{1,0:T(8,128)(2,1)}, u32[]{:S(2)}, u32[]{:S(2)}) collective-permute-start(bf16[128,1152]{1,0:T(8,128)(2,1)} %get-tuple-element.98), channel_id=1, source_target_pairs={{0,2},{1,3},{2,0},{3,1},{4,6},{5,7},{6,4},{7,5},{8,10},{9,11},{10,... | collective-permute-start | bytes 884744 | tf_op jit(solution)/shard_map/ppermute | solution.py:637
  130.7 0.0 collective-permute-done.6.refs_1_
  130.7 0.0 collective-permute-start.17
  130.7 0.0 collective-permute-done.7.refs_2_
  130.7 1.3 collective-permute-done.8.refs_3_
  132.0 9.7 %collective-permute-done.15.refs_5_ = bf16[128,1152]{1,0:T(8,128)(2,1)} collective-permute-done((bf16[128,1152]{1,0:T(8,128)(2,1)}, bf16[128,1152]{1,0:T(8,128)(2,1)}, u32[]{:S(2)}, u32[]{:S(2)}) %collective-permute-start.15) | collective-permute-done | bytes 294944 | tf_op jit(solution)/shard_map/ppermute | solution.py:637
  141.6 0.0 collective-permute-done.16.refs_6_
  141.6 3.7 %collective-permute-done.17.refs_7_ = bf16[128,1152]{1,0:T(8,128)(2,1)} collective-permute-done((bf16[128,1152]{1,0:T(8,128)(2,1)}, bf16[128,1152]{1,0:T(8,128)(2,1)}, u32[]{:S(2)}, u32[]{:S(2)}) %collective-permute-start.17) | collective-permute-done | bytes 294944 | tf_op jit(solution)/shard_map/ppermute | solution.py:637
  145.3 3.0 %unpack.1 = (bf16[128,2048]{1,0:T(8,128)(2,1)}, bf16[128,2048]{1,0:T(8,128)(2,1)}, bf16[128,4096]{1,0:T(8,128)(2,1)}, bf16[32,128]{1,0:T(8,128)(2,1)}, bf16[32,128]{1,0:T(8,128)(2,1)}) custom-call(s32[1]{0:T(128)} %bitcast.me_ref, bf16[128,1152]{1,0:T(8,128)(2,1)} %get-tuple-element.78.refs_0_, bf16[128,1152]{1,0:T(8,128)(2,1)} %collective-permute-done.6.refs_1_, ...), custom_call_target="tpu_custom_call" | custom-call | tf_op jit(solution)/shard_map/unpack/pallas_call | solution.py:530
Async XLA Ops:
  3.5 14.2 %collective-permute-start = (bf16[128,1664]{1,0:T(8,128)(2,1)}, bf16[128,1664]{1,0:T(8,128)(2,1)}, u32[]{:S(2)}, u32[]{:S(2)}) collective-permute-start(bf16[128,1664]{1,0:T(8,128)(2,1)} %get-tuple-element.60), channel_id=1, source_target_pairs={{0,1},{1,2},{2,3},{3,0},{4,5},{5,6},{6,7},{7,4},{8,9},{9,10},{10,1... | collective-permute-start | bytes 1277960 | tf_op jit(solution)/shard_map/ppermute | solution.py:637
  5.5 22.6 %collective-permute-start.1 = (bf16[128,1664]{1,0:T(8,128)(2,1)}, bf16[128,1664]{1,0:T(8,128)(2,1)}, u32[]{:S(2)}, u32[]{:S(2)}) collective-permute-start(bf16[128,1664]{1,0:T(8,128)(2,1)} %get-tuple-element.61), channel_id=1, source_target_pairs={{0,2},{1,3},{2,0},{3,1},{4,6},{5,7},{6,4},{7,5},{8,10},{9,11},{10,... | collective-permute-start | bytes 1277960 | tf_op jit(solution)/shard_map/ppermute | solution.py:637
  9.0 19.0 %collective-permute-start.2 = (bf16[128,1664]{1,0:T(8,128)(2,1)}, bf16[128,1664]{1,0:T(8,128)(2,1)}, u32[]{:S(2)}, u32[]{:S(2)}) collective-permute-start(bf16[128,1664]{1,0:T(8,128)(2,1)} %get-tuple-element.62), channel_id=1, source_target_pairs={{0,3},{1,0},{2,1},{3,2},{4,7},{5,4},{6,5},{7,6},{8,11},{9,8},{10,9... | collective-permute-start | bytes 1277960 | tf_op jit(solution)/shard_map/ppermute | solution.py:637
  28.0 20.5 %collective-permute-start.9 = (bf16[128,1536]{1,0:T(8,128)(2,1)}, bf16[128,1536]{1,0:T(8,128)(2,1)}, u32[]{:S(2)}, u32[]{:S(2)}) collective-permute-start(bf16[128,1536]{1,0:T(8,128)(2,1)} %get-tuple-element.83), channel_id=1, source_target_pairs={{0,1},{1,2},{2,3},{3,0},{4,5},{5,6},{6,7},{7,4},{8,9},{9,10},{10,1... | collective-permute-start | bytes 1179656 | tf_op jit(solution)/shard_map/ppermute | solution.py:637
  29.2 20.1 %collective-permute-start.10 = (bf16[128,1536]{1,0:T(8,128)(2,1)}, bf16[128,1536]{1,0:T(8,128)(2,1)}, u32[]{:S(2)}, u32[]{:S(2)}) collective-permute-start(bf16[128,1536]{1,0:T(8,128)(2,1)} %get-tuple-element.84), channel_id=1, source_target_pairs={{0,2},{1,3},{2,0},{3,1},{4,6},{5,7},{6,4},{7,5},{8,10},{9,11},{10,... | collective-permute-start | bytes 1179656 | tf_op jit(solution)/shard_map/ppermute | solution.py:637
  31.6 17.8 %collective-permute-start.11 = (bf16[128,1536]{1,0:T(8,128)(2,1)}, bf16[128,1536]{1,0:T(8,128)(2,1)}, u32[]{:S(2)}, u32[]{:S(2)}) collective-permute-start(bf16[128,1536]{1,0:T(8,128)(2,1)} %get-tuple-element.85), channel_id=1, source_target_pairs={{0,3},{1,0},{2,1},{3,2},{4,7},{5,4},{6,5},{7,6},{8,11},{9,8},{10,9... | collective-permute-start | bytes 1179656 | tf_op jit(solution)/shard_map/ppermute | solution.py:637
  44.2 16.5 %all-to-all-start = ((bf16[8,272,128]{2,1,0:T(8,128)(2,1)}), bf16[8,272,128]{2,1,0:T(8,128)(2,1)}, u32[]{:S(2)}, u32[]{:S(2)}) async-start(bf16[8,272,128]{2,1,0:T(8,128)(2,1)} %bitcast.11), calls=%async_computation | async-start | bytes 1114112 | tf_op jit(solution)/shard_map/all_to_all | solution.py:645
  60.7 15.1 %all-to-all-start.2 = ((bf16[8,272,128]{2,1,0:T(8,128)(2,1)}), bf16[8,272,128]{2,1,0:T(8,128)(2,1)}, u32[]{:S(2)}, u32[]{:S(2)}) async-start(bf16[8,272,128]{2,1,0:T(8,128)(2,1)} %bitcast.12), calls=%async_computation.2 | async-start | bytes 1114112 | tf_op jit(solution)/shard_map/all_to_all | solution.py:645
  68.8 12.4 %collective-permute-start.5 = (f32[264,128]{1,0:T(8,128)}, f32[264,128]{1,0:T(8,128)}, u32[]{:S(2)}, u32[]{:S(2)}) collective-permute-start(f32[264,128]{1,0:T(8,128)} %get-tuple-element.77), channel_id=1, source_target_pairs={{0,96},{4,100},{8,104},{12,108},{16,112},{20,116},{24,120},{28,124... | collective-permute-start | bytes 405512 | tf_op jit(solution)/shard_map/ppermute | solution.py:650
  69.6 13.9 %collective-permute-start.4 = (f32[264,128]{1,0:T(8,128)}, f32[264,128]{1,0:T(8,128)}, u32[]{:S(2)}, u32[]{:S(2)}) collective-permute-start(f32[264,128]{1,0:T(8,128)} %get-tuple-element.77), channel_id=1, source_target_pairs={{0,64},{4,68},{8,72},{12,76},{16,80},{20,84},{24,88},{28,92},{32,9... | collective-permute-start | bytes 405512 | tf_op jit(solution)/shard_map/ppermute | solution.py:650
  70.5 12.9 %collective-permute-start.3 = (f32[264,128]{1,0:T(8,128)}, f32[264,128]{1,0:T(8,128)}, u32[]{:S(2)}, u32[]{:S(2)}) collective-permute-start(f32[264,128]{1,0:T(8,128)} %get-tuple-element.77), channel_id=1, source_target_pairs={{0,32},{4,36},{8,40},{12,44},{16,48},{20,52},{24,56},{28,60},{32,6... | collective-permute-start | bytes 405512 | tf_op jit(solution)/shard_map/ppermute | solution.py:650
  79.6 11.3 %collective-permute-start.14 = (f32[264,128]{1,0:T(8,128)}, f32[264,128]{1,0:T(8,128)}, u32[]{:S(2)}, u32[]{:S(2)}) collective-permute-start(f32[264,128]{1,0:T(8,128)} %get-tuple-element.95), channel_id=1, source_target_pairs={{0,96},{4,100},{8,104},{12,108},{16,112},{20,116},{24,120},{28,124... | collective-permute-start | bytes 405512 | tf_op jit(solution)/shard_map/ppermute | solution.py:650
  80.3 10.5 %collective-permute-start.13 = (f32[264,128]{1,0:T(8,128)}, f32[264,128]{1,0:T(8,128)}, u32[]{:S(2)}, u32[]{:S(2)}) collective-permute-start(f32[264,128]{1,0:T(8,128)} %get-tuple-element.95), channel_id=1, source_target_pairs={{0,64},{4,68},{8,72},{12,76},{16,80},{20,84},{24,88},{28,92},{32,9... | collective-permute-start | bytes 405512 | tf_op jit(solution)/shard_map/ppermute | solution.py:650
  81.3 9.6 %collective-permute-start.12 = (f32[264,128]{1,0:T(8,128)}, f32[264,128]{1,0:T(8,128)}, u32[]{:S(2)}, u32[]{:S(2)}) collective-permute-start(f32[264,128]{1,0:T(8,128)} %get-tuple-element.95), channel_id=1, source_target_pairs={{0,32},{4,36},{8,40},{12,44},{16,48},{20,52},{24,56},{28,60},{32,6... | collective-permute-start | bytes 405512 | tf_op jit(solution)/shard_map/ppermute | solution.py:650
  86.8 11.6 %all-to-all-start.1 = ((bf16[8,128,128]{2,1,0:T(8,128)(2,1)}), bf16[8,128,128]{2,1,0:T(8,128)(2,1)}, u32[]{:S(2)}, u32[]{:S(2)}) async-start(bf16[8,128,128]{2,1,0:T(8,128)(2,1)} %chain_pass.2), calls=%async_computation.1 | async-start | bytes 524288 | tf_op jit(solution)/shard_map/all_to_all | solution.py:655
  98.4 17.5 %all-to-all-start.3 = ((bf16[8,128,128]{2,1,0:T(8,128)(2,1)}), bf16[8,128,128]{2,1,0:T(8,128)(2,1)}, u32[]{:S(2)}, u32[]{:S(2)}) async-start(bf16[8,128,128]{2,1,0:T(8,128)(2,1)} %chain_pass.3), calls=%async_computation.3 | async-start | bytes 524288 | tf_op jit(solution)/shard_map/all_to_all | solution.py:655
  112.7 18.0 %collective-permute-start.6 = (bf16[128,1152]{1,0:T(8,128)(2,1)}, bf16[128,1152]{1,0:T(8,128)(2,1)}, u32[]{:S(2)}, u32[]{:S(2)}) collective-permute-start(bf16[128,1152]{1,0:T(8,128)(2,1)} %get-tuple-element.79), channel_id=1, source_target_pairs={{0,3},{1,0},{2,1},{3,2},{4,7},{5,4},{6,5},{7,6},{8,11},{9,8},{10,9... | collective-permute-start | bytes 884744 | tf_op jit(solution)/shard_map/ppermute | solution.py:637
  114.9 15.8 %collective-permute-start.7 = (bf16[128,1152]{1,0:T(8,128)(2,1)}, bf16[128,1152]{1,0:T(8,128)(2,1)}, u32[]{:S(2)}, u32[]{:S(2)}) collective-permute-start(bf16[128,1152]{1,0:T(8,128)(2,1)} %get-tuple-element.80), channel_id=1, source_target_pairs={{0,2},{1,3},{2,0},{3,1},{4,6},{5,7},{6,4},{7,5},{8,10},{9,11},{10,... | collective-permute-start | bytes 884744 | tf_op jit(solution)/shard_map/ppermute | solution.py:637
  115.6 16.4 %collective-permute-start.8 = (bf16[128,1152]{1,0:T(8,128)(2,1)}, bf16[128,1152]{1,0:T(8,128)(2,1)}, u32[]{:S(2)}, u32[]{:S(2)}) collective-permute-start(bf16[128,1152]{1,0:T(8,128)(2,1)} %get-tuple-element.81), channel_id=1, source_target_pairs={{0,1},{1,2},{2,3},{3,0},{4,5},{5,6},{6,7},{7,4},{8,9},{9,10},{10,1... | collective-permute-start | bytes 884744 | tf_op jit(solution)/shard_map/ppermute | solution.py:637
  126.0 15.6 %collective-permute-start.15 = (bf16[128,1152]{1,0:T(8,128)(2,1)}, bf16[128,1152]{1,0:T(8,128)(2,1)}, u32[]{:S(2)}, u32[]{:S(2)}) collective-permute-start(bf16[128,1152]{1,0:T(8,128)(2,1)} %get-tuple-element.97), channel_id=1, source_target_pairs={{0,3},{1,0},{2,1},{3,2},{4,7},{5,4},{6,5},{7,6},{8,11},{9,8},{10,9... | collective-permute-start | bytes 884744 | tf_op jit(solution)/shard_map/ppermute | solution.py:637
  129.1 12.6 %collective-permute-start.16 = (bf16[128,1152]{1,0:T(8,128)(2,1)}, bf16[128,1152]{1,0:T(8,128)(2,1)}, u32[]{:S(2)}, u32[]{:S(2)}) collective-permute-start(bf16[128,1152]{1,0:T(8,128)(2,1)} %get-tuple-element.98), channel_id=1, source_target_pairs={{0,2},{1,3},{2,0},{3,1},{4,6},{5,7},{6,4},{7,5},{8,10},{9,11},{10,... | collective-permute-start | bytes 884744 | tf_op jit(solution)/shard_map/ppermute | solution.py:637
  130.7 14.6 %collective-permute-start.17 = (bf16[128,1152]{1,0:T(8,128)(2,1)}, bf16[128,1152]{1,0:T(8,128)(2,1)}, u32[]{:S(2)}, u32[]{:S(2)}) collective-permute-start(bf16[128,1152]{1,0:T(8,128)(2,1)} %get-tuple-element.99), channel_id=1, source_target_pairs={{0,1},{1,2},{2,3},{3,0},{4,5},{5,6},{6,7},{7,4},{8,9},{9,10},{10,1... | collective-permute-start | bytes 884744 | tf_op jit(solution)/shard_map/ppermute | solution.py:637
